TPU v7x, 256 devices: a whole 4x4x8 slice. The times are simulated.
256 devices in a mesh: dom: 64 (over z, y, core), blk: 4 (over x).
Axes of the slice: x: 4, y: 4, z: 8, core: 2. Of those that a mesh axis runs over, the one named last changes fastest.
Arguments:
- current: bfloat16 [1048576, 128], P(('dom', 'blk')), may hold values from -6 to 6
- resistivity: bfloat16 [1048576], P(('dom', 'blk')), may hold values from 0.5 to 4
- temp_coef: bfloat16 [1048576], P(('dom', 'blk')), may hold values from 0.099609375 to 0.5
- dest_part: int32 [1048576, 1], P(('dom', 'blk')), may hold values from 0 to 63; in each aligned block of 4096 rows (0 to 4095, 4096 to 8191, ...) at most 128 rows name the same one
- dest_row: int32 [1048576], P(('dom', 'blk')), may hold values from 0 to 2047
- temp_old: float32 [524288, 128], P(('dom', 'blk')), may hold values from -6 to 6
- heat_cap: float32 [524288], P(('dom', 'blk')), may hold values from 0.25 to 2
- conduction: bfloat16 [8192, 64, 1024], P(('dom', 'blk'))
- block_cols: int32 [8192, 16], P(('dom', 'blk')), may hold values from 0 to 8191, as said below
Outputs:
- temperature: float32 [524288, 128], P(('dom', 'blk'))
- resist_new: bfloat16 [1048576, 128], P(('dom', 'blk'))
Inputs may be any that keep to these rules, and one draw needn't show every extreme that they name: `dest_part`: the rows of one device name each partition at most 128 times; in every draw some device's rows name some partition exactly 128 times. `block_cols`: column 0 of block row r is r itself; the other 15 entries are distinct blocks r + o mod 8192 with 0 < |o| <= 12.
All inputs are finite; a program needn't handle non-finite values.
Results may differ from a plain program's by a relative error of at most 0.001.
The roundings to bfloat16 on the way count: a program that leaves them out, or rounds other values in their place, can miss the bound.
Values may be sent and summed in bfloat16 or wider, within the bound.
No kernel may reach another device: no remote copies, remote signals or barrier semaphores. Data moves between devices by JAX's collectives and lax.ppermute only.
A program may use at most 128 MiB of HBM per device.

v0:
```python
import jax
import jax.numpy as jnp
from jax import lax
from jax.sharding import PartitionSpec as P

HB = 12
SWEEPS = 2


def extended(cells, sides, width):
    for axis, dim in sides:
        count = lax.axis_size(axis)
        head = lax.slice_in_dim(cells, 0, width, axis=dim)
        tail = lax.slice_in_dim(cells, cells.shape[dim] - width, cells.shape[dim], axis=dim)
        cells = jnp.concatenate(
            [
                lax.ppermute(tail, axis, [(i, (i + 1) % count) for i in range(count)]),
                cells,
                lax.ppermute(head, axis, [((i + 1) % count, i) for i in range(count)]),
            ],
            axis=dim,
        )
    return cells


def deposit(values, row_ids, total_rows):
    flattened = values.reshape(-1, values.shape[-1])
    return jax.ops.segment_sum(flattened, row_ids.reshape(-1), num_segments=total_rows)


def body(
    current, resistivity, temp_coef, dest_part, dest_row, temp_old, heat_cap, conduction, block_cols
):
    em_count, samples = current.shape
    peer_count = lax.axis_size("dom")
    slot_count = 2 * em_count // peer_count
    node_count = temp_old.shape[0]
    block_count = conduction.shape[0]
    block_size = conduction.shape[1]
    col_slots = block_cols.shape[1]
    target = dest_part[:, 0]
    one_hot = (target[:, None] == jnp.arange(peer_count, dtype=jnp.int32)[None, :]).astype(
        jnp.int32
    )
    slot_rank = jnp.sum((jnp.cumsum(one_hot, axis=0) - 1) * one_hot, axis=1)
    row_buffer = (
        jnp.full((peer_count, slot_count), node_count, jnp.int32)
        .at[target, slot_rank]
        .set(dest_row)
    )
    resist_wide = resistivity.astype(jnp.float32)
    current_wide = current.astype(jnp.float32)
    power_loss = resist_wide[:, None] * current_wide * current_wide
    loss_buffer = (
        jnp.zeros((peer_count, slot_count, samples), jnp.float32)
        .at[target, slot_rank]
        .set(power_loss)
    )
    recv_loss, recv_rows = (
        lax.all_to_all(loss_buffer, "dom", split_axis=0, concat_axis=0, tiled=True),
        lax.all_to_all(row_buffer, "dom", split_axis=0, concat_axis=0, tiled=True),
    )
    heat_source = deposit(recv_loss, recv_rows, node_count)
    right_side = heat_cap[:, None] * temp_old + heat_source
    diag_cond = (
        jnp.diagonal(conduction[:, :, :block_size], axis1=1, axis2=2)
        .reshape(-1)
        .astype(jnp.float32)
    )
    pivot_sum = heat_cap + diag_cond
    device_count = lax.axis_size(("dom", "blk"))
    first_block = lax.axis_index(("dom", "blk")) * block_count
    local_cols = jnp.mod(block_cols - first_block + HB, block_count * device_count)
    field_now = temp_old
    for sweep_idx in range(SWEEPS):
        field_low = field_now.astype(jnp.bfloat16)
        padded = extended(field_low, ((("dom", "blk"), 0),), HB * block_size)
        blocks = padded.reshape(block_count + 2 * HB, block_size, samples)
        picked = blocks[local_cols].reshape(block_count, col_slots * block_size, samples)
        applied = jnp.einsum(
            "rik,rkw->riw", conduction, picked, preferred_element_type=jnp.float32
        ).reshape(node_count, samples)
        field_now = (
            field_now + (right_side - heat_cap[:, None] * field_now - applied) / pivot_sum[:, None]
        )
    safe_rows = jnp.minimum(recv_rows, node_count - 1)
    node_temps = field_now[safe_rows]
    returned = lax.all_to_all(node_temps, "dom", split_axis=0, concat_axis=0, tiled=True)
    seen_temps = returned[target, slot_rank]
    coef_wide = temp_coef.astype(jnp.float32)
    resist_new = (resist_wide[:, None] * (1.0 + coef_wide[:, None] * seen_temps)).astype(
        jnp.bfloat16
    )
    return (field_now, resist_new)


def solution(mesh):
    placed = (
        P(("dom", "blk"), None),
        P(("dom", "blk")),
        P(("dom", "blk")),
        P(("dom", "blk"), None),
        P(("dom", "blk")),
        P(("dom", "blk"), None),
        P(("dom", "blk")),
        P(("dom", "blk"), None, None),
        P(("dom", "blk"), None),
    )
    return jax.shard_map(
        body,
        mesh=mesh,
        in_specs=placed,
        out_specs=(P(("dom", "blk"), None), P(("dom", "blk"), None)),
        check_vma=False,
    )
```

profile of v0, /device:TPU:6, one launch (start us, length us, event | category | flops | bytes accessed | tf_op | source)
XLA Modules:
  0.0 446.4 jit_solution(8131909469418314934)
XLA Ops:
  0.6 0.8 fusion.10
  1.5 18.4 %reduce-window.6 = s32[64,32,128]{2,1,0:T(8,128)S(1)} reduce-window(s32[64,32,128]{2,1,0:T(8,128)S(1)} %fusion.10, s32[]{:T(128)} %constant.19.clone.1), window={size=1x1x128 pad=0_0x0_0x127_0}, to_apply=%region_0.0 | reduce-window | flops 33292288 | bytes 2097156 | tf_op jit(solution)/shard_map/reduce-window
  21.3 0.8 fusion.4
  22.5 16.3 %scatter_custom_fusion.1 = s32[8192]{0:T(1024)} fusion(s32[4096]{0:T(1024)S(1)} %broadcast_select_fusion, s32[4096]{0:T(1024)} %param.13, s32[]{:T(128)} %constant.18.clone.1), kind=kCustom, calls=%fused_computation.41 | custom fusion | bytes 33280
  38.8 12.1 %all-to-all-start = ((s32[64,1,128]{2,1,0:T(1,128)}), s32[64,1,128]{2,1,0:T(1,128)S(1)}, u32[]{:S(2)}, u32[]{:S(2)}) async-start(s32[64,1,128]{2,1,0:T(1,128)} %bitcast.6), calls=%async_computation | async-start | bytes 65536 | tf_op jit(solution)/shard_map/all_to_all | solution.py:61
  50.9 14.8 %scatter_custom_fusion.2 = f32[8192,128]{1,0:T(8,128)} fusion(s32[4096]{0:T(1024)S(1)} %broadcast_select_fusion, f32[]{:T(128)} %constant.26.clone.1, bf16[4096,128]{1,0:T(8,128)(2,1)S(1)} %copy-done.4, f32[4096]{0:T(1024)S(1)} %convert_element_type.30), kind=kCustom, calls=%fused_computation.9 | custom fusion | flops 1572864 | bytes 5259268
  65.7 10.7 %all-to-all-start.1 = ((f32[64,128,128]{2,1,0:T(8,128)}), f32[64,128,128]{2,1,0:T(8,128)}, u32[]{:S(2)}, u32[]{:S(2)}) async-start(f32[64,128,128]{2,1,0:T(8,128)} %bitcast.64), calls=%async_computation.1 | async-start | bytes 8388608 | tf_op jit(solution)/shard_map/all_to_all | solution.py:60
  76.9 0.8 fusion.19
  77.6 0.8 collective-permute-start.1
  78.5 2.1 collective-permute-start
  80.6 1.7 copy.18
  82.3 1.7 gather_fusion.1
  84.3 0.7 copy-done.7
  85.0 1.0 collective-permute-done
  86.0 1.2 pad_maximum_fusion
  87.3 13.5 %gather_fusion = bf16[512,64,128]{2,1,0:T(8,128)(2,1)} fusion(bf16[56,64,128]{2,1,0:T(8,128)(2,1)S(1)} %bitcast.61, s32[1024]{0:T(1024)S(1)} %pad_clamp_fusion), kind=kCustom, calls=%fused_computation | custom fusion | bytes 16779264 | tf_op jit(solution)/shard_map/gather | solution.py:79
  100.7 6.3 %fusion.20 = f32[32,128,64]{1,2,0:T(8,128)S(1)} fusion(bf16[32,64,1024]{2,1,0:T(8,128)(2,1)} %param.16, bf16[32,1024,128]{2,1,0:T(8,128)(2,1)} %bitcast.63), kind=kOutput, calls=%fused_computation.54 | convolution fusion | flops 536870912 | bytes 13631488 | tf_op jit(solution)/shard_map/rik,rkw->riw/dot_general | solution.py:80
  107.0 65.7 %all-to-all-done.1 = f32[64,128,128]{2,1,0:T(8,128)} async-done(((f32[64,128,128]{2,1,0:T(8,128)}), f32[64,128,128]{2,1,0:T(8,128)}, u32[]{:S(2)}, u32[]{:S(2)}) %all-to-all-start.1) | async-done | bytes 4194336 | tf_op jit(solution)/shard_map/all_to_all | solution.py:60
  172.7 44.7 %scatter_fusion = f32[2048,128]{1,0:T(8,128)S(1)} fusion(f32[2048,128]{1,0:T(8,128)S(1)} %get-tuple-element.4, s32[8192]{0:T(1024)S(1)} %bitcast.67, f32[8192,128]{1,0:T(8,128)} %bitcast.9), kind=kCustom, calls=%fused_computation.5 | custom fusion | flops 1048576 | bytes 12615680 | tf_op jit(solution)/shard_map/scatter-add | solution.py:28
  217.4 1.6 fusion.16
  219.0 0.9 collective-permute-start.3
  219.9 2.1 collective-permute-start.2
  222.1 3.3 collective-permute-done.3
  225.4 1.6 collective-permute-done.2
  227.1 13.5 %gather_fusion.2 = bf16[512,64,128]{2,1,0:T(8,128)(2,1)} fusion(bf16[56,64,128]{2,1,0:T(8,128)(2,1)S(1)} %bitcast.60, s32[1024]{0:T(1024)S(1)} %pad_clamp_fusion), kind=kCustom, calls=%fused_computation.2 | custom fusion | bytes 16779264 | tf_op jit(solution)/shard_map/gather | solution.py:79
  240.6 6.3 %fusion.21 = f32[32,128,64]{1,2,0:T(8,128)S(1)} fusion(bf16[32,64,1024]{2,1,0:T(8,128)(2,1)} %param.16, bf16[32,1024,128]{2,1,0:T(8,128)(2,1)} %bitcast.62), kind=kOutput, calls=%fused_computation.55 | convolution fusion | flops 536870912 | bytes 13631488 | tf_op jit(solution)/shard_map/rik,rkw->riw/dot_general | solution.py:80
  246.9 0.8 fusion.6
  247.8 27.7 %gather_fusion.3 = f32[8192,128]{1,0:T(8,128)} fusion(f32[2048,128]{1,0:T(8,128)S(1)} %fusion.6, s32[8192]{0:T(1024)S(1)} %fusion.12), kind=kCustom, calls=%fused_computation.3 | custom fusion | bytes 8421376 | tf_op jit(solution)/shard_map/gather | solution.py:87
  275.5 30.9 %all-to-all-start.2 = ((f32[64,128,128]{2,1,0:T(8,128)}), f32[64,128,128]{2,1,0:T(8,128)}, u32[]{:S(2)}, u32[]{:S(2)}) async-start(f32[64,128,128]{2,1,0:T(8,128)} %bitcast.65), calls=%async_computation.2 | async-start | bytes 8388608 | tf_op jit(solution)/shard_map/all_to_all | solution.py:88
  306.5 96.2 %all-to-all-done.2 = f32[64,128,128]{2,1,0:T(8,128)} async-done(((f32[64,128,128]{2,1,0:T(8,128)}), f32[64,128,128]{2,1,0:T(8,128)}, u32[]{:S(2)}, u32[]{:S(2)}) %all-to-all-start.2) | async-done | bytes 4194336 | tf_op jit(solution)/shard_map/all_to_all | solution.py:88
  402.7 40.6 %gather_fusion.4 = f32[4096,128]{1,0:T(8,128)S(1)} fusion(f32[64,128,128]{2,1,0:T(8,128)} %all-to-all-done.2, s32[4096]{0:T(1024)S(1)} %bitcast.59), kind=kCustom, calls=%fused_computation.4 | custom fusion | bytes 4227072 | tf_op jit(solution)/shard_map/gather | solution.py:89
  443.3 3.1 multiply_convert_fusion
  (63 shorter events, 2.6 us)
Async XLA Ops:
  20.3 1.1 copy-start.8
  20.3 1.9 copy-start.17
  20.3 2.1 copy-start.16
  20.3 30.6 %copy-start.13 = (bf16[4096]{0:T(1024)(128)(2,1)S(1)}, bf16[4096]{0:T(1024)(128)(2,1)}, u32[]{:S(2)}) copy-start(bf16[4096]{0:T(1024)(128)(2,1)} %param.10) | copy-start | bytes 24580
  20.3 30.6 %copy-start.4 = (bf16[4096,128]{1,0:T(8,128)(2,1)S(1)}, bf16[4096,128]{1,0:T(8,128)(2,1)}, u32[]{:S(2)}) copy-start(bf16[4096,128]{1,0:T(8,128)(2,1)} %param.9) | copy-start | bytes 3145732
  38.8 26.9 %all-to-all-start = ((s32[64,1,128]{2,1,0:T(1,128)}), s32[64,1,128]{2,1,0:T(1,128)S(1)}, u32[]{:S(2)}, u32[]{:S(2)}) async-start(s32[64,1,128]{2,1,0:T(1,128)} %bitcast.6), calls=%async_computation | async-start | bytes 65536 | tf_op jit(solution)/shard_map/all_to_all | solution.py:61
  50.9 14.8 %copy-start.9 = (f32[4096]{0:T(1024)}, f32[4096]{0:T(1024)S(1)}, u32[]{:S(2)}) copy-start(f32[4096]{0:T(1024)S(1)} %convert_element_type.30) | copy-start | bytes 49156
  65.7 18.6 %copy-start.5 = (s32[64,1,128]{2,1,0:T(1,128)}, s32[64,1,128]{2,1,0:T(1,128)S(1)}, u32[]{:S(2)}) copy-start(s32[64,1,128]{2,1,0:T(1,128)S(1)} %all-to-all-done) | copy-start | bytes 98308
  65.7 10.7 %copy-start.1 = (f32[2048,128]{1,0:T(8,128)S(1)}, f32[2048,128]{1,0:T(8,128)}, u32[]{:S(2)}) copy-start(f32[2048,128]{1,0:T(8,128)} %param.14) | copy-start | bytes 3145732
  65.7 10.7 %copy-start.11 = (f32[2048]{0:T(1024)S(1)}, f32[2048]{0:T(1024)}, u32[]{:S(2)}) copy-start(f32[2048]{0:T(1024)} %param.15) | copy-start | bytes 24580
  65.7 106.9 %all-to-all-start.1 = ((f32[64,128,128]{2,1,0:T(8,128)}), f32[64,128,128]{2,1,0:T(8,128)}, u32[]{:S(2)}, u32[]{:S(2)}) async-start(f32[64,128,128]{2,1,0:T(8,128)} %bitcast.64), calls=%async_computation.1 | async-start | bytes 8388608 | tf_op jit(solution)/shard_map/all_to_all | solution.py:60
  76.5 4.1 slice-start
  76.8 7.5 %copy-start.3 = (bf16[2048,128]{1,0:T(8,128)(2,1)}, bf16[2048,128]{1,0:T(8,128)(2,1)S(1)}, u32[]{:S(2)}) copy-start(bf16[2048,128]{1,0:T(8,128)(2,1)S(1)} %get-tuple-element.5) | copy-start | bytes 1572868
  76.8 7.2 %copy-start.15 = (s32[32,16]{0,1:T(8,128)S(1)}, s32[32,16]{0,1:T(8,128)}, u32[]{:S(2)}) copy-start(s32[32,16]{0,1:T(8,128)} %param.17) | copy-start | bytes 6148
  77.6 6.7 %collective-permute-start.1 = (bf16[768,128]{1,0:T(8,128)(2,1)}, bf16[768,128]{1,0:T(8,128)(2,1)S(1)}, u32[]{:S(2)}, u32[]{:S(2)}) collective-permute-start(bf16[768,128]{1,0:T(8,128)(2,1)} %get-tuple-element.9), channel_id=1, source_target_pairs={{1,0},{2,1},{3,2},{4,3},{5,4},{6,5},{7,6},{8,7},{9,8},{10,9},{11,1... | collective-permute-start | bytes 589832 | tf_op jit(solution)/shard_map/ppermute | solution.py:19
  78.5 7.5 %collective-permute-start = (bf16[768,128]{1,0:T(8,128)(2,1)}, bf16[768,128]{1,0:T(8,128)(2,1)}, u32[]{:S(2)}, u32[]{:S(2)}) collective-permute-start(bf16[768,128]{1,0:T(8,128)(2,1)} %get-tuple-element.8), channel_id=1, source_target_pairs={{0,1},{1,2},{2,3},{3,4},{4,5},{5,6},{6,7},{7,8},{8,9},{9,10},{10,1... | collective-permute-start | bytes 589832 | tf_op jit(solution)/shard_map/ppermute | solution.py:17
  84.3 0.7 copy-start.7
  100.7 72.0 %copy-start.6 = (s32[64,1,128]{2,1,0:T(1,128)S(1)}, s32[64,1,128]{2,1,0:T(1,128)}, u32[]{:S(2)}) copy-start(s32[64,1,128]{2,1,0:T(1,128)} %copy-done.5) | copy-start | bytes 98308
  172.7 44.7 %copy-start.12 = (f32[2048]{0:T(1024)S(1)}, f32[2048]{0:T(1024)}, u32[]{:S(2)}) copy-start(f32[2048]{0:T(1024)} %param.15) | copy-start | bytes 24580
  219.0 6.4 %collective-permute-start.3 = (bf16[768,128]{1,0:T(8,128)(2,1)S(1)}, bf16[768,128]{1,0:T(8,128)(2,1)S(1)}, u32[]{:S(2)}, u32[]{:S(2)}) collective-permute-start(bf16[768,128]{1,0:T(8,128)(2,1)S(1)} %get-tuple-element.7), channel_id=1, source_target_pairs={{1,0},{2,1},{3,2},{4,3},{5,4},{6,5},{7,6},{8,7},{9,8},{10,9},{11,1... | collective-permute-start | bytes 589832 | tf_op jit(solution)/shard_map/ppermute | solution.py:19
  219.9 7.1 %collective-permute-start.2 = (bf16[768,128]{1,0:T(8,128)(2,1)S(1)}, bf16[768,128]{1,0:T(8,128)(2,1)S(1)}, u32[]{:S(2)}, u32[]{:S(2)}) collective-permute-start(bf16[768,128]{1,0:T(8,128)(2,1)S(1)} %get-tuple-element.6), channel_id=1, source_target_pairs={{0,1},{1,2},{2,3},{3,4},{4,5},{5,6},{6,7},{7,8},{8,9},{9,10},{10,1... | collective-permute-start | bytes 589832 | tf_op jit(solution)/shard_map/ppermute | solution.py:17
  240.6 6.3 %copy-start.2 = (f32[2048,128]{1,0:T(8,128)S(1)}, f32[2048,128]{1,0:T(8,128)}, u32[]{:S(2)}) copy-start(f32[2048,128]{1,0:T(8,128)} %get-tuple-element.3) | copy-start | bytes 3145732
  247.7 27.7 %copy-start = (f32[2048,128]{1,0:T(8,128)}, f32[2048,128]{1,0:T(8,128)S(1)}, u32[]{:S(2)}) copy-start(f32[2048,128]{1,0:T(8,128)S(1)} %fusion.6) | copy-start | bytes 3145732
  275.5 30.9 %copy-start.14 = (bf16[4096]{0:T(1024)(128)(2,1)S(1)}, bf16[4096]{0:T(1024)(128)(2,1)}, u32[]{:S(2)}) copy-start(bf16[4096]{0:T(1024)(128)(2,1)} %param.11) | copy-start | bytes 24580
  275.5 127.2 %all-to-all-start.2 = ((f32[64,128,128]{2,1,0:T(8,128)}), f32[64,128,128]{2,1,0:T(8,128)}, u32[]{:S(2)}, u32[]{:S(2)}) async-start(f32[64,128,128]{2,1,0:T(8,128)} %bitcast.65), calls=%async_computation.2 | async-start | bytes 8388608 | tf_op jit(solution)/shard_map/all_to_all | solution.py:88
  402.7 40.6 %copy-start.10 = (f32[4096]{0:T(1024)S(1)}, f32[4096]{0:T(1024)}, u32[]{:S(2)}) copy-start(f32[4096]{0:T(1024)} %copy-done.9) | copy-start | bytes 49156
where the time goes:
time: 452 us; the launch traced here: 446 us
  waiting for transfers between devices  168 us (37%)
  local copies, waits for them, and re-layouts  117 us (26%)
  other arithmetic  87.7 us (19%)
  starting transfers between devices  59.7 us (13%)
  matrix products  12.6 us (3%)
    all_to_all x1, waiting for transfers between devices, body(): lax.all_to_all(node_temps, 'dom', split_axis=0, concat_axis=0, tiled=True)  96.2 us
    all_to_all x1, waiting for transfers between devices, body(): lax.all_to_all(loss_buffer, 'dom', split_axis=0, concat_axis=0, tiled=True)  65.7 us
    scatter-add x1, other arithmetic, deposit(): jax.ops.segment_sum(flattened, row_ids.reshape(-1), num_segments=total_rows)  44.7 us
    gather x1, local copies, waits for them, and re-layouts, body(): seen_temps = returned[target, slot_rank]  40.6 us
    all_to_all x1, starting transfers between devices, body(): lax.all_to_all(node_temps, 'dom', split_axis=0, concat_axis=0, tiled=True)  30.9 us
    gather x1, local copies, waits for them, and re-layouts, body(): node_temps = field_now[safe_rows]  27.7 us
    gather x2, local copies, waits for them, and re-layouts, body(): blocks[local_cols].reshape(block_count, col_slots * block_size, samples)  26.9 us
    unnamed x38, local copies, waits for them, and re-layouts  18.7 us
  transfers between devices with their start and end apart: 7, of which 5 were waited for; matrix products, arithmetic and copies ran while one was open for 9% of the time, Pallas kernels for 0%

commit v1 on v0

v1 whole, which is shorter than its diff:
```python
import jax
import jax.numpy as jnp
from jax import lax
from jax.experimental import pallas as pl
from jax.experimental.pallas import tpu as pltpu
from jax.sharding import PartitionSpec as P

HB = 12
CAP = 128
META = 8
LANES = 128
F32 = jnp.float32
BF16 = jnp.bfloat16
VMEM = pl.BlockSpec(memory_space=pltpu.VMEM)
SMEM = pl.BlockSpec(memory_space=pltpu.SMEM)
PARAMS = pltpu.CompilerParams(vmem_limit_bytes=56 * 1024 * 1024)


def dot(a, b):
    return jnp.dot(a, b, preferred_element_type=F32)


def iota(shape, dim):
    return lax.broadcasted_iota(jnp.int32, shape, dim)


def pack_kernel(part_ref, row_ref, res_ref, coef_ref, cur_ref, send_ref, slot_ref, slot_vmem, wide, spread, sem):
    peers = send_ref.shape[0]
    chunks = part_ref.shape[0]
    before = (iota((LANES, LANES), 0) < iota((LANES, LANES), 1)).astype(BF16)
    counter = jnp.concatenate([before, jnp.ones((LANES, LANES), BF16)], axis=1)
    carry = jnp.zeros((peers, LANES), F32)
    meta = jnp.zeros((4 * peers, LANES), F32)
    part = part_ref[...]
    row = row_ref[...]
    high = lax.shift_right_logical(row, 7).astype(F32)
    low = jnp.bitwise_and(row, 127).astype(F32)
    res = res_ref[...].astype(F32)
    coef = coef_ref[...].astype(F32)
    slots = []
    for r in range(chunks):
        hit = (iota((peers, LANES), 0) == part[r : r + 1]).astype(F32)
        counted = dot(hit.astype(BF16), counter)
        rank = jnp.sum(hit * (counted[:, :LANES] + carry), axis=0, keepdims=True)
        carry = carry + counted[:, LANES:]
        rank = rank.astype(jnp.int32)
        slots.append(part[r : r + 1] * CAP + rank)
        place = (iota((CAP, LANES), 0) == rank).astype(F32).astype(BF16)
        values = jnp.concatenate(
            [hit * res[r : r + 1], hit * coef[r : r + 1], hit * high[r : r + 1], hit * low[r : r + 1]], axis=0
        ).astype(BF16)
        meta = meta + lax.dot_general(values, place, (((1,), (1,)), ((), ())), preferred_element_type=F32)
    slot_vmem[...] = jnp.concatenate(slots, axis=0)
    copy = pltpu.make_async_copy(slot_vmem, slot_ref, sem)
    copy.start()
    wide[...] = cur_ref[...].astype(F32)
    spread[...] = jnp.zeros(spread.shape, F32)
    copy.wait()

    def scatter(r, carry):
        for lane in range(LANES):
            spread[pl.ds(slot_ref[r, lane], 1), :] = wide[pl.ds(r * LANES + lane, 1), :]
        return carry

    lax.fori_loop(0, chunks, scatter, 0)
    for p in range(peers):
        send_ref[p, :CAP] = spread[p * CAP : (p + 1) * CAP].astype(BF16)
    rows = [meta[i * peers : (i + 1) * peers] for i in range(4)]
    for p in range(peers):
        own = jnp.concatenate([m[p : p + 1] for m in rows] + [jnp.zeros((META - 4, LANES), F32)], axis=0)
        send_ref[p, CAP:] = own.astype(BF16)


def pack(part, row, res, coef, cur, peers):
    count, samples = cur.shape
    chunks = count // LANES
    return pl.pallas_call(
        pack_kernel,
        out_shape=(
            jax.ShapeDtypeStruct((peers, CAP + META, samples), BF16),
            jax.ShapeDtypeStruct((chunks, LANES), jnp.int32),
        ),
        in_specs=[VMEM] * 5,
        out_specs=(VMEM, SMEM),
        scratch_shapes=[
            pltpu.VMEM((chunks, LANES), jnp.int32),
            pltpu.VMEM((count, samples), F32),
            pltpu.VMEM((peers * CAP, samples), F32),
            pltpu.SemaphoreType.DMA,
        ],
        compiler_params=PARAMS,
        name="pack",
    )(part, row, res, coef, cur)


def apply_blocks(cols_ref, cond_ref, window_ref, r):
    size = cond_ref.shape[1]
    picked = []
    for k in range(cols_ref.shape[1]):
        start = pl.multiple_of(cols_ref[r, k] * size, size)
        picked.append(window_ref[pl.ds(start, size), :])
    return dot(cond_ref[r], jnp.concatenate(picked, axis=0))


def first_kernel(cols_ref, cond_ref, window_ref, cap_ref, applied_ref, pivot_ref):
    blocks, size, _ = cond_ref.shape
    samples = window_ref.shape[1]
    eye = iota((size, size), 0) == iota((size, size), 1)

    def step(r, carry):
        rows = pl.ds(pl.multiple_of(r * size, size), size)
        applied_ref[rows, :] = apply_blocks(cols_ref, cond_ref, window_ref, r)
        corner = cond_ref[r, :, :size].astype(F32)
        diag = jnp.sum(jnp.where(eye, corner, 0.0), axis=1, keepdims=True)
        pivot = diag + cap_ref[rows, :]
        pivot_ref[rows, :] = jnp.broadcast_to(1.0 / pivot, (size, samples))
        return carry

    lax.fori_loop(0, blocks, step, 0, unroll=2)


def first_sweep(cols, cond, window, cap):
    nodes = cond.shape[0] * cond.shape[1]
    samples = window.shape[1]
    return pl.pallas_call(
        first_kernel,
        out_shape=(jax.ShapeDtypeStruct((nodes, samples), F32),) * 2,
        in_specs=[SMEM, VMEM, VMEM, VMEM],
        out_specs=(VMEM, VMEM),
        compiler_params=PARAMS,
        cost_estimate=pl.CostEstimate(flops=8_000_000_000, bytes_accessed=8_000_000, transcendentals=0),
        name="first_sweep",
    )(cols, cond, window, cap)


GROUP = 8


def gather_kernel(recv_ref, old_ref, cap_ref, applied_ref, pivot_ref, field_ref, right_ref, low_ref, chosen, values, total):
    peers = recv_ref.shape[0]
    nodes, samples = old_ref.shape
    tiles = nodes // LANES
    sub = iota((LANES, LANES), 0).astype(F32)
    total[...] = jnp.zeros(total.shape, F32)

    def step(g, carry):
        for j in range(GROUP):
            p = g * GROUP + j
            cur = recv_ref[p, :CAP].astype(F32)
            square = cur * cur
            top = square.astype(BF16)
            rest = (square - top.astype(F32)).astype(BF16)
            values[j * CAP : (j + 1) * CAP, :] = jnp.concatenate([top, rest], axis=1)
            meta = recv_ref[p, CAP:].astype(F32)
            low_hit = jnp.where(sub == meta[3:4], meta[0:1], 0.0).astype(BF16)
            for t in range(tiles):
                high_hit = jnp.where(meta[2:3] == float(t), 1.0, 0.0)
                high_hit = jnp.broadcast_to(high_hit, (LANES, CAP)).astype(BF16)
                chosen[t * LANES : (t + 1) * LANES, j * CAP : (j + 1) * CAP] = low_hit * high_hit
        total[...] += dot(chosen[...], values[...])
        return carry

    lax.fori_loop(0, peers // GROUP, step, 0)
    heat = total[:, :samples] + total[:, samples:]
    old = old_ref[...]
    field = old + (heat - applied_ref[...]) * pivot_ref[...]
    field_ref[...] = field
    right_ref[...] = cap_ref[...] * old + heat
    low_ref[...] = field.astype(BF16)


def gather_heat(recv, old, cap, applied, pivot):
    nodes, samples = old.shape
    return pl.pallas_call(
        gather_kernel,
        out_shape=(
            jax.ShapeDtypeStruct((nodes, samples), F32),
            jax.ShapeDtypeStruct((nodes, samples), F32),
            jax.ShapeDtypeStruct((nodes, samples), BF16),
        ),
        in_specs=[VMEM] * 5,
        out_specs=(VMEM,) * 3,
        scratch_shapes=[
            pltpu.VMEM((nodes, GROUP * CAP), BF16),
            pltpu.VMEM((GROUP * CAP, 2 * samples), BF16),
            pltpu.VMEM((nodes, 2 * samples), F32),
        ],
        compiler_params=PARAMS,
        name="gather_heat",
    )(recv, old, cap, applied, pivot)


def last_kernel(cols_ref, cond_ref, window_ref, cap_ref, pivot_ref, field_ref, right_ref, recv_ref, temp_ref, back_ref, pair, columns):
    blocks, size, _ = cond_ref.shape
    nodes, samples = field_ref.shape
    peers = recv_ref.shape[0]
    tiles = nodes // LANES

    def step(r, carry):
        rows = pl.ds(pl.multiple_of(r * size, size), size)
        applied = apply_blocks(cols_ref, cond_ref, window_ref, r)
        field = field_ref[rows, :]
        temp = field + (right_ref[rows, :] - cap_ref[rows, :] * field - applied) * pivot_ref[rows, :]
        temp_ref[rows, :] = temp
        top = temp.astype(BF16)
        rest = (temp - top.astype(F32)).astype(BF16)
        pair[rows, :] = jnp.concatenate([top, rest], axis=1)
        return carry

    lax.fori_loop(0, blocks, step, 0, unroll=2)
    for g in range(peers // 16):
        stacked = jnp.concatenate([recv_ref[g * 16 + j, CAP:].astype(F32) for j in range(16)], axis=0)
        columns[g] = stacked.T
    lane = iota((CAP, LANES), 1).astype(F32)

    def send(g, carry):
        for j in range(16):
            own = columns[g, :, j * META : j * META + 4]
            low = jnp.broadcast_to(own[:, 3:4], (CAP, LANES))
            low_hit = jnp.where(low == lane, 1.0, 0.0).astype(BF16)
            high = jnp.broadcast_to(own[:, 2:3], (CAP, LANES))
            hits = [low_hit * jnp.where(high == float(t), 1.0, 0.0).astype(BF16) for t in range(tiles)]
            both = dot(jnp.concatenate(hits, axis=1), pair[...])
            seen = both[:, :samples] + both[:, samples:]
            back_ref[g * 16 + j] = (own[:, 0:1] * (1.0 + own[:, 1:2] * seen)).astype(BF16)
        return carry

    lax.fori_loop(0, peers // 16, send, 0)


def last_sweep(cols, cond, window, cap, pivot, field, right, recv):
    nodes, samples = field.shape
    peers = recv.shape[0]
    return pl.pallas_call(
        last_kernel,
        out_shape=(
            jax.ShapeDtypeStruct((nodes, samples), F32),
            jax.ShapeDtypeStruct((peers, CAP, samples), BF16),
        ),
        in_specs=[SMEM] + [VMEM] * 7,
        out_specs=(VMEM, VMEM),
        scratch_shapes=[
            pltpu.VMEM((nodes, 2 * samples), BF16),
            pltpu.VMEM((peers // 16, CAP, LANES), F32),
        ],
        compiler_params=PARAMS,
        name="last_sweep",
    )(cols, cond, window, cap, pivot, field, right, recv)


def unpack_kernel(slot_ref, back_ref, out_ref, wide, picked):
    peers, _, samples = back_ref.shape
    for p in range(peers):
        wide[p * CAP : (p + 1) * CAP] = back_ref[p].astype(F32)

    def gather(r, carry):
        for lane in range(LANES):
            picked[pl.ds(r * LANES + lane, 1), :] = wide[pl.ds(slot_ref[r, lane], 1), :]
        return carry

    lax.fori_loop(0, slot_ref.shape[0], gather, 0)
    out_ref[...] = picked[...].astype(BF16)


def unpack(slots, back):
    peers, _, samples = back.shape
    count = slots.shape[0] * slots.shape[1]
    return pl.pallas_call(
        unpack_kernel,
        out_shape=jax.ShapeDtypeStruct((count, samples), BF16),
        in_specs=[SMEM, VMEM],
        out_specs=VMEM,
        scratch_shapes=[pltpu.VMEM((peers * CAP, samples), F32), pltpu.VMEM((count, samples), F32)],
        compiler_params=PARAMS,
        name="unpack",
    )(slots, back)


def extended(cells, width):
    axes = ("dom", "blk")
    count = lax.axis_size(axes)
    head = cells[:width]
    tail = cells[cells.shape[0] - width :]
    return jnp.concatenate(
        [
            lax.ppermute(tail, axes, [(i, (i + 1) % count) for i in range(count)]),
            cells,
            lax.ppermute(head, axes, [((i + 1) % count, i) for i in range(count)]),
        ],
        axis=0,
    )


def body(current, resistivity, temp_coef, dest_part, dest_row, temp_old, heat_cap, conduction, block_cols):
    count, samples = current.shape
    peers = lax.axis_size("dom")
    blocks, size, _ = conduction.shape
    chunks = count // LANES
    send, slots = pack(
        dest_part.reshape(chunks, LANES),
        dest_row.reshape(chunks, LANES),
        resistivity.reshape(chunks, LANES),
        temp_coef.reshape(chunks, LANES),
        current,
        peers,
    )
    recv = lax.all_to_all(send, "dom", split_axis=0, concat_axis=0, tiled=True)
    devices = lax.axis_size(("dom", "blk"))
    first_block = lax.axis_index(("dom", "blk")) * blocks
    cols = jnp.mod(block_cols - first_block + HB, blocks * devices)
    cap = heat_cap[:, None]
    window = extended(temp_old.astype(BF16), HB * size)
    applied, pivot = first_sweep(cols, conduction, window, cap)
    field, right, low = gather_heat(recv, temp_old, cap, applied, pivot)
    window = extended(low, HB * size)
    temp, back = last_sweep(cols, conduction, window, cap, pivot, field, right, recv)
    returned = lax.all_to_all(back, "dom", split_axis=0, concat_axis=0, tiled=True)
    return temp, unpack(slots, returned)


def solution(mesh):
    both = ("dom", "blk")
    placed = (
        P(both, None),
        P(both),
        P(both),
        P(both, None),
        P(both),
        P(both, None),
        P(both),
        P(both, None, None),
        P(both, None),
    )
    return jax.shard_map(
        body,
        mesh=mesh,
        in_specs=placed,
        out_specs=(P(both, None), P(both, None)),
        check_vma=False,
    )
```

time: 452 us -> 206 us (0.46); the launches traced: 446 us -> 206 us
  waiting for transfers between devices: 168 us -> 44.3 us
  local copies, waits for them, and re-layouts: 117 us -> 4.68 us
  other arithmetic: 87.7 us -> 4.79 us
  blocking collectives: 0 us -> 76.3 us
  Pallas kernels: 0 us -> 58.6 us
  starting transfers between devices: 59.7 us -> 16.5 us
  matrix products: 12.6 us -> 0 us
    all_to_all x3 -> x1, waiting for transfers between devices: 162 us -> 36.4 us  [body(): recv = lax.all_to_all(send, 'dom', split_axis=0, concat_axis=0, tiled=True)]
    gather x5 -> x0, local copies, waits for them, and re-layouts: 96.9 us -> none  [the longest x1 40.6 us: body(): seen_temps = returned[target, slot_rank]]
    all_to_all x0 -> x1, blocking collectives: none -> 76.3 us  [body(): lax.all_to_all(back, 'dom', split_axis=0, concat_axis=0, tiled=True)]
    pallas_call x0 -> x5, Pallas kernels: none -> 58.6 us  [the longest x1 19.5 us: last_sweep(): pl.pallas_call(last_kernel, out_shape=(jax.ShapeDtypeStruct((nodes, sampl...]
    scatter-add x1 -> x0, other arithmetic: 44.7 us -> none  [deposit(): jax.ops.segment_sum(flattened, row_ids.reshape(-1), num_segments=total_rows)]
    all_to_all x3 -> x1, starting transfers between devices: 53.7 us -> 12.2 us  [body(): recv = lax.all_to_all(send, 'dom', split_axis=0, concat_axis=0, tiled=True)]
    another operation x2 -> x0, other arithmetic: 18.6 us -> none
    unnamed x38 -> x11, local copies, waits for them, and re-layouts: 18.7 us -> 2.26 us
  transfers between devices with their start and end apart: 7 -> 5, of which waited for: 5 -> 3; matrix products, arithmetic and copies ran while one was open for 9% -> 2% of each run, Pallas kernels for 0% -> 4%
where the time goes in v1:
time: 206 us
  blocking collectives  76.3 us (37%)
  Pallas kernels  58.6 us (28%)
  waiting for transfers between devices  44.3 us (22%)
  starting transfers between devices  16.5 us (8%)
  other arithmetic  4.79 us (2%)
  local copies, waits for them, and re-layouts  4.68 us (2%)
    all_to_all x1, blocking collectives, body(): lax.all_to_all(back, 'dom', split_axis=0, concat_axis=0, tiled=True)  76.3 us
    all_to_all x1, waiting for transfers between devices, body(): recv = lax.all_to_all(send, 'dom', split_axis=0, concat_axis=0, tiled=True)  36.4 us
    pallas_call x1, Pallas kernels, last_sweep(): pl.pallas_call(last_kernel, out_shape=(jax.ShapeDtypeStruct((nodes, sampl...  19.5 us
    pallas_call x1, Pallas kernels, gather_heat(): pl.pallas_call(gather_kernel, out_shape=(jax.ShapeDtypeStruct((nodes, sam...  15.6 us
    all_to_all x1, starting transfers between devices, body(): recv = lax.all_to_all(send, 'dom', split_axis=0, concat_axis=0, tiled=True)  12.2 us
    pallas_call x1, Pallas kernels, pack(): pl.pallas_call(pack_kernel, out_shape=(jax.ShapeDtypeStruct((peers, CAP +...  9.4 us
    ppermute x2, waiting for transfers between devices, extended(): lax.ppermute(tail, axes, [(i, (i + 1) % count) for i in range(count)])  7.9 us
    pallas_call x1, Pallas kernels, first_sweep(): pl.pallas_call(first_kernel, out_shape=(jax.ShapeDtypeStruct((nodes, samp...  7.84 us
  transfers between devices with their start and end apart: 5, of which 3 were waited for; matrix products, arithmetic and copies ran while one was open for 2% of the time, Pallas kernels for 4%

profile of v1, /device:TPU:6, one launch (start us, length us, event | category | flops | bytes accessed | tf_op | source)
XLA Modules:
  0.0 205.9 jit_solution(12240979065792582441)
XLA Ops:
  0.6 9.4 %pack.1 = (bf16[64,136,128]{2,1,0:T(8,128)(2,1)}, s32[32,128]{1,0:T(8,128)}) custom-call(s32[32,128]{1,0:T(8,128)} %bitcast.5, s32[32,128]{1,0:T(8,128)} %bitcast.6, bf16[32,128]{1,0:T(8,128)(2,1)} %bitcast.7, bf16[32,128]{1,0:T(8,128)(2,1)} %bitcast.8, bf16[4096,128]{1,0:T(8,128)(2,1)} %cur_ref.1), custom_call_target="tpu_custom_call" | custom-call | tf_op jit(solution)/shard_map/pack/pallas_call | solution.py:77
  10.0 0.0 copy-start.1
  10.1 12.2 %all-to-all-start = ((bf16[64,136,128]{2,1,0:T(8,128)(2,1)}), bf16[64,136,128]{2,1,0:T(8,128)(2,1)S(1)}, u32[]{:S(2)}, u32[]{:S(2)}) async-start(bf16[64,136,128]{2,1,0:T(8,128)(2,1)} %get-tuple-element.11), calls=%async_computation | async-start | bytes 4456448 | tf_op jit(solution)/shard_map/all_to_all | solution.py:307
  22.3 0.0 copy-done.1
  22.3 0.0 copy-start.4
  22.3 0.0 copy-start.3
  22.3 0.1 convert_element_type.3
  22.4 0.0 copy-start.2
  22.4 0.8 copy-done.2
  23.2 0.2 collective-permute-start
  23.5 1.9 collective-permute-start.1
  25.3 0.0 copy-done.4
  25.3 0.1 copy.12
  25.4 0.0 copy-done.3
  25.4 1.3 copy.14.cap_ref
  26.8 0.6 add_select_fusion.cols_ref
  27.4 2.8 %collective-permute-done = bf16[768,128]{1,0:T(8,128)(2,1)S(1)} collective-permute-done((bf16[768,128]{1,0:T(8,128)(2,1)S(1)}, bf16[768,128]{1,0:T(8,128)(2,1)S(1)}, u32[]{:S(2)}, u32[]{:S(2)}) %collective-permute-start) | collective-permute-done | bytes 196640 | tf_op jit(solution)/shard_map/ppermute | solution.py:286
  30.2 0.0 collective-permute-done.1
  30.2 2.0 pad_maximum_fusion.window_ref
  32.2 7.8 %first_sweep.1 = (f32[2048,128]{1,0:T(8,128)}, f32[2048,128]{1,0:T(8,128)}) custom-call(s32[32,16]{1,0:T(8,128)} %add_select_fusion.cols_ref, bf16[32,64,1024]{2,1,0:T(8,128)(2,1)} %cond_ref.3, bf16[3584,128]{1,0:T(8,128)(2,1)} %pad_maximum_fusion.window_ref, f32[2048,1]{1,0:T(8,128)} %copy.14.cap_ref), custom_call_target="tpu_custom_call" | custom-call | flops 8000000000 | bytes 8000000 | tf_op jit(solution)/shard_map/first_sweep/pallas_call | solution.py:125
  40.0 36.4 %all-to-all-done.recv_ref = bf16[64,136,128]{2,1,0:T(8,128)(2,1)S(1)} async-done(((bf16[64,136,128]{2,1,0:T(8,128)(2,1)}), bf16[64,136,128]{2,1,0:T(8,128)(2,1)S(1)}, u32[]{:S(2)}, u32[]{:S(2)}) %all-to-all-start) | async-done | bytes 2228256 | tf_op jit(solution)/shard_map/all_to_all | solution.py:307
  76.5 1.4 copy-done
  77.9 15.6 %gather_heat.1 = (f32[2048,128]{1,0:T(8,128)}, f32[2048,128]{1,0:T(8,128)}, bf16[2048,128]{1,0:T(8,128)(2,1)}) custom-call(bf16[64,136,128]{2,1,0:T(8,128)(2,1)} %copy-done, f32[2048,128]{1,0:T(8,128)} %old_ref.1, f32[2048,1]{1,0:T(8,128)} %copy.14.cap_ref, f32[2048,128]{1,0:T(8,128)} %get-tuple-element.12.applied_ref, f32[2048,128]{1,0:T(8,128)} %get-tuple-element.13.pivot_ref), custom_call_target="tpu_custom_call" | custom-call | tf_op jit(solution)/shard_map/gather_heat/pallas_call | solution.py:174
  93.4 1.0 fusion.1
  94.5 0.1 collective-permute-start.2
  94.6 2.0 collective-permute-start.3
  96.6 5.1 %collective-permute-done.2 = bf16[768,128]{1,0:T(8,128)(2,1)S(1)} collective-permute-done((bf16[768,128]{1,0:T(8,128)(2,1)S(1)}, bf16[768,128]{1,0:T(8,128)(2,1)S(1)}, u32[]{:S(2)}, u32[]{:S(2)}) %collective-permute-start.2) | collective-permute-done | bytes 196640 | tf_op jit(solution)/shard_map/ppermute | solution.py:286
  101.7 0.0 collective-permute-done.3
  101.7 2.1 %pad_maximum_fusion.1.window_ref = bf16[3584,128]{1,0:T(8,128)(2,1)} fusion(bf16[768,128]{1,0:T(8,128)(2,1)S(1)} %collective-permute-done.3, bf16[2048,128]{1,0:T(8,128)(2,1)} %get-tuple-element.14, bf16[768,128]{1,0:T(8,128)(2,1)S(1)} %collective-permute-done.2), kind=kLoop, calls=%fused_computation.1 | loop fusion | flops 2752512 | bytes 1835008 | tf_op jit(solution)/shard_map/concatenate | solution.py:284
  103.8 19.5 %last_sweep.1 = (f32[2048,128]{1,0:T(8,128)}, bf16[64,128,128]{2,1,0:T(8,128)(2,1)}) custom-call(s32[32,16]{1,0:T(8,128)} %add_select_fusion.cols_ref, bf16[32,64,1024]{2,1,0:T(8,128)(2,1)} %cond_ref.3, bf16[3584,128]{1,0:T(8,128)(2,1)} %pad_maximum_fusion.1.window_ref, f32[2048,1]{1,0:T(8,128)} %copy.14.cap_ref, f32[2048,128]{1,0:T(8,128)} %get-tuple-element.13.pivot_ref, ...), custom_call_target="tpu_custom_call" | custom-call | tf_op jit(solution)/shard_map/last_sweep/pallas_call | solution.py:234
  123.3 76.3 %all_to_all.10.back_ref = bf16[64,128,128]{2,1,0:T(8,128)(2,1)} all-to-all(bf16[64,128,128]{2,1,0:T(8,128)(2,1)} %get-tuple-element.19), channel_id=1, replica_groups=mesh['dom'=64,'blk'=4] {'dom'}, dimensions={0} | all-to-all | bytes 4194304 | tf_op jit(solution)/shard_map/all_to_all | solution.py:317
  199.5 6.3 %unpack.1 = bf16[4096,128]{1,0:T(8,128)(2,1)} custom-call(s32[32,128]{1,0:T(8,128)} %get-tuple-element.18.slot_ref, bf16[64,128,128]{2,1,0:T(8,128)(2,1)} %all_to_all.10.back_ref), custom_call_target="tpu_custom_call" | custom-call | tf_op jit(solution)/shard_map/unpack/pallas_call | solution.py:268
  (2 shorter events, 0.0 us)
Async XLA Ops:
  10.0 12.3 %copy-start.1 = (f32[2048,128]{1,0:T(8,128)S(1)}, f32[2048,128]{1,0:T(8,128)}, u32[]{:S(2)}) copy-start(f32[2048,128]{1,0:T(8,128)} %old_ref.1) | copy-start | bytes 3145732
  10.1 66.4 %all-to-all-start = ((bf16[64,136,128]{2,1,0:T(8,128)(2,1)}), bf16[64,136,128]{2,1,0:T(8,128)(2,1)S(1)}, u32[]{:S(2)}, u32[]{:S(2)}) async-start(bf16[64,136,128]{2,1,0:T(8,128)(2,1)} %get-tuple-element.11), calls=%async_computation | async-start | bytes 4456448 | tf_op jit(solution)/shard_map/all_to_all | solution.py:307
  22.3 3.0 %copy-start.4 = (s32[32,16]{0,1:T(8,128)S(1)}, s32[32,16]{0,1:T(8,128)}, u32[]{:S(2)}) copy-start(s32[32,16]{0,1:T(8,128)} %param.17) | copy-start | bytes 6148
  22.3 3.1 %copy-start.3 = (f32[2048]{0:T(1024)S(1)}, f32[2048]{0:T(1024)}, u32[]{:S(2)}) copy-start(f32[2048]{0:T(1024)} %param.15) | copy-start | bytes 24580
  22.4 0.8 copy-start.2
  23.2 6.9 %collective-permute-start = (bf16[768,128]{1,0:T(8,128)(2,1)S(1)}, bf16[768,128]{1,0:T(8,128)(2,1)S(1)}, u32[]{:S(2)}, u32[]{:S(2)}) collective-permute-start(bf16[768,128]{1,0:T(8,128)(2,1)S(1)} %get-tuple-element.22), channel_id=1, source_target_pairs={{0,1},{1,2},{2,3},{3,4},{4,5},{5,6},{6,7},{7,8},{8,9},{9,10},{10,1... | collective-permute-start | bytes 589832 | tf_op jit(solution)/shard_map/ppermute | solution.py:286
  23.5 6.7 %collective-permute-start.1 = (bf16[768,128]{1,0:T(8,128)(2,1)S(1)}, bf16[768,128]{1,0:T(8,128)(2,1)S(1)}, u32[]{:S(2)}, u32[]{:S(2)}) collective-permute-start(bf16[768,128]{1,0:T(8,128)(2,1)S(1)} %get-tuple-element.23), channel_id=1, source_target_pairs={{1,0},{2,1},{3,2},{4,3},{5,4},{6,5},{7,6},{8,7},{9,8},{10,9},{11,1... | collective-permute-start | bytes 589832 | tf_op jit(solution)/shard_map/ppermute | solution.py:288
  76.5 1.4 copy-start
  94.5 7.2 %collective-permute-start.2 = (bf16[768,128]{1,0:T(8,128)(2,1)S(1)}, bf16[768,128]{1,0:T(8,128)(2,1)S(1)}, u32[]{:S(2)}, u32[]{:S(2)}) collective-permute-start(bf16[768,128]{1,0:T(8,128)(2,1)S(1)} %get-tuple-element.20), channel_id=1, source_target_pairs={{0,1},{1,2},{2,3},{3,4},{4,5},{5,6},{6,7},{7,8},{8,9},{9,10},{10,1... | collective-permute-start | bytes 589832 | tf_op jit(solution)/shard_map/ppermute | solution.py:286
  94.6 7.1 %collective-permute-start.3 = (bf16[768,128]{1,0:T(8,128)(2,1)S(1)}, bf16[768,128]{1,0:T(8,128)(2,1)S(1)}, u32[]{:S(2)}, u32[]{:S(2)}) collective-permute-start(bf16[768,128]{1,0:T(8,128)(2,1)S(1)} %get-tuple-element.21), channel_id=1, source_target_pairs={{1,0},{2,1},{3,2},{4,3},{5,4},{6,5},{7,6},{8,7},{9,8},{10,9},{11,1... | collective-permute-start | bytes 589832 | tf_op jit(solution)/shard_map/ppermute | solution.py:288

commit v2 on v1

--- a/solution.py
+++ b/solution.py
@@ -13,7 +13,10 @@
 BF16 = jnp.bfloat16
 VMEM = pl.BlockSpec(memory_space=pltpu.VMEM)
 SMEM = pl.BlockSpec(memory_space=pltpu.SMEM)
-PARAMS = pltpu.CompilerParams(vmem_limit_bytes=56 * 1024 * 1024)
+
+
+def params(mib):
+    return pltpu.CompilerParams(vmem_limit_bytes=mib * 1024 * 1024)
 
 
 def dot(a, b):
@@ -88,7 +91,7 @@
             pltpu.VMEM((peers * CAP, samples), F32),
             pltpu.SemaphoreType.DMA,
         ],
-        compiler_params=PARAMS,
+        compiler_params=params(24),
         name="pack",
     )(part, row, res, coef, cur)
 
@@ -102,7 +105,15 @@
     return dot(cond_ref[r], jnp.concatenate(picked, axis=0))
 
 
-def first_kernel(cols_ref, cond_ref, window_ref, cap_ref, applied_ref, pivot_ref):
+def fill(window_ref, left_ref, own_ref, right_ref):
+    width, nodes = left_ref.shape[0], own_ref.shape[0]
+    window_ref[:width] = left_ref[...]
+    window_ref[width : width + nodes] = own_ref[...].astype(BF16)
+    window_ref[width + nodes :] = right_ref[...]
+
+
+def first_kernel(cols_ref, cond_ref, left_ref, old_ref, right_ref, cap_ref, applied_ref, pivot_ref, window_ref):
+    fill(window_ref, left_ref, old_ref, right_ref)
     blocks, size, _ = cond_ref.shape
     samples = window_ref.shape[1]
     eye = iota((size, size), 0) == iota((size, size), 1)
@@ -116,84 +127,105 @@
         pivot_ref[rows, :] = jnp.broadcast_to(1.0 / pivot, (size, samples))
         return carry
 
-    lax.fori_loop(0, blocks, step, 0, unroll=2)
-
-
-def first_sweep(cols, cond, window, cap):
+    lax.fori_loop(0, blocks, step, 0, unroll=8)
+
+
+def first_sweep(cols, cond, left, old, right, cap):
     nodes = cond.shape[0] * cond.shape[1]
-    samples = window.shape[1]
+    samples = old.shape[1]
     return pl.pallas_call(
         first_kernel,
         out_shape=(jax.ShapeDtypeStruct((nodes, samples), F32),) * 2,
-        in_specs=[SMEM, VMEM, VMEM, VMEM],
+        in_specs=[SMEM] + [VMEM] * 5,
         out_specs=(VMEM, VMEM),
-        compiler_params=PARAMS,
+        scratch_shapes=[pltpu.VMEM((nodes + 2 * left.shape[0], samples), BF16)],
+        compiler_params=params(16),
         cost_estimate=pl.CostEstimate(flops=8_000_000_000, bytes_accessed=8_000_000, transcendentals=0),
         name="first_sweep",
-    )(cols, cond, window, cap)
-
-
-GROUP = 8
-
-
-def gather_kernel(recv_ref, old_ref, cap_ref, applied_ref, pivot_ref, field_ref, right_ref, low_ref, chosen, values, total):
+    )(cols, cond, left, old, right, cap)
+
+
+MT = 4
+STEP = 8
+
+
+def gather_kernel(recv_ref, old_ref, cap_ref, applied_ref, pivot_ref, field_ref, right_ref, low_ref, head_ref, tail_ref, base, high, values):
     peers = recv_ref.shape[0]
     nodes, samples = old_ref.shape
     tiles = nodes // LANES
+    outer = head_ref.shape[0] // LANES
     sub = iota((LANES, LANES), 0).astype(F32)
-    total[...] = jnp.zeros(total.shape, F32)
-
-    def step(g, carry):
-        for j in range(GROUP):
-            p = g * GROUP + j
-            cur = recv_ref[p, :CAP].astype(F32)
-            square = cur * cur
-            top = square.astype(BF16)
-            rest = (square - top.astype(F32)).astype(BF16)
-            values[j * CAP : (j + 1) * CAP, :] = jnp.concatenate([top, rest], axis=1)
-            meta = recv_ref[p, CAP:].astype(F32)
-            low_hit = jnp.where(sub == meta[3:4], meta[0:1], 0.0).astype(BF16)
-            for t in range(tiles):
-                high_hit = jnp.where(meta[2:3] == float(t), 1.0, 0.0)
-                high_hit = jnp.broadcast_to(high_hit, (LANES, CAP)).astype(BF16)
-                chosen[t * LANES : (t + 1) * LANES, j * CAP : (j + 1) * CAP] = low_hit * high_hit
-        total[...] += dot(chosen[...], values[...])
-        return carry
-
-    lax.fori_loop(0, peers // GROUP, step, 0)
-    heat = total[:, :samples] + total[:, samples:]
-    old = old_ref[...]
-    field = old + (heat - applied_ref[...]) * pivot_ref[...]
-    field_ref[...] = field
-    right_ref[...] = cap_ref[...] * old + heat
-    low_ref[...] = field.astype(BF16)
-
-
-def gather_heat(recv, old, cap, applied, pivot):
+
+    def split(p, carry):
+        rows = pl.ds(pl.multiple_of(p * CAP, CAP), CAP)
+        cur = recv_ref[p, :CAP].astype(F32)
+        square = cur * cur
+        top = square.astype(BF16)
+        rest = (square - top.astype(F32)).astype(BF16)
+        values[rows, :] = jnp.concatenate([top, rest], axis=1)
+        meta = recv_ref[p, CAP:].astype(F32)
+        base[:, rows] = jnp.where(sub == meta[3:4], meta[0:1], 0.0).astype(BF16)
+        high[:, rows] = jnp.broadcast_to(meta[2:3], (16, CAP)).astype(BF16)
+        return carry
+
+    lax.fori_loop(0, peers, split, 0, unroll=4)
+    part = peers * CAP // STEP
+
+    def tile(t, carry):
+        both = jnp.zeros((MT * LANES, 2 * samples), F32)
+        for c in range(STEP):
+            cols = slice(c * part, (c + 1) * part)
+            own_base = base[:, cols]
+            own_high = high[:, cols]
+            hits = []
+            for i in range(MT):
+                own = (t * MT + i).astype(F32).astype(BF16)
+                hit = (own_high == own).astype(BF16)
+                hits.append(own_base * jnp.concatenate([hit] * (LANES // 16), axis=0))
+            both = both + dot(jnp.concatenate(hits, axis=0), values[cols, :])
+        rows = pl.ds(pl.multiple_of(t * MT * LANES, LANES), MT * LANES)
+        heat = both[:, :samples] + both[:, samples:]
+        old = old_ref[rows, :]
+        field = old + (heat - applied_ref[rows, :]) * pivot_ref[rows, :]
+        field_ref[rows, :] = field
+        right_ref[rows, :] = cap_ref[rows, :] * old + heat
+        low_ref[rows, :] = field.astype(BF16)
+        return carry
+
+    lax.fori_loop(0, tiles // MT, tile, 0)
+    head_ref[...] = low_ref[: outer * LANES]
+    tail_ref[...] = low_ref[nodes - outer * LANES :]
+
+
+def gather_heat(recv, old, cap, applied, pivot, width):
     nodes, samples = old.shape
+    slots = recv.shape[0] * CAP
     return pl.pallas_call(
         gather_kernel,
         out_shape=(
             jax.ShapeDtypeStruct((nodes, samples), F32),
             jax.ShapeDtypeStruct((nodes, samples), F32),
             jax.ShapeDtypeStruct((nodes, samples), BF16),
+            jax.ShapeDtypeStruct((width, samples), BF16),
+            jax.ShapeDtypeStruct((width, samples), BF16),
         ),
         in_specs=[VMEM] * 5,
-        out_specs=(VMEM,) * 3,
+        out_specs=(VMEM,) * 5,
         scratch_shapes=[
-            pltpu.VMEM((nodes, GROUP * CAP), BF16),
-            pltpu.VMEM((GROUP * CAP, 2 * samples), BF16),
-            pltpu.VMEM((nodes, 2 * samples), F32),
+            pltpu.VMEM((LANES, slots), BF16),
+            pltpu.VMEM((16, slots), BF16),
+            pltpu.VMEM((slots, 2 * samples), BF16),
         ],
-        compiler_params=PARAMS,
+        compiler_params=params(24),
         name="gather_heat",
     )(recv, old, cap, applied, pivot)
 
 
-def last_kernel(cols_ref, cond_ref, window_ref, cap_ref, pivot_ref, field_ref, right_ref, recv_ref, temp_ref, back_ref, pair, columns):
+def last_kernel(cols_ref, cond_ref, left_ref, low_ref, next_ref, cap_ref, pivot_ref, field_ref, right_ref, meta_ref, temp_ref, back_ref, window_ref, pair, columns):
+    fill(window_ref, left_ref, low_ref, next_ref)
     blocks, size, _ = cond_ref.shape
     nodes, samples = field_ref.shape
-    peers = recv_ref.shape[0]
+    peers = meta_ref.shape[0]
     tiles = nodes // LANES
 
     def step(r, carry):
@@ -207,9 +239,9 @@
         pair[rows, :] = jnp.concatenate([top, rest], axis=1)
         return carry
 
-    lax.fori_loop(0, blocks, step, 0, unroll=2)
+    lax.fori_loop(0, blocks, step, 0, unroll=8)
     for g in range(peers // 16):
-        stacked = jnp.concatenate([recv_ref[g * 16 + j, CAP:].astype(F32) for j in range(16)], axis=0)
+        stacked = jnp.concatenate([meta_ref[g * 16 + j].astype(F32) for j in range(16)], axis=0)
         columns[g] = stacked.T
     lane = iota((CAP, LANES), 1).astype(F32)
 
@@ -228,24 +260,25 @@
     lax.fori_loop(0, peers // 16, send, 0)
 
 
-def last_sweep(cols, cond, window, cap, pivot, field, right, recv):
+def last_sweep(cols, cond, left, low, next, cap, pivot, field, right, meta):
     nodes, samples = field.shape
-    peers = recv.shape[0]
+    peers = meta.shape[0]
     return pl.pallas_call(
         last_kernel,
         out_shape=(
             jax.ShapeDtypeStruct((nodes, samples), F32),
             jax.ShapeDtypeStruct((peers, CAP, samples), BF16),
         ),
-        in_specs=[SMEM] + [VMEM] * 7,
+        in_specs=[SMEM] + [VMEM] * 9,
         out_specs=(VMEM, VMEM),
         scratch_shapes=[
+            pltpu.VMEM((nodes + 2 * left.shape[0], samples), BF16),
             pltpu.VMEM((nodes, 2 * samples), BF16),
             pltpu.VMEM((peers // 16, CAP, LANES), F32),
         ],
-        compiler_params=PARAMS,
+        compiler_params=params(24),
         name="last_sweep",
-    )(cols, cond, window, cap, pivot, field, right, recv)
+    )(cols, cond, left, low, next, cap, pivot, field, right, meta)
 
 
 def unpack_kernel(slot_ref, back_ref, out_ref, wide, picked):
@@ -271,24 +304,17 @@
         in_specs=[SMEM, VMEM],
         out_specs=VMEM,
         scratch_shapes=[pltpu.VMEM((peers * CAP, samples), F32), pltpu.VMEM((count, samples), F32)],
-        compiler_params=PARAMS,
+        compiler_params=params(24),
         name="unpack",
     )(slots, back)
 
 
-def extended(cells, width):
+def halo(head, tail):
     axes = ("dom", "blk")
     count = lax.axis_size(axes)
-    head = cells[:width]
-    tail = cells[cells.shape[0] - width :]
-    return jnp.concatenate(
-        [
-            lax.ppermute(tail, axes, [(i, (i + 1) % count) for i in range(count)]),
-            cells,
-            lax.ppermute(head, axes, [((i + 1) % count, i) for i in range(count)]),
-        ],
-        axis=0,
-    )
+    left = lax.ppermute(tail, axes, [(i, (i + 1) % count) for i in range(count)])
+    right = lax.ppermute(head, axes, [((i + 1) % count, i) for i in range(count)])
+    return left, right
 
 
 def body(current, resistivity, temp_coef, dest_part, dest_row, temp_old, heat_cap, conduction, block_cols):
@@ -296,6 +322,8 @@
     peers = lax.axis_size("dom")
     blocks, size, _ = conduction.shape
     chunks = count // LANES
+    width = HB * size
+    left, right = halo(temp_old[:width].astype(BF16), temp_old[-width:].astype(BF16))
     send, slots = pack(
         dest_part.reshape(chunks, LANES),
         dest_row.reshape(chunks, LANES),
@@ -304,16 +332,16 @@
         current,
         peers,
     )
+    send, left, right = lax.optimization_barrier((send, left, right))
     recv = lax.all_to_all(send, "dom", split_axis=0, concat_axis=0, tiled=True)
     devices = lax.axis_size(("dom", "blk"))
     first_block = lax.axis_index(("dom", "blk")) * blocks
     cols = jnp.mod(block_cols - first_block + HB, blocks * devices)
     cap = heat_cap[:, None]
-    window = extended(temp_old.astype(BF16), HB * size)
-    applied, pivot = first_sweep(cols, conduction, window, cap)
-    field, right, low = gather_heat(recv, temp_old, cap, applied, pivot)
-    window = extended(low, HB * size)
-    temp, back = last_sweep(cols, conduction, window, cap, pivot, field, right, recv)
+    applied, pivot = first_sweep(cols, conduction, left, temp_old, right, cap)
+    field, total, low, head, tail = gather_heat(recv, temp_old, cap, applied, pivot, width)
+    left, right = halo(head, tail)
+    temp, back = last_sweep(cols, conduction, left, low, right, cap, pivot, field, total, recv[:, CAP:])
     returned = lax.all_to_all(back, "dom", split_axis=0, concat_axis=0, tiled=True)
     return temp, unpack(slots, returned)
 

time: 206 us -> 185 us (0.90)
  Pallas kernels: 58.6 us -> 39.1 us
  blocking collectives: 76.3 us -> 64.3 us
  local copies, waits for them, and re-layouts: 4.68 us -> 12.5 us
  waiting for transfers between devices: 44.3 us -> 49.8 us
  other arithmetic: 4.79 us -> 1.38 us
    all_to_all x1, blocking collectives: 76.3 us -> 64.3 us  [body(): lax.all_to_all(back, 'dom', split_axis=0, concat_axis=0, tiled=True)]
    unnamed x11 -> x39, local copies, waits for them, and re-layouts: 2.26 us -> 12.1 us
    all_to_all x1, waiting for transfers between devices: 36.4 us -> 44.6 us  [body(): recv = lax.all_to_all(send, 'dom', split_axis=0, concat_axis=0, tiled=True)]
    pallas_call x1, Pallas kernels: 19.5 us -> 12.9 us  [last_sweep(): pl.pallas_call(last_kernel, out_shape=(jax.ShapeDtypeStruct((nodes, sampl...]
    pallas_call x1, Pallas kernels: 7.84 us -> 2.79 us  [first_sweep(): pl.pallas_call(first_kernel, out_shape=(jax.ShapeDtypeStruct((nodes, samp...]
    pallas_call x1, Pallas kernels: 15.6 us -> 10.8 us  [gather_heat(): pl.pallas_call(gather_kernel, out_shape=(jax.ShapeDtypeStruct((nodes, sam...]
    concatenate x2 -> x0, other arithmetic: 4.13 us -> none  [extended(): jnp.concatenate([lax.ppermute(tail, axes, [(i, (i + 1) % count) for i in...]
    ppermute x4, waiting for transfers between devices: 7.91 us -> 5.17 us  [the longest x2 3.63 us: halo(): lax.ppermute(tail, axes, [(i, (i + 1) % count) for i in range(count)])]
  transfers between devices with their start and end apart: 5 -> 5, of which waited for: 3 -> 3; matrix products, arithmetic and copies ran while one was open for 2% -> 0% of each run, Pallas kernels for 4% -> 5%
where the time goes in v2:
time: 185 us; the launch traced here: 184 us
  blocking collectives  64.3 us (35%)
  waiting for transfers between devices  49.8 us (27%)
  Pallas kernels  39.1 us (21%)
  starting transfers between devices  16.4 us (9%)
  local copies, waits for them, and re-layouts  12.5 us (7%)
    all_to_all x1, blocking collectives, body(): lax.all_to_all(back, 'dom', split_axis=0, concat_axis=0, tiled=True)  64.3 us
    all_to_all x1, waiting for transfers between devices, body(): recv = lax.all_to_all(send, 'dom', split_axis=0, concat_axis=0, tiled=True)  44.6 us
    pallas_call x1, Pallas kernels, last_sweep(): pl.pallas_call(last_kernel, out_shape=(jax.ShapeDtypeStruct((nodes, sampl...  12.9 us
    all_to_all x1, starting transfers between devices, body(): recv = lax.all_to_all(send, 'dom', split_axis=0, concat_axis=0, tiled=True)  12.2 us
    unnamed x39, local copies, waits for them, and re-layouts  12.1 us
    pallas_call x1, Pallas kernels, gather_heat(): pl.pallas_call(gather_kernel, out_shape=(jax.ShapeDtypeStruct((nodes, sam...  10.8 us
    pallas_call x1, Pallas kernels, pack(): pl.pallas_call(pack_kernel, out_shape=(jax.ShapeDtypeStruct((peers, CAP +...  7.19 us
    pallas_call x1, Pallas kernels, unpack(): pl.pallas_call(unpack_kernel, out_shape=jax.ShapeDtypeStruct((count, samp...  5.53 us
  transfers between devices with their start and end apart: 5, of which 3 were waited for; matrix products, arithmetic and copies ran while one was open for 0% of the time, Pallas kernels for 5%

profile of v2, /device:TPU:6, one launch (start us, length us, event | category | flops | bytes accessed | tf_op | source)
XLA Modules:
  0.0 184.3 jit_solution(2344628247287860794)
XLA Ops:
  0.7 1.4 convert.4
  2.1 0.1 collective-permute-start
  2.2 2.0 %collective-permute-start.1 = (bf16[768,128]{1,0:T(8,128)(2,1)S(1)}, bf16[768,128]{1,0:T(8,128)(2,1)S(1)}, u32[]{:S(2)}, u32[]{:S(2)}) collective-permute-start(bf16[768,128]{1,0:T(8,128)(2,1)S(1)} %get-tuple-element.30), channel_id=1, source_target_pairs={{1,0},{2,1},{3,2},{4,3},{5,4},{6,5},{7,6},{8,7},{9,8},{10,9},{11,1... | collective-permute-start | bytes 589832 | tf_op jit(solution)/shard_map/ppermute | solution.py:316
  4.2 0.0 copy-done.13
  4.2 7.2 %pack.1 = (bf16[64,136,128]{2,1,0:T(8,128)(2,1)S(1)}, s32[32,128]{1,0:T(8,128)S(1)}) custom-call(s32[32,128]{1,0:T(8,128)S(1)} %bitcast.5, s32[32,128]{1,0:T(8,128)S(1)} %bitcast.6, bf16[32,128]{1,0:T(8,128)(2,1)S(1)} %bitcast.7, bf16[32,128]{1,0:T(8,128)(2,1)S(1)} %bitcast.8, bf16[4096,128]{1,0:T(8,128)(2,1)S(1)} %copy-done.10), custom_call_target="tpu_custom_call" | custom-call | tf_op jit(solution)/shard_map/pack/pallas_call | solution.py:80
  11.4 1.4 copy-done.7
  12.8 0.0 collective-permute-done.left_ref
  12.8 0.0 collective-permute-done.1.right_ref
  12.8 0.7 copy-done.15
  13.5 12.2 %all-to-all-start = ((bf16[64,136,128]{2,1,0:T(8,128)(2,1)}), bf16[64,136,128]{2,1,0:T(8,128)(2,1)S(1)}, u32[]{:S(2)}, u32[]{:S(2)}) async-start(bf16[64,136,128]{2,1,0:T(8,128)(2,1)} %copy-done.7), calls=%async_computation | async-start | bytes 4456448 | tf_op jit(solution)/shard_map/all_to_all | solution.py:336
  25.8 0.1 copy.12
  25.8 0.4 copy.14.cap_ref
  26.2 0.0 copy-start.3
  26.3 1.2 copy-done.3
  27.5 2.2 %copy-done.5 = bf16[32,64,1024]{2,1,0:T(8,128)(2,1)S(1)} copy-done((bf16[32,64,1024]{2,1,0:T(8,128)(2,1)S(1)}, bf16[32,64,1024]{2,1,0:T(8,128)(2,1)}, u32[]{:S(2)}) %copy-start.5) | copy-done | bytes 4194328
  29.7 0.9 copy-done.16
  30.6 2.8 %first_sweep.1 = (f32[2048,128]{1,0:T(8,128)S(1)}, f32[2048,128]{1,0:T(8,128)S(1)}) custom-call(s32[32,16]{1,0:T(8,128)S(1)} %add_select_fusion.cols_ref, bf16[32,64,1024]{2,1,0:T(8,128)(2,1)S(1)} %copy-done.5, bf16[768,128]{1,0:T(8,128)(2,1)S(1)} %collective-permute-done.left_ref, f32[2048,128]{1,0:T(8,128)S(1)} %copy-done.3, ...), custom_call_target="tpu_custom_call" | custom-call | flops 8000000000 | bytes 8000000 | tf_op jit(solution)/shard_map/first_sweep/pallas_call | solution.py:136
  33.4 0.0 copy-start
  33.4 1.0 copy-done
  34.4 1.0 copy-done.8
  35.3 44.6 %all-to-all-done.recv_ref = bf16[64,136,128]{2,1,0:T(8,128)(2,1)S(1)} async-done(((bf16[64,136,128]{2,1,0:T(8,128)(2,1)}), bf16[64,136,128]{2,1,0:T(8,128)(2,1)S(1)}, u32[]{:S(2)}, u32[]{:S(2)}) %all-to-all-start) | async-done | bytes 2228256 | tf_op jit(solution)/shard_map/all_to_all | solution.py:336
  79.9 1.2 copy-done.1
  81.1 1.2 copy-done.4
  82.4 1.2 copy-done.9
  83.6 10.8 %gather_heat.1 = (f32[2048,128]{1,0:T(8,128)S(1)}, f32[2048,128]{1,0:T(8,128)S(1)}, bf16[2048,128]{1,0:T(8,128)(2,1)S(1)}, bf16[768,128]{1,0:T(8,128)(2,1)S(1)}, bf16[768,128]{1,0:T(8,128)(2,1)S(1)}) custom-call(bf16[64,136,128]{2,1,0:T(8,128)(2,1)S(1)} %all-to-all-done.recv_ref, f32[2048,128]{1,0:T(8,128)S(1)} %copy-done.4, f32[2048,1]{1,0:T(8,128)S(1)} %copy.14.cap_ref, ...), custom_call_target="tpu_custom_call" | custom-call | tf_op jit(solution)/shard_map/gather_heat/pallas_call | solution.py:203
  94.4 1.0 collective-permute-start.2
  95.4 1.1 collective-permute-start.3
  96.5 3.6 %collective-permute-done.2.left_ref = bf16[768,128]{1,0:T(8,128)(2,1)S(1)} collective-permute-done((bf16[768,128]{1,0:T(8,128)(2,1)S(1)}, bf16[768,128]{1,0:T(8,128)(2,1)S(1)}, u32[]{:S(2)}, u32[]{:S(2)}) %collective-permute-start.2) | collective-permute-done | bytes 196640 | tf_op jit(solution)/shard_map/ppermute | solution.py:315
  100.1 1.5 collective-permute-done.3.next_ref
  101.7 12.9 %last_sweep.1 = (f32[2048,128]{1,0:T(8,128)}, bf16[64,128,128]{2,1,0:T(8,128)(2,1)S(1)}) custom-call(s32[32,16]{1,0:T(8,128)S(1)} %add_select_fusion.cols_ref, bf16[32,64,1024]{2,1,0:T(8,128)(2,1)S(1)} %copy-done.6, bf16[768,128]{1,0:T(8,128)(2,1)S(1)} %collective-permute-done.2.left_ref, bf16[2048,128]{1,0:T(8,128)(2,1)S(1)} %get-tuple-element.23.low_ref, ...), custom_call_target="tpu_custom_call" | custom-call | tf_op jit(solution)/shard_map/last_sweep/pallas_call | solution.py:266
  114.5 64.3 %all_to_all.10.back_ref = bf16[64,128,128]{2,1,0:T(8,128)(2,1)S(1)} all-to-all(bf16[64,128,128]{2,1,0:T(8,128)(2,1)S(1)} %get-tuple-element.29), channel_id=1, replica_groups=mesh['dom'=64,'blk'=4] {'dom'}, dimensions={0} | all-to-all | bytes 4194304 | tf_op jit(solution)/shard_map/all_to_all | solution.py:345
  178.8 5.5 %unpack.1 = bf16[4096,128]{1,0:T(8,128)(2,1)} custom-call(s32[32,128]{1,0:T(8,128)S(1)} %get-tuple-element.28.slot_ref, bf16[64,128,128]{2,1,0:T(8,128)(2,1)S(1)} %all_to_all.10.back_ref), custom_call_target="tpu_custom_call" | custom-call | tf_op jit(solution)/shard_map/unpack/pallas_call | solution.py:301
  (28 shorter events, 0.1 us)
Async XLA Ops:
  0.6 3.6 %copy-start.11 = (s32[4096,1]{0,1:T(1,128)S(1)}, s32[4096,1]{0,1:T(1,128)}, u32[]{:S(2)}) copy-start(s32[4096,1]{0,1:T(1,128)} %param.12) | copy-start | bytes 49156
  0.6 3.6 %copy-start.12 = (s32[4096]{0:T(1024)S(1)}, s32[4096]{0:T(1024)}, u32[]{:S(2)}) copy-start(s32[4096]{0:T(1024)} %param.13) | copy-start | bytes 49156
  0.7 3.6 %copy-start.13 = (bf16[4096]{0:T(1024)(128)(2,1)S(1)}, bf16[4096]{0:T(1024)(128)(2,1)}, u32[]{:S(2)}) copy-start(bf16[4096]{0:T(1024)(128)(2,1)} %param.10) | copy-start | bytes 24580
  0.7 3.5 %copy-start.14 = (bf16[4096]{0:T(1024)(128)(2,1)S(1)}, bf16[4096]{0:T(1024)(128)(2,1)}, u32[]{:S(2)}) copy-start(bf16[4096]{0:T(1024)(128)(2,1)} %param.11) | copy-start | bytes 24580
  0.7 3.5 %copy-start.10 = (bf16[4096,128]{1,0:T(8,128)(2,1)S(1)}, bf16[4096,128]{1,0:T(8,128)(2,1)}, u32[]{:S(2)}) copy-start(bf16[4096,128]{1,0:T(8,128)(2,1)} %cur_ref.1) | copy-start | bytes 3145732
  2.1 10.7 %collective-permute-start = (bf16[768,128]{1,0:T(8,128)(2,1)S(1)}, bf16[768,128]{1,0:T(8,128)(2,1)S(1)}, u32[]{:S(2)}, u32[]{:S(2)}) collective-permute-start(bf16[768,128]{1,0:T(8,128)(2,1)S(1)} %get-tuple-element.31), channel_id=1, source_target_pairs={{0,1},{1,2},{2,3},{3,4},{4,5},{5,6},{6,7},{7,8},{8,9},{9,10},{10,1... | collective-permute-start | bytes 589832 | tf_op jit(solution)/shard_map/ppermute | solution.py:315
  2.2 10.6 %collective-permute-start.1 = (bf16[768,128]{1,0:T(8,128)(2,1)S(1)}, bf16[768,128]{1,0:T(8,128)(2,1)S(1)}, u32[]{:S(2)}, u32[]{:S(2)}) collective-permute-start(bf16[768,128]{1,0:T(8,128)(2,1)S(1)} %get-tuple-element.30), channel_id=1, source_target_pairs={{1,0},{2,1},{3,2},{4,3},{5,4},{6,5},{7,6},{8,7},{9,8},{10,9},{11,1... | collective-permute-start | bytes 589832 | tf_op jit(solution)/shard_map/ppermute | solution.py:316
  11.4 1.4 copy-start.7
  12.8 0.7 copy-start.15
  13.5 12.3 %copy-start.18 = (s32[32,16]{0,1:T(8,128)S(1)}, s32[32,16]{0,1:T(8,128)}, u32[]{:S(2)}) copy-start(s32[32,16]{0,1:T(8,128)} %param.17) | copy-start | bytes 6148
  13.5 12.3 %copy-start.17 = (f32[2048]{0:T(1024)S(1)}, f32[2048]{0:T(1024)}, u32[]{:S(2)}) copy-start(f32[2048]{0:T(1024)} %param.15) | copy-start | bytes 24580
  13.5 66.4 %all-to-all-start = ((bf16[64,136,128]{2,1,0:T(8,128)(2,1)}), bf16[64,136,128]{2,1,0:T(8,128)(2,1)S(1)}, u32[]{:S(2)}, u32[]{:S(2)}) async-start(bf16[64,136,128]{2,1,0:T(8,128)(2,1)} %copy-done.7), calls=%async_computation | async-start | bytes 4456448 | tf_op jit(solution)/shard_map/all_to_all | solution.py:336
  26.2 1.2 copy-start.3
  27.5 2.2 %copy-start.5 = (bf16[32,64,1024]{2,1,0:T(8,128)(2,1)S(1)}, bf16[32,64,1024]{2,1,0:T(8,128)(2,1)}, u32[]{:S(2)}) copy-start(bf16[32,64,1024]{2,1,0:T(8,128)(2,1)} %cond_ref.3) | copy-start | bytes 12582916
  29.7 0.9 copy-start.16
  33.4 1.0 copy-start
  34.4 1.0 copy-start.8
  79.9 1.2 copy-start.1
  81.1 1.2 copy-start.4
  82.4 1.2 copy-start.9
  83.6 18.1 %copy-start.2 = (f32[2048,128]{1,0:T(8,128)S(1)}, f32[2048,128]{1,0:T(8,128)}, u32[]{:S(2)}) copy-start(f32[2048,128]{1,0:T(8,128)} %copy-done) | copy-start | bytes 3145732
  83.6 18.1 %copy-start.6 = (bf16[32,64,1024]{2,1,0:T(8,128)(2,1)S(1)}, bf16[32,64,1024]{2,1,0:T(8,128)(2,1)}, u32[]{:S(2)}) copy-start(bf16[32,64,1024]{2,1,0:T(8,128)(2,1)} %cond_ref.3) | copy-start | bytes 12582916
  94.4 5.8 %collective-permute-start.2 = (bf16[768,128]{1,0:T(8,128)(2,1)S(1)}, bf16[768,128]{1,0:T(8,128)(2,1)S(1)}, u32[]{:S(2)}, u32[]{:S(2)}) collective-permute-start(bf16[768,128]{1,0:T(8,128)(2,1)S(1)} %get-tuple-element.22), channel_id=1, source_target_pairs={{0,1},{1,2},{2,3},{3,4},{4,5},{5,6},{6,7},{7,8},{8,9},{9,10},{10,1... | collective-permute-start | bytes 589832 | tf_op jit(solution)/shard_map/ppermute | solution.py:315
  95.4 6.3 %collective-permute-start.3 = (bf16[768,128]{1,0:T(8,128)(2,1)S(1)}, bf16[768,128]{1,0:T(8,128)(2,1)S(1)}, u32[]{:S(2)}, u32[]{:S(2)}) collective-permute-start(bf16[768,128]{1,0:T(8,128)(2,1)S(1)} %get-tuple-element.24), channel_id=1, source_target_pairs={{1,0},{2,1},{3,2},{4,3},{5,4},{6,5},{7,6},{8,7},{9,8},{10,9},{11,1... | collective-permute-start | bytes 589832 | tf_op jit(solution)/shard_map/ppermute | solution.py:316

commit v3 on v2

v3 whole, which is shorter than its diff:
```python
import jax
import jax.numpy as jnp
from jax import lax
from jax.experimental import pallas as pl
from jax.experimental.pallas import tpu as pltpu
from jax.sharding import PartitionSpec as P

HB = 12
CAP = 128
META = 8
PARTS = 4
LANES = 128
F32 = jnp.float32
BF16 = jnp.bfloat16
VMEM = pl.BlockSpec(memory_space=pltpu.VMEM)
SMEM = pl.BlockSpec(memory_space=pltpu.SMEM)
HBM = pl.BlockSpec(memory_space=pltpu.HBM)


def params(mib):
    return pltpu.CompilerParams(vmem_limit_bytes=mib * 1024 * 1024)


def dot(a, b):
    return jnp.dot(a, b, preferred_element_type=F32)


def iota(shape, dim):
    return lax.broadcasted_iota(jnp.int32, shape, dim)


def pack_kernel(part_ref, row_ref, res_ref, coef_ref, cur_hbm, send_ref, slot_ref, slot_vmem, cur, wide, spread, ready, sem, out_sems):
    peers = send_ref.shape[0]
    fetch = pltpu.make_async_copy(cur_hbm, cur, sem.at[0])
    fetch.start()
    chunks = part_ref.shape[0]
    before = (iota((LANES, LANES), 0) < iota((LANES, LANES), 1)).astype(BF16)
    counter = jnp.concatenate([before, jnp.ones((LANES, LANES), BF16)], axis=1)
    carry = jnp.zeros((peers, LANES), F32)
    meta = jnp.zeros((4 * peers, LANES), F32)
    part = part_ref[...]
    row = row_ref[...]
    high = lax.shift_right_logical(row, 7).astype(F32)
    low = jnp.bitwise_and(row, 127).astype(F32)
    res = res_ref[...].astype(F32)
    coef = coef_ref[...].astype(F32)
    slots = []
    for r in range(chunks):
        hit = (iota((peers, LANES), 0) == part[r : r + 1]).astype(F32)
        counted = dot(hit.astype(BF16), counter)
        rank = jnp.sum(hit * (counted[:, :LANES] + carry), axis=0, keepdims=True)
        carry = carry + counted[:, LANES:]
        rank = rank.astype(jnp.int32)
        slots.append(part[r : r + 1] * CAP + rank)
        place = (iota((CAP, LANES), 0) == rank).astype(F32).astype(BF16)
        values = jnp.concatenate(
            [hit * res[r : r + 1], hit * coef[r : r + 1], hit * high[r : r + 1], hit * low[r : r + 1]], axis=0
        ).astype(BF16)
        meta = meta + lax.dot_general(values, place, (((1,), (1,)), ((), ())), preferred_element_type=F32)
    slot_vmem[...] = jnp.concatenate(slots, axis=0)
    copy = pltpu.make_async_copy(slot_vmem, slot_ref, sem.at[1])
    copy.start()
    spread[...] = jnp.zeros(spread.shape, F32)
    fetch.wait()
    wide[...] = cur[...].astype(F32)
    copy.wait()

    def scatter(r, carry):
        for lane in range(LANES):
            spread[pl.ds(slot_ref[r, lane], 1), :] = wide[pl.ds(r * LANES + lane, 1), :]
        return carry

    lax.fori_loop(0, chunks, scatter, 0)
    rows = [meta[i * peers : (i + 1) * peers] for i in range(4)]
    group = peers // PARTS
    copies = []
    for g in range(PARTS):
        for p in range(g * group, (g + 1) * group):
            own = jnp.concatenate([m[p : p + 1] for m in rows] + [jnp.zeros((META - 4, LANES), F32)], axis=0)
            ready[p, :CAP] = spread[p * CAP : (p + 1) * CAP].astype(BF16)
            ready[p, CAP:] = own.astype(BF16)
        span = pl.ds(g * group, group)
        copies.append(pltpu.make_async_copy(ready.at[span], send_ref.at[span], out_sems.at[g]))
        copies[g].start()
    for copy in copies:
        copy.wait()


def pack(part, row, res, coef, cur, peers):
    count, samples = cur.shape
    chunks = count // LANES
    return pl.pallas_call(
        pack_kernel,
        out_shape=(
            jax.ShapeDtypeStruct((peers, CAP + META, samples), BF16),
            jax.ShapeDtypeStruct((chunks, LANES), jnp.int32),
        ),
        in_specs=[VMEM] * 4 + [HBM],
        out_specs=(HBM, SMEM),
        scratch_shapes=[
            pltpu.VMEM((chunks, LANES), jnp.int32),
            pltpu.VMEM((count, samples), BF16),
            pltpu.VMEM((count, samples), F32),
            pltpu.VMEM((peers * CAP, samples), F32),
            pltpu.VMEM((peers, CAP + META, samples), BF16),
            pltpu.SemaphoreType.DMA((2,)),
            pltpu.SemaphoreType.DMA((PARTS,)),
        ],
        compiler_params=params(60),
        cost_estimate=pl.CostEstimate(flops=8_000_000_000, bytes_accessed=4_000_000, transcendentals=0),
        name="pack",
    )(part, row, res, coef, cur)


def apply_blocks(cols_ref, cond_ref, window_ref, r):
    size = cond_ref.shape[1]
    picked = []
    for k in range(cols_ref.shape[1]):
        start = pl.multiple_of(cols_ref[r, k] * size, size)
        picked.append(window_ref[pl.ds(start, size), :])
    return dot(cond_ref[r], jnp.concatenate(picked, axis=0))


def fill(window_ref, left_ref, own_ref, right_ref):
    width, nodes = left_ref.shape[0], own_ref.shape[0]
    window_ref[:width] = left_ref[...]
    window_ref[width : width + nodes] = own_ref[...].astype(BF16)
    window_ref[width + nodes :] = right_ref[...]


def first_kernel(cols_ref, cond_ref, left_ref, old_ref, right_ref, cap_ref, base_ref, gain_ref, next_ref, slope_ref, window_ref):
    fill(window_ref, left_ref, old_ref, right_ref)
    blocks, size, _ = cond_ref.shape
    samples = window_ref.shape[1]
    eye = iota((size, size), 0) == iota((size, size), 1)

    def step(r, carry):
        rows = pl.ds(pl.multiple_of(r * size, size), size)
        applied = apply_blocks(cols_ref, cond_ref, window_ref, r)
        corner = cond_ref[r, :, :size].astype(F32)
        diag = jnp.sum(jnp.where(eye, corner, 0.0), axis=1, keepdims=True)
        cap = cap_ref[rows, :]
        gain = jnp.broadcast_to(1.0 / (diag + cap), (size, samples))
        cap = jnp.broadcast_to(cap, (size, samples))
        old = old_ref[rows, :]
        base = old - applied * gain
        share = cap * gain
        base_ref[rows, :] = base
        gain_ref[rows, :] = gain
        next_ref[rows, :] = base * (1.0 - share) + share * old
        slope_ref[rows, :] = gain * (2.0 - share)
        return carry

    lax.fori_loop(0, blocks, step, 0, unroll=8)


def first_sweep(cols, cond, left, old, right, cap):
    nodes, samples = old.shape
    return pl.pallas_call(
        first_kernel,
        out_shape=(jax.ShapeDtypeStruct((nodes, samples), F32),) * 4,
        in_specs=[SMEM] + [VMEM] * 5,
        out_specs=(VMEM,) * 4,
        scratch_shapes=[pltpu.VMEM((nodes + 2 * left.shape[0], samples), BF16)],
        compiler_params=params(48),
        cost_estimate=pl.CostEstimate(flops=8_000_000_000, bytes_accessed=8_000_000, transcendentals=0),
        name="first_sweep",
    )(cols, cond, left, old, right, cap)


MT = 4
STEP = 8


def gather_kernel(recv_hbm, base_hbm, gain_hbm, next_hbm, slope_hbm, next_ref, low_ref, head_ref, tail_ref, recv_ref, node_in, chosen, high, values, recv_sems, sems):
    peers = recv_ref.shape[0]
    group = peers // PARTS
    arrivals = []
    for g in range(PARTS):
        span = pl.ds(g * group, group)
        arrivals.append(pltpu.make_async_copy(recv_hbm.at[span], recv_ref.at[span], recv_sems.at[g]))
        arrivals[g].start()
    nodes, samples = next_ref.shape
    tiles = nodes // LANES
    outer = head_ref.shape[0] // LANES
    sources = (base_hbm, gain_hbm, next_hbm, slope_hbm)
    copies = [pltpu.make_async_copy(ref, node_in.at[i], sems.at[i]) for i, ref in enumerate(sources)]
    for copy in copies:
        copy.start()
    sub = iota((LANES, LANES), 0).astype(F32)

    def split(p, carry):
        rows = pl.ds(pl.multiple_of(p * CAP, CAP), CAP)
        cur = recv_ref[p, :CAP].astype(F32)
        square = cur * cur
        top = square.astype(BF16)
        rest = (square - top.astype(F32)).astype(BF16)
        values[rows, :] = jnp.concatenate([top, rest], axis=1)
        meta = recv_ref[p, CAP:].astype(F32)
        chosen[:, rows] = jnp.where(sub == meta[3:4], meta[0:1], 0.0).astype(BF16)
        high[:, rows] = jnp.broadcast_to(meta[2:3], (16, CAP)).astype(BF16)
        return carry

    for g in range(PARTS):
        arrivals[g].wait()
        lax.fori_loop(g * group, (g + 1) * group, split, 0, unroll=4)
    part = peers * CAP // STEP
    for copy in copies:
        copy.wait()

    def tile(t, carry):
        both = jnp.zeros((MT * LANES, 2 * samples), F32)
        for c in range(STEP):
            cols = slice(c * part, (c + 1) * part)
            own_base = chosen[:, cols]
            own_high = high[:, cols]
            hits = []
            for i in range(MT):
                own = (t * MT + i).astype(F32).astype(BF16)
                hit = (own_high == own).astype(BF16)
                hits.append(own_base * jnp.concatenate([hit] * (LANES // 16), axis=0))
            both = both + dot(jnp.concatenate(hits, axis=0), values[cols, :])
        rows = pl.ds(pl.multiple_of(t * MT * LANES, LANES), MT * LANES)
        heat = both[:, :samples] + both[:, samples:]
        field = node_in[0, rows, :] + heat * node_in[1, rows, :]
        next_ref[rows, :] = node_in[2, rows, :] + heat * node_in[3, rows, :]
        low_ref[rows, :] = field.astype(BF16)
        return carry

    lax.fori_loop(0, tiles // MT, tile, 0)
    head_ref[...] = low_ref[: outer * LANES]
    tail_ref[...] = low_ref[nodes - outer * LANES :]


def gather_heat(recv, base, gain, following, slope, width):
    nodes, samples = base.shape
    slots = recv.shape[0] * CAP
    return pl.pallas_call(
        gather_kernel,
        out_shape=(
            jax.ShapeDtypeStruct((nodes, samples), F32),
            jax.ShapeDtypeStruct((nodes, samples), BF16),
            jax.ShapeDtypeStruct((width, samples), BF16),
            jax.ShapeDtypeStruct((width, samples), BF16),
        ),
        in_specs=[HBM] * 5,
        out_specs=(VMEM,) * 4,
        scratch_shapes=[
            pltpu.VMEM(recv.shape, BF16),
            pltpu.VMEM((4, nodes, samples), F32),
            pltpu.VMEM((LANES, slots), BF16),
            pltpu.VMEM((16, slots), BF16),
            pltpu.VMEM((slots, 2 * samples), BF16),
            pltpu.SemaphoreType.DMA((PARTS,)),
            pltpu.SemaphoreType.DMA((4,)),
        ],
        compiler_params=params(52),
        name="gather_heat",
    )(recv, base, gain, following, slope)


def turn_kernel(meta_ref, turned_ref):
    for g in range(meta_ref.shape[0] // 16):
        stacked = jnp.concatenate([meta_ref[g * 16 + j].astype(F32) for j in range(16)], axis=0)
        turned_ref[g] = stacked.T


def turn(meta):
    groups = meta.shape[0] // 16
    return pl.pallas_call(
        turn_kernel,
        out_shape=jax.ShapeDtypeStruct((groups, CAP, LANES), F32),
        in_specs=[VMEM],
        out_specs=VMEM,
        compiler_params=params(8),
        name="turn",
    )(meta)


def last_kernel(cols_ref, cond_ref, left_ref, low_ref, right_ref, next_ref, gain_ref, turned_ref, temp_hbm, back_ref, window_ref, temp, pair, temp_sem):
    fill(window_ref, left_ref, low_ref, right_ref)
    blocks, size, _ = cond_ref.shape
    nodes, samples = next_ref.shape
    groups = turned_ref.shape[0]
    tiles = nodes // LANES

    def step(r, carry):
        rows = pl.ds(pl.multiple_of(r * size, size), size)
        applied = apply_blocks(cols_ref, cond_ref, window_ref, r)
        field = next_ref[rows, :] - applied * gain_ref[rows, :]
        temp[rows, :] = field
        top = field.astype(BF16)
        rest = (field - top.astype(F32)).astype(BF16)
        pair[rows, :] = jnp.concatenate([top, rest], axis=1)
        return carry

    lax.fori_loop(0, blocks, step, 0, unroll=8)
    temp_copy = pltpu.make_async_copy(temp, temp_hbm, temp_sem)
    temp_copy.start()
    lane = iota((CAP, LANES), 1).astype(F32)

    def send(g, carry):
        for j in range(16):
            own = turned_ref[g, :, j * META : j * META + 4]
            low = jnp.broadcast_to(own[:, 3:4], (CAP, LANES))
            low_hit = jnp.where(low == lane, 1.0, 0.0).astype(BF16)
            high = jnp.broadcast_to(own[:, 2:3], (CAP, LANES))
            hits = [low_hit * jnp.where(high == float(t), 1.0, 0.0).astype(BF16) for t in range(tiles)]
            both = dot(jnp.concatenate(hits, axis=1), pair[...])
            seen = both[:, :samples] + both[:, samples:]
            back_ref[g * 16 + j] = (own[:, 0:1] * (1.0 + own[:, 1:2] * seen)).astype(BF16)
        return carry

    lax.fori_loop(0, groups, send, 0)
    temp_copy.wait()


def last_sweep(cols, cond, left, low, right, following, gain, turned):
    nodes, samples = following.shape
    peers = turned.shape[0] * 16
    return pl.pallas_call(
        last_kernel,
        out_shape=(
            jax.ShapeDtypeStruct((nodes, samples), F32),
            jax.ShapeDtypeStruct((peers, CAP, samples), BF16),
        ),
        in_specs=[SMEM] + [VMEM] * 7,
        out_specs=(HBM, VMEM),
        scratch_shapes=[
            pltpu.VMEM((nodes + 2 * left.shape[0], samples), BF16),
            pltpu.VMEM((nodes, samples), F32),
            pltpu.VMEM((nodes, 2 * samples), BF16),
            pltpu.SemaphoreType.DMA,
        ],
        compiler_params=params(24),
        name="last_sweep",
    )(cols, cond, left, low, right, following, gain, turned)


def unpack_kernel(slot_ref, back_ref, out_hbm, wide, picked, out, sems):
    peers, _, samples = back_ref.shape
    for p in range(peers):
        wide[p * CAP : (p + 1) * CAP] = back_ref[p].astype(F32)
    chunks = slot_ref.shape[0] // PARTS

    def gather(r, carry):
        for lane in range(LANES):
            picked[pl.ds(r * LANES + lane, 1), :] = wide[pl.ds(slot_ref[r, lane], 1), :]
        return carry

    copies = []
    for g in range(PARTS):
        lax.fori_loop(g * chunks, (g + 1) * chunks, gather, 0)
        span = pl.ds(g * chunks * LANES, chunks * LANES)
        out[span, :] = picked[span, :].astype(BF16)
        copies.append(pltpu.make_async_copy(out.at[span], out_hbm.at[span], sems.at[g]))
        copies[g].start()
    for copy in copies:
        copy.wait()


def unpack(slots, back):
    peers, _, samples = back.shape
    count = slots.shape[0] * slots.shape[1]
    return pl.pallas_call(
        unpack_kernel,
        out_shape=jax.ShapeDtypeStruct((count, samples), BF16),
        in_specs=[SMEM, VMEM],
        out_specs=HBM,
        scratch_shapes=[
            pltpu.VMEM((peers * CAP, samples), F32),
            pltpu.VMEM((count, samples), F32),
            pltpu.VMEM((count, samples), BF16),
            pltpu.SemaphoreType.DMA((PARTS,)),
        ],
        compiler_params=params(24),
        name="unpack",
    )(slots, back)


def ends_kernel(old_hbm, head_ref, tail_ref, head, tail, sems):
    width, nodes = head.shape[0], old_hbm.shape[0]
    first = pltpu.make_async_copy(old_hbm.at[pl.ds(0, width)], head, sems.at[0])
    last = pltpu.make_async_copy(old_hbm.at[pl.ds(nodes - width, width)], tail, sems.at[1])
    first.start()
    last.start()
    first.wait()
    head_ref[...] = head[...].astype(BF16)
    last.wait()
    tail_ref[...] = tail[...].astype(BF16)


def ends(old, width):
    samples = old.shape[1]
    return pl.pallas_call(
        ends_kernel,
        out_shape=(jax.ShapeDtypeStruct((width, samples), BF16),) * 2,
        in_specs=[HBM],
        out_specs=(VMEM, VMEM),
        scratch_shapes=[
            pltpu.VMEM((width, samples), F32),
            pltpu.VMEM((width, samples), F32),
            pltpu.SemaphoreType.DMA((2,)),
        ],
        compiler_params=params(62),
        name="ends",
    )(old)


def halo(head, tail):
    axes = ("dom", "blk")
    count = lax.axis_size(axes)
    left = lax.ppermute(tail, axes, [(i, (i + 1) % count) for i in range(count)])
    right = lax.ppermute(head, axes, [((i + 1) % count, i) for i in range(count)])
    return left, right


def body(current, resistivity, temp_coef, dest_part, dest_row, temp_old, heat_cap, conduction, block_cols):
    count, samples = current.shape
    peers = lax.axis_size("dom")
    blocks, size, _ = conduction.shape
    chunks = count // LANES
    width = HB * size
    left, right = halo(*ends(temp_old, width))
    send, slots = pack(
        dest_part.reshape(chunks, LANES),
        dest_row.reshape(chunks, LANES),
        resistivity.reshape(chunks, LANES),
        temp_coef.reshape(chunks, LANES),
        current,
        peers,
    )
    send, _, _ = lax.optimization_barrier((send, left, right))
    recv = lax.all_to_all(send, "dom", split_axis=0, concat_axis=0, tiled=True)
    devices = lax.axis_size(("dom", "blk"))
    first_block = lax.axis_index(("dom", "blk")) * blocks
    cols = jnp.mod(block_cols - first_block + HB, blocks * devices)
    base, gain, following, slope = first_sweep(cols, conduction, left, temp_old, right, heat_cap[:, None])
    following, low, head, tail = gather_heat(recv, base, gain, following, slope, width)
    left, right = halo(head, tail)
    temp, back = last_sweep(cols, conduction, left, low, right, following, gain, turn(recv[:, CAP:]))
    returned = lax.all_to_all(back, "dom", split_axis=0, concat_axis=0, tiled=True)
    return temp, unpack(slots, returned)


def solution(mesh):
    both = ("dom", "blk")
    placed = (
        P(both, None),
        P(both),
        P(both),
        P(both, None),
        P(both),
        P(both, None),
        P(both),
        P(both, None, None),
        P(both, None),
    )
    return jax.shard_map(
        body,
        mesh=mesh,
        in_specs=placed,
        out_specs=(P(both, None), P(both, None)),
        check_vma=False,
    )
```

time: 185 us -> 183 us (0.989)
  Pallas kernels: 39.1 us -> 46.4 us
  local copies, waits for them, and re-layouts: 12.5 us -> 6.33 us
    unnamed x39 -> x21, local copies, waits for them, and re-layouts: 12.1 us -> 4.07 us
    pallas_call x1, Pallas kernels: 7.19 us -> 9.33 us  [pack(): pl.pallas_call(pack_kernel, out_shape=(jax.ShapeDtypeStruct((peers, CAP +...]
    pallas_call x0 -> x2, Pallas kernels: none -> 1.98 us  [the longest x1 1.88 us: ends(): pl.pallas_call(ends_kernel, out_shape=(jax.ShapeDtypeStruct((width, sampl...]
    pallas_call x1, Pallas kernels: 2.79 us -> 4.74 us  [first_sweep(): pl.pallas_call(first_kernel, out_shape=(jax.ShapeDtypeStruct((nodes, samp...]
  transfers between devices with their start and end apart: 5 -> 5, of which waited for: 3 -> 3; matrix products, arithmetic and copies ran while one was open for 0% -> 1% of each run, Pallas kernels for 5% -> 8%
where the time goes in v3:
time: 183 us
  blocking collectives  64.2 us (35%)
  waiting for transfers between devices  48 us (26%)
  Pallas kernels  46.4 us (25%)
  starting transfers between devices  16.7 us (9%)
  local copies, waits for them, and re-layouts  6.33 us (3%)
    all_to_all x1, blocking collectives, body(): lax.all_to_all(back, 'dom', split_axis=0, concat_axis=0, tiled=True)  64.2 us
    all_to_all x1, waiting for transfers between devices, body(): recv = lax.all_to_all(send, 'dom', split_axis=0, concat_axis=0, tiled=True)  43.8 us
    pallas_call x1, Pallas kernels, last_sweep(): pl.pallas_call(last_kernel, out_shape=(jax.ShapeDtypeStruct((nodes, sampl...  12.6 us
    all_to_all x1, starting transfers between devices, body(): recv = lax.all_to_all(send, 'dom', split_axis=0, concat_axis=0, tiled=True)  12.5 us
    pallas_call x1, Pallas kernels, gather_heat(): pl.pallas_call(gather_kernel, out_shape=(jax.ShapeDtypeStruct((nodes, sam...  12.4 us
    pallas_call x1, Pallas kernels, pack(): pl.pallas_call(pack_kernel, out_shape=(jax.ShapeDtypeStruct((peers, CAP +...  9.33 us
    pallas_call x1, Pallas kernels, unpack(): pl.pallas_call(unpack_kernel, out_shape=jax.ShapeDtypeStruct((count, samp...  5.3 us
    pallas_call x1, Pallas kernels, first_sweep(): pl.pallas_call(first_kernel, out_shape=(jax.ShapeDtypeStruct((nodes, samp...  4.74 us
  transfers between devices with their start and end apart: 5, of which 3 were waited for; matrix products, arithmetic and copies ran while one was open for 1% of the time, Pallas kernels for 8%

profile of v3, /device:TPU:6, one launch (start us, length us, event | category | flops | bytes accessed | tf_op | source)
XLA Modules:
  0.0 182.6 jit_solution(9138961929415575816)
XLA Ops:
  0.6 1.9 %ends.1 = (bf16[768,128]{1,0:T(8,128)(2,1)}, bf16[768,128]{1,0:T(8,128)(2,1)}) custom-call(f32[2048,128]{1,0:T(8,128)} %old_ref.1), custom_call_target="tpu_custom_call" | custom-call | tf_op jit(solution)/shard_map/ends/pallas_call | solution.py:395
  2.5 0.1 collective-permute-start
  2.6 2.0 %collective-permute-start.1 = (bf16[768,128]{1,0:T(8,128)(2,1)}, bf16[768,128]{1,0:T(8,128)(2,1)S(1)}, u32[]{:S(2)}, u32[]{:S(2)}) collective-permute-start(bf16[768,128]{1,0:T(8,128)(2,1)} %get-tuple-element.19), channel_id=1, source_target_pairs={{1,0},{2,1},{3,2},{4,3},{5,4},{6,5},{7,6},{8,7},{9,8},{10,9},{11,1... | collective-permute-start | bytes 589832 | tf_op jit(solution)/shard_map/ppermute | solution.py:414
  4.6 9.3 %pack.1 = (bf16[64,136,128]{2,1,0:T(8,128)(2,1)}, s32[32,128]{1,0:T(8,128)}) custom-call(s32[32,128]{1,0:T(8,128)} %bitcast.6, s32[32,128]{1,0:T(8,128)} %bitcast.7, bf16[32,128]{1,0:T(8,128)(2,1)} %bitcast.8, bf16[32,128]{1,0:T(8,128)(2,1)} %bitcast.9, bf16[4096,128]{1,0:T(8,128)(2,1)} %cur_hbm.1), custom_call_target="tpu_custom_call" | custom-call | flops 8000000000 | bytes 4000000 | tf_op jit(solution)/shard_map/pack/pallas_call | solution.py:92
  14.0 0.0 collective-permute-done.left_ref
  14.0 0.0 collective-permute-done.1.right_ref
  14.0 0.0 copy-start.9
  14.0 0.0 copy-start.8
  14.0 0.0 copy-start.6
  14.0 12.5 %all-to-all-start = ((bf16[64,136,128]{2,1,0:T(8,128)(2,1)}), bf16[64,136,128]{2,1,0:T(8,128)(2,1)}, u32[]{:S(2)}, u32[]{:S(2)}) async-start(bf16[64,136,128]{2,1,0:T(8,128)(2,1)} %get-tuple-element.20), calls=%async_computation | async-start | bytes 4456448 | tf_op jit(solution)/shard_map/all_to_all | solution.py:434
  26.5 0.1 copy.12
  26.6 0.0 copy-done.8
  26.6 1.3 copy.13.cap_ref
  28.0 4.7 %first_sweep.1 = (f32[2048,128]{1,0:T(8,128)S(1)}, f32[2048,128]{1,0:T(8,128)S(1)}, f32[2048,128]{1,0:T(8,128)S(1)}, f32[2048,128]{1,0:T(8,128)S(1)}) custom-call(s32[32,16]{1,0:T(8,128)S(1)} %add_select_fusion.cols_ref, bf16[32,64,1024]{2,1,0:T(8,128)(2,1)} %cond_ref.3, bf16[768,128]{1,0:T(8,128)(2,1)S(1)} %collective-permute-done.left_ref, ...), custom_call_target="tpu_custom_call" | custom-call | flops 8000000000 | bytes 8000000 | tf_op jit(solution)/shard_map/first_sweep/pallas_call | solution.py:159
  32.7 0.0 copy-start
  32.7 1.0 copy-done
  33.7 1.0 copy-done.3
  34.7 1.0 copy-done.4
  35.7 1.0 copy-done.5
  36.7 43.8 %all-to-all-done.recv_hbm = bf16[64,136,128]{2,1,0:T(8,128)(2,1)} async-done(((bf16[64,136,128]{2,1,0:T(8,128)(2,1)}), bf16[64,136,128]{2,1,0:T(8,128)(2,1)}, u32[]{:S(2)}, u32[]{:S(2)}) %all-to-all-start) | async-done | bytes 2228256 | tf_op jit(solution)/shard_map/all_to_all | solution.py:434
  80.6 12.4 %gather_heat.1 = (f32[2048,128]{1,0:T(8,128)S(1)}, bf16[2048,128]{1,0:T(8,128)(2,1)S(1)}, bf16[768,128]{1,0:T(8,128)(2,1)S(1)}, bf16[768,128]{1,0:T(8,128)(2,1)S(1)}) custom-call(bf16[64,136,128]{2,1,0:T(8,128)(2,1)} %all-to-all-done.recv_hbm, f32[2048,128]{1,0:T(8,128)} %copy-done.3, f32[2048,128]{1,0:T(8,128)} %copy-done, f32[2048,128]{1,0:T(8,128)} %copy-done.4, ...), custom_call_target="tpu_custom_call" | custom-call | tf_op jit(solution)/shard_map/gather_heat/pallas_call | solution.py:238
  93.0 1.0 collective-permute-start.2
  94.0 1.1 collective-permute-start.3
  95.1 0.9 slice.4.meta_ref
  96.0 0.1 turn.1.turned_ref
  96.1 2.6 %collective-permute-done.2.left_ref = bf16[768,128]{1,0:T(8,128)(2,1)S(1)} collective-permute-done((bf16[768,128]{1,0:T(8,128)(2,1)S(1)}, bf16[768,128]{1,0:T(8,128)(2,1)S(1)}, u32[]{:S(2)}, u32[]{:S(2)}) %collective-permute-start.2) | collective-permute-done | bytes 196640 | tf_op jit(solution)/shard_map/ppermute | solution.py:413
  98.7 1.5 collective-permute-done.3.right_ref
  100.3 0.0 copy-done.1
  100.3 12.6 %last_sweep.1 = (f32[2048,128]{1,0:T(8,128)}, bf16[64,128,128]{2,1,0:T(8,128)(2,1)S(1)}) custom-call(s32[32,16]{1,0:T(8,128)S(1)} %add_select_fusion.cols_ref, bf16[32,64,1024]{2,1,0:T(8,128)(2,1)S(1)} %copy-done.2, bf16[768,128]{1,0:T(8,128)(2,1)S(1)} %collective-permute-done.2.left_ref, bf16[2048,128]{1,0:T(8,128)(2,1)S(1)} %get-tuple-element.26.low_ref, ...), custom_call_target="tpu_custom_call" | custom-call | tf_op jit(solution)/shard_map/last_sweep/pallas_call | solution.py:321
  112.9 64.2 %all_to_all.10.back_ref = bf16[64,128,128]{2,1,0:T(8,128)(2,1)S(1)} all-to-all(bf16[64,128,128]{2,1,0:T(8,128)(2,1)S(1)} %get-tuple-element.31), channel_id=1, replica_groups=mesh['dom'=64,'blk'=4] {'dom'}, dimensions={0} | all-to-all | bytes 4194304 | tf_op jit(solution)/shard_map/all_to_all | solution.py:442
  177.2 0.0 copy-done.7
  177.2 5.3 %unpack.1 = bf16[4096,128]{1,0:T(8,128)(2,1)} custom-call(s32[32,128]{1,0:T(8,128)S(1)} %copy-done.7, bf16[64,128,128]{2,1,0:T(8,128)(2,1)S(1)} %all_to_all.10.back_ref), custom_call_target="tpu_custom_call" | custom-call | tf_op jit(solution)/shard_map/unpack/pallas_call | solution.py:365
  (10 shorter events, 0.0 us)
Async XLA Ops:
  2.5 11.5 %collective-permute-start = (bf16[768,128]{1,0:T(8,128)(2,1)}, bf16[768,128]{1,0:T(8,128)(2,1)S(1)}, u32[]{:S(2)}, u32[]{:S(2)}) collective-permute-start(bf16[768,128]{1,0:T(8,128)(2,1)} %get-tuple-element.18), channel_id=1, source_target_pairs={{0,1},{1,2},{2,3},{3,4},{4,5},{5,6},{6,7},{7,8},{8,9},{9,10},{10,1... | collective-permute-start | bytes 589832 | tf_op jit(solution)/shard_map/ppermute | solution.py:413
  2.6 11.4 %collective-permute-start.1 = (bf16[768,128]{1,0:T(8,128)(2,1)}, bf16[768,128]{1,0:T(8,128)(2,1)S(1)}, u32[]{:S(2)}, u32[]{:S(2)}) collective-permute-start(bf16[768,128]{1,0:T(8,128)(2,1)} %get-tuple-element.19), channel_id=1, source_target_pairs={{1,0},{2,1},{3,2},{4,3},{5,4},{6,5},{7,6},{8,7},{9,8},{10,9},{11,1... | collective-permute-start | bytes 589832 | tf_op jit(solution)/shard_map/ppermute | solution.py:414
  14.0 12.5 %copy-start.9 = (s32[32,16]{0,1:T(8,128)S(1)}, s32[32,16]{0,1:T(8,128)}, u32[]{:S(2)}) copy-start(s32[32,16]{0,1:T(8,128)} %param.17) | copy-start | bytes 6148
  14.0 12.6 %copy-start.8 = (f32[2048]{0:T(1024)S(1)}, f32[2048]{0:T(1024)}, u32[]{:S(2)}) copy-start(f32[2048]{0:T(1024)} %param.15) | copy-start | bytes 24580
  14.0 14.0 %copy-start.6 = (f32[2048,128]{1,0:T(8,128)S(1)}, f32[2048,128]{1,0:T(8,128)}, u32[]{:S(2)}) copy-start(f32[2048,128]{1,0:T(8,128)} %old_ref.1) | copy-start | bytes 3145732
  14.0 66.5 %all-to-all-start = ((bf16[64,136,128]{2,1,0:T(8,128)(2,1)}), bf16[64,136,128]{2,1,0:T(8,128)(2,1)}, u32[]{:S(2)}, u32[]{:S(2)}) async-start(bf16[64,136,128]{2,1,0:T(8,128)(2,1)} %get-tuple-element.20), calls=%async_computation | async-start | bytes 4456448 | tf_op jit(solution)/shard_map/all_to_all | solution.py:434
  32.7 1.0 copy-start
  33.7 1.0 copy-start.3
  34.7 1.0 copy-start.4
  35.7 1.0 copy-start.5
  80.5 19.7 %copy-start.1 = (f32[2048,128]{1,0:T(8,128)S(1)}, f32[2048,128]{1,0:T(8,128)}, u32[]{:S(2)}) copy-start(f32[2048,128]{1,0:T(8,128)} %copy-done) | copy-start | bytes 3145732
  80.5 19.7 %copy-start.2 = (bf16[32,64,1024]{2,1,0:T(8,128)(2,1)S(1)}, bf16[32,64,1024]{2,1,0:T(8,128)(2,1)}, u32[]{:S(2)}) copy-start(bf16[32,64,1024]{2,1,0:T(8,128)(2,1)} %cond_ref.3) | copy-start | bytes 12582916
  93.0 5.8 %collective-permute-start.2 = (bf16[768,128]{1,0:T(8,128)(2,1)S(1)}, bf16[768,128]{1,0:T(8,128)(2,1)S(1)}, u32[]{:S(2)}, u32[]{:S(2)}) collective-permute-start(bf16[768,128]{1,0:T(8,128)(2,1)S(1)} %get-tuple-element.25), channel_id=1, source_target_pairs={{0,1},{1,2},{2,3},{3,4},{4,5},{5,6},{6,7},{7,8},{8,9},{9,10},{10,1... | collective-permute-start | bytes 589832 | tf_op jit(solution)/shard_map/ppermute | solution.py:413
  94.0 6.3 %collective-permute-start.3 = (bf16[768,128]{1,0:T(8,128)(2,1)S(1)}, bf16[768,128]{1,0:T(8,128)(2,1)S(1)}, u32[]{:S(2)}, u32[]{:S(2)}) collective-permute-start(bf16[768,128]{1,0:T(8,128)(2,1)S(1)} %get-tuple-element.27), channel_id=1, source_target_pairs={{1,0},{2,1},{3,2},{4,3},{5,4},{6,5},{7,6},{8,7},{9,8},{10,9},{11,1... | collective-permute-start | bytes 589832 | tf_op jit(solution)/shard_map/ppermute | solution.py:414
  112.9 64.3 %copy-start.7 = (s32[32,128]{1,0:T(8,128)S(1)}, s32[32,128]{1,0:T(8,128)}, u32[]{:S(2)}) copy-start(s32[32,128]{1,0:T(8,128)} %get-tuple-element.30.slot_ref) | copy-start | bytes 49156

commit v4 on v3

--- a/solution.py
+++ b/solution.py
@@ -1,3 +1,5 @@
+import functools
+
 import jax
 import jax.numpy as jnp
 from jax import lax
@@ -121,11 +123,11 @@
     return dot(cond_ref[r], jnp.concatenate(picked, axis=0))
 
 
-def fill(window_ref, left_ref, own_ref, right_ref):
-    width, nodes = left_ref.shape[0], own_ref.shape[0]
-    window_ref[:width] = left_ref[...]
-    window_ref[width : width + nodes] = own_ref[...].astype(BF16)
-    window_ref[width + nodes :] = right_ref[...]
+def fill(window_ref, *parts):
+    start = 0
+    for ref in parts:
+        window_ref[start : start + ref.shape[0]] = ref[...].astype(BF16)
+        start += ref.shape[0]
 
 
 def first_kernel(cols_ref, cond_ref, left_ref, old_ref, right_ref, cap_ref, base_ref, gain_ref, next_ref, slope_ref, window_ref):
@@ -168,23 +170,28 @@
     )(cols, cond, left, old, right, cap)
 
 
-MT = 4
 STEP = 8
 
 
-def gather_kernel(recv_hbm, base_hbm, gain_hbm, next_hbm, slope_hbm, next_ref, low_ref, head_ref, tail_ref, recv_ref, node_in, chosen, high, values, recv_sems, sems):
+def gather_kernel(spans, recv_hbm, base_hbm, gain_hbm, next_hbm, slope_hbm, *rest):
+    count = len(spans)
+    next_refs, low_refs = rest[:count], rest[count : 2 * count]
+    recv_ref, node_in, chosen, high, values, recv_sems, sems = rest[2 * count :]
     peers = recv_ref.shape[0]
     group = peers // PARTS
+    samples = node_in.shape[2]
     arrivals = []
     for g in range(PARTS):
         span = pl.ds(g * group, group)
         arrivals.append(pltpu.make_async_copy(recv_hbm.at[span], recv_ref.at[span], recv_sems.at[g]))
         arrivals[g].start()
-    nodes, samples = next_ref.shape
-    tiles = nodes // LANES
-    outer = head_ref.shape[0] // LANES
-    sources = (base_hbm, gain_hbm, next_hbm, slope_hbm)
-    copies = [pltpu.make_async_copy(ref, node_in.at[i], sems.at[i]) for i, ref in enumerate(sources)]
+    copies, offsets, offset = [], [], 0
+    for k, (first, size) in enumerate(spans):
+        for i, ref in enumerate((base_hbm, gain_hbm, next_hbm, slope_hbm)):
+            target = node_in.at[i, pl.ds(offset, size)]
+            copies.append(pltpu.make_async_copy(ref.at[pl.ds(first, size)], target, sems.at[4 * k + i]))
+        offsets.append(offset)
+        offset += size
     for copy in copies:
         copy.start()
     sub = iota((LANES, LANES), 0).astype(F32)
@@ -207,54 +214,54 @@
     part = peers * CAP // STEP
     for copy in copies:
         copy.wait()
-
-    def tile(t, carry):
-        both = jnp.zeros((MT * LANES, 2 * samples), F32)
-        for c in range(STEP):
-            cols = slice(c * part, (c + 1) * part)
-            own_base = chosen[:, cols]
-            own_high = high[:, cols]
-            hits = []
-            for i in range(MT):
-                own = (t * MT + i).astype(F32).astype(BF16)
-                hit = (own_high == own).astype(BF16)
-                hits.append(own_base * jnp.concatenate([hit] * (LANES // 16), axis=0))
-            both = both + dot(jnp.concatenate(hits, axis=0), values[cols, :])
-        rows = pl.ds(pl.multiple_of(t * MT * LANES, LANES), MT * LANES)
-        heat = both[:, :samples] + both[:, samples:]
-        field = node_in[0, rows, :] + heat * node_in[1, rows, :]
-        next_ref[rows, :] = node_in[2, rows, :] + heat * node_in[3, rows, :]
-        low_ref[rows, :] = field.astype(BF16)
-        return carry
-
-    lax.fori_loop(0, tiles // MT, tile, 0)
-    head_ref[...] = low_ref[: outer * LANES]
-    tail_ref[...] = low_ref[nodes - outer * LANES :]
-
-
-def gather_heat(recv, base, gain, following, slope, width):
-    nodes, samples = base.shape
+    for k, (first, size) in enumerate(spans):
+        mt = next(m for m in (6, 4, 3, 2, 1) if size // LANES % m == 0)
+
+        def tile(t, carry):
+            both = jnp.zeros((mt * LANES, 2 * samples), F32)
+            for c in range(STEP):
+                cols = slice(c * part, (c + 1) * part)
+                own_base = chosen[:, cols]
+                own_high = high[:, cols]
+                hits = []
+                for i in range(mt):
+                    own = (first // LANES + t * mt + i).astype(F32).astype(BF16)
+                    hit = (own_high == own).astype(BF16)
+                    hits.append(own_base * jnp.concatenate([hit] * (LANES // 16), axis=0))
+                both = both + dot(jnp.concatenate(hits, axis=0), values[cols, :])
+            start = pl.multiple_of(t * mt * LANES, LANES)
+            rows = pl.ds(start, mt * LANES)
+            here = pl.ds(offsets[k] + start, mt * LANES)
+            heat = both[:, :samples] + both[:, samples:]
+            field = node_in[0, here, :] + heat * node_in[1, here, :]
+            next_refs[k][rows, :] = node_in[2, here, :] + heat * node_in[3, here, :]
+            low_refs[k][rows, :] = field.astype(BF16)
+            return carry
+
+        lax.fori_loop(0, size // LANES // mt, tile, 0)
+
+
+def gather_heat(recv, base, gain, following, slope, spans):
+    samples = base.shape[1]
     slots = recv.shape[0] * CAP
-    return pl.pallas_call(
-        gather_kernel,
-        out_shape=(
-            jax.ShapeDtypeStruct((nodes, samples), F32),
-            jax.ShapeDtypeStruct((nodes, samples), BF16),
-            jax.ShapeDtypeStruct((width, samples), BF16),
-            jax.ShapeDtypeStruct((width, samples), BF16),
-        ),
+    count = sum(size for _, size in spans)
+    shapes = [jax.ShapeDtypeStruct((size, samples), kind) for kind in (F32, BF16) for _, size in spans]
+    return pl.pallas_call(
+        functools.partial(gather_kernel, spans),
+        out_shape=tuple(shapes),
         in_specs=[HBM] * 5,
-        out_specs=(VMEM,) * 4,
+        out_specs=(VMEM,) * len(shapes),
         scratch_shapes=[
             pltpu.VMEM(recv.shape, BF16),
-            pltpu.VMEM((4, nodes, samples), F32),
+            pltpu.VMEM((4, count, samples), F32),
             pltpu.VMEM((LANES, slots), BF16),
             pltpu.VMEM((16, slots), BF16),
             pltpu.VMEM((slots, 2 * samples), BF16),
             pltpu.SemaphoreType.DMA((PARTS,)),
-            pltpu.SemaphoreType.DMA((4,)),
+            pltpu.SemaphoreType.DMA((4 * len(spans),)),
         ],
         compiler_params=params(52),
+        cost_estimate=pl.CostEstimate(flops=4 * slots * count * samples, bytes_accessed=8_000_000, transcendentals=0),
         name="gather_heat",
     )(recv, base, gain, following, slope)
 
@@ -277,24 +284,29 @@
     )(meta)
 
 
-def last_kernel(cols_ref, cond_ref, left_ref, low_ref, right_ref, next_ref, gain_ref, turned_ref, temp_hbm, back_ref, window_ref, temp, pair, temp_sem):
-    fill(window_ref, left_ref, low_ref, right_ref)
+def last_kernel(cols_ref, cond_ref, left_ref, head_ref, mid_ref, tail_ref, right_ref, next_head, next_mid, next_tail, gain_ref, turned_ref, temp_hbm, back_ref, window_ref, temp, pair, temp_sem):
+    fill(window_ref, left_ref, head_ref, mid_ref, tail_ref, right_ref)
     blocks, size, _ = cond_ref.shape
-    nodes, samples = next_ref.shape
+    nodes, samples = gain_ref.shape
     groups = turned_ref.shape[0]
     tiles = nodes // LANES
 
-    def step(r, carry):
-        rows = pl.ds(pl.multiple_of(r * size, size), size)
-        applied = apply_blocks(cols_ref, cond_ref, window_ref, r)
-        field = next_ref[rows, :] - applied * gain_ref[rows, :]
-        temp[rows, :] = field
-        top = field.astype(BF16)
-        rest = (field - top.astype(F32)).astype(BF16)
-        pair[rows, :] = jnp.concatenate([top, rest], axis=1)
-        return carry
-
-    lax.fori_loop(0, blocks, step, 0, unroll=8)
+    first = 0
+    for ref in (next_head, next_mid, next_tail):
+
+        def step(i, carry):
+            r = first + i
+            rows = pl.ds(pl.multiple_of(r * size, size), size)
+            applied = apply_blocks(cols_ref, cond_ref, window_ref, r)
+            field = ref[pl.ds(pl.multiple_of(i * size, size), size), :] - applied * gain_ref[rows, :]
+            temp[rows, :] = field
+            top = field.astype(BF16)
+            rest = (field - top.astype(F32)).astype(BF16)
+            pair[rows, :] = jnp.concatenate([top, rest], axis=1)
+            return carry
+
+        lax.fori_loop(0, ref.shape[0] // size, step, 0, unroll=8 if ref is next_mid else 12)
+        first += ref.shape[0] // size
     temp_copy = pltpu.make_async_copy(temp, temp_hbm, temp_sem)
     temp_copy.start()
     lane = iota((CAP, LANES), 1).astype(F32)
@@ -315,8 +327,8 @@
     temp_copy.wait()
 
 
-def last_sweep(cols, cond, left, low, right, following, gain, turned):
-    nodes, samples = following.shape
+def last_sweep(cols, cond, window, following, gain, turned):
+    nodes, samples = gain.shape
     peers = turned.shape[0] * 16
     return pl.pallas_call(
         last_kernel,
@@ -324,17 +336,17 @@
             jax.ShapeDtypeStruct((nodes, samples), F32),
             jax.ShapeDtypeStruct((peers, CAP, samples), BF16),
         ),
-        in_specs=[SMEM] + [VMEM] * 7,
+        in_specs=[SMEM] + [VMEM] * 11,
         out_specs=(HBM, VMEM),
         scratch_shapes=[
-            pltpu.VMEM((nodes + 2 * left.shape[0], samples), BF16),
+            pltpu.VMEM((sum(part.shape[0] for part in window), samples), BF16),
             pltpu.VMEM((nodes, samples), F32),
             pltpu.VMEM((nodes, 2 * samples), BF16),
             pltpu.SemaphoreType.DMA,
         ],
         compiler_params=params(24),
         name="last_sweep",
-    )(cols, cond, left, low, right, following, gain, turned)
+    )(cols, cond, *window, *following, gain, turned)
 
 
 def unpack_kernel(slot_ref, back_ref, out_hbm, wide, picked, out, sems):
@@ -378,35 +390,6 @@
     )(slots, back)
 
 
-def ends_kernel(old_hbm, head_ref, tail_ref, head, tail, sems):
-    width, nodes = head.shape[0], old_hbm.shape[0]
-    first = pltpu.make_async_copy(old_hbm.at[pl.ds(0, width)], head, sems.at[0])
-    last = pltpu.make_async_copy(old_hbm.at[pl.ds(nodes - width, width)], tail, sems.at[1])
-    first.start()
-    last.start()
-    first.wait()
-    head_ref[...] = head[...].astype(BF16)
-    last.wait()
-    tail_ref[...] = tail[...].astype(BF16)
-
-
-def ends(old, width):
-    samples = old.shape[1]
-    return pl.pallas_call(
-        ends_kernel,
-        out_shape=(jax.ShapeDtypeStruct((width, samples), BF16),) * 2,
-        in_specs=[HBM],
-        out_specs=(VMEM, VMEM),
-        scratch_shapes=[
-            pltpu.VMEM((width, samples), F32),
-            pltpu.VMEM((width, samples), F32),
-            pltpu.SemaphoreType.DMA((2,)),
-        ],
-        compiler_params=params(62),
-        name="ends",
-    )(old)
-
-
 def halo(head, tail):
     axes = ("dom", "blk")
     count = lax.axis_size(axes)
@@ -421,7 +404,7 @@
     blocks, size, _ = conduction.shape
     chunks = count // LANES
     width = HB * size
-    left, right = halo(*ends(temp_old, width))
+    left, right = halo(temp_old[:width], temp_old[-width:])
     send, slots = pack(
         dest_part.reshape(chunks, LANES),
         dest_row.reshape(chunks, LANES),
@@ -436,9 +419,14 @@
     first_block = lax.axis_index(("dom", "blk")) * blocks
     cols = jnp.mod(block_cols - first_block + HB, blocks * devices)
     base, gain, following, slope = first_sweep(cols, conduction, left, temp_old, right, heat_cap[:, None])
-    following, low, head, tail = gather_heat(recv, base, gain, following, slope, width)
+    nodes = temp_old.shape[0]
+    outer = ((0, width), (nodes - width, width))
+    inner = ((width, nodes - 2 * width),)
+    next_head, next_tail, head, tail = gather_heat(recv, base, gain, following, slope, outer)
     left, right = halo(head, tail)
-    temp, back = last_sweep(cols, conduction, left, low, right, following, gain, turn(recv[:, CAP:]))
+    next_mid, mid = gather_heat(recv, base, gain, following, slope, inner)
+    window = (left, head, mid, tail, right)
+    temp, back = last_sweep(cols, conduction, window, (next_head, next_mid, next_tail), gain, turn(recv[:, CAP:]))
     returned = lax.all_to_all(back, "dom", split_axis=0, concat_axis=0, tiled=True)
     return temp, unpack(slots, returned)
 

time: 183 us -> 179 us (0.978)
  waiting for transfers between devices: 48 us -> 43.9 us
  blocking collectives: 64.2 us -> 61.9 us
    ppermute x2, waiting for transfers between devices: 2.62 us -> 0.01 us  [halo(): lax.ppermute(tail, axes, [(i, (i + 1) % count) for i in range(count)])]
    all_to_all x1, blocking collectives: 64.2 us -> 61.9 us  [body(): lax.all_to_all(back, 'dom', split_axis=0, concat_axis=0, tiled=True)]
    unnamed x21 -> x23, local copies, waits for them, and re-layouts: 4.07 us -> 4.06 us
  transfers between devices with their start and end apart: 5 -> 5, of which waited for: 3 -> 1; matrix products, arithmetic and copies ran while one was open for 1% -> 1% of each run, Pallas kernels for 8% -> 11%
where the time goes in v4:
time: 179 us
  blocking collectives  61.9 us (35%)
  Pallas kernels  46.5 us (26%)
  waiting for transfers between devices  43.9 us (25%)
  starting transfers between devices  18.1 us (10%)
  local copies, waits for them, and re-layouts  7.49 us (4%)
    all_to_all x1, blocking collectives, body(): lax.all_to_all(back, 'dom', split_axis=0, concat_axis=0, tiled=True)  61.9 us
    all_to_all x1, waiting for transfers between devices, body(): recv = lax.all_to_all(send, 'dom', split_axis=0, concat_axis=0, tiled=True)  43.9 us
    pallas_call x2, Pallas kernels, gather_heat(): pl.pallas_call(functools.partial(gather_kernel, spans), out_shape=tuple(s...  14.8 us
    all_to_all x1, starting transfers between devices, body(): recv = lax.all_to_all(send, 'dom', split_axis=0, concat_axis=0, tiled=True)  13.9 us
    pallas_call x1, Pallas kernels, last_sweep(): pl.pallas_call(last_kernel, out_shape=(jax.ShapeDtypeStruct((nodes, sampl...  12.2 us
    pallas_call x1, Pallas kernels, pack(): pl.pallas_call(pack_kernel, out_shape=(jax.ShapeDtypeStruct((peers, CAP +...  9.35 us
    pallas_call x1, Pallas kernels, unpack(): pl.pallas_call(unpack_kernel, out_shape=jax.ShapeDtypeStruct((count, samp...  5.3 us
    pallas_call x1, Pallas kernels, first_sweep(): pl.pallas_call(first_kernel, out_shape=(jax.ShapeDtypeStruct((nodes, samp...  4.75 us
  transfers between devices with their start and end apart: 5, of which 1 were waited for; matrix products, arithmetic and copies ran while one was open for 1% of the time, Pallas kernels for 11%

profile of v4, /device:TPU:6, one launch (start us, length us, event | category | flops | bytes accessed | tf_op | source)
XLA Modules:
  0.0 178.9 jit_solution(4192325465849846357)
XLA Ops:
  0.6 1.2 fusion.1
  1.8 0.1 collective-permute-start
  1.9 2.0 %collective-permute-start.1 = (f32[768,128]{1,0:T(8,128)S(1)}, f32[768,128]{1,0:T(8,128)S(1)}, u32[]{:S(2)}, u32[]{:S(2)}) collective-permute-start(f32[768,128]{1,0:T(8,128)S(1)} %get-tuple-element.32), channel_id=1, source_target_pairs={{1,0},{2,1},{3,2},{4,3},{5,4},{6,5},{7,6},{8,7},{9,8},{10,9},{11,1... | collective-permute-start | bytes 1179656 | tf_op jit(solution)/shard_map/ppermute | solution.py:397
  3.9 9.4 %pack.1 = (bf16[64,136,128]{2,1,0:T(8,128)(2,1)}, s32[32,128]{1,0:T(8,128)}) custom-call(s32[32,128]{1,0:T(8,128)} %bitcast.6, s32[32,128]{1,0:T(8,128)} %bitcast.7, bf16[32,128]{1,0:T(8,128)(2,1)} %bitcast.8, bf16[32,128]{1,0:T(8,128)(2,1)} %bitcast.9, bf16[4096,128]{1,0:T(8,128)(2,1)} %cur_hbm.1), custom_call_target="tpu_custom_call" | custom-call | flops 8000000000 | bytes 4000000 | tf_op jit(solution)/shard_map/pack/pallas_call | solution.py:94
  13.3 0.0 collective-permute-done.left_ref
  13.3 0.0 collective-permute-done.1.right_ref
  13.3 0.0 copy-start.10
  13.3 0.0 copy-start.9
  13.3 0.0 copy-start.3
  13.3 13.9 %all-to-all-start = ((bf16[64,136,128]{2,1,0:T(8,128)(2,1)}), bf16[64,136,128]{2,1,0:T(8,128)(2,1)}, u32[]{:S(2)}, u32[]{:S(2)}) async-start(bf16[64,136,128]{2,1,0:T(8,128)(2,1)} %get-tuple-element.18), calls=%async_computation | async-start | bytes 4456448 | tf_op jit(solution)/shard_map/all_to_all | solution.py:417
  27.2 0.1 copy.12
  27.3 1.3 copy.13.cap_ref
  28.7 4.7 %first_sweep.1 = (f32[2048,128]{1,0:T(8,128)S(1)}, f32[2048,128]{1,0:T(8,128)S(1)}, f32[2048,128]{1,0:T(8,128)S(1)}, f32[2048,128]{1,0:T(8,128)S(1)}) custom-call(s32[32,16]{1,0:T(8,128)S(1)} %add_select_fusion.cols_ref, bf16[32,64,1024]{2,1,0:T(8,128)(2,1)} %cond_ref.3, f32[768,128]{1,0:T(8,128)S(1)} %collective-permute-done.left_ref, ...), custom_call_target="tpu_custom_call" | custom-call | flops 8000000000 | bytes 8000000 | tf_op jit(solution)/shard_map/first_sweep/pallas_call | solution.py:161
  33.5 0.0 copy-start.1
  33.5 1.0 copy-done.1
  34.4 1.0 copy-done.5
  35.4 1.0 copy-done.7
  36.4 1.0 copy-done.8
  37.4 43.9 %all-to-all-done.recv_hbm = bf16[64,136,128]{2,1,0:T(8,128)(2,1)} async-done(((bf16[64,136,128]{2,1,0:T(8,128)(2,1)}), bf16[64,136,128]{2,1,0:T(8,128)(2,1)}, u32[]{:S(2)}, u32[]{:S(2)}) %all-to-all-start) | async-done | bytes 2228256 | tf_op jit(solution)/shard_map/all_to_all | solution.py:417
  81.3 9.8 %gather_heat.2 = (f32[768,128]{1,0:T(8,128)S(1)}, f32[768,128]{1,0:T(8,128)S(1)}, bf16[768,128]{1,0:T(8,128)(2,1)S(1)}, bf16[768,128]{1,0:T(8,128)(2,1)S(1)}) custom-call(bf16[64,136,128]{2,1,0:T(8,128)(2,1)} %all-to-all-done.recv_hbm, f32[2048,128]{1,0:T(8,128)} %copy-done.5, f32[2048,128]{1,0:T(8,128)} %copy-done.1, f32[2048,128]{1,0:T(8,128)} %copy-done.7, ...), custom_call_target="tpu_custom_call" | custom-call | flops 6442450944 | bytes 8000000 | tf_op jit(solution)/shard_map/gather_heat/pallas_call | solution.py:249
  91.1 0.1 collective-permute-start.2
  91.2 2.0 %collective-permute-start.3 = (bf16[768,128]{1,0:T(8,128)(2,1)S(1)}, bf16[768,128]{1,0:T(8,128)(2,1)S(1)}, u32[]{:S(2)}, u32[]{:S(2)}) collective-permute-start(bf16[768,128]{1,0:T(8,128)(2,1)S(1)} %get-tuple-element.24.head_ref), channel_id=1, source_target_pairs={{1,0},{2,1},{3,2},{4,3},{5,4},{6,5},{7,6},{8,7},{9,8},{10,9},{11,1... | collective-permute-start | bytes 589832 | tf_op jit(solution)/shard_map/ppermute | solution.py:397
  93.2 0.9 slice.12.meta_ref
  94.1 0.1 turn.1.turned_ref
  94.2 0.0 copy-start
  94.2 0.0 copy-start.2
  94.3 5.0 %gather_heat.3 = (f32[512,128]{1,0:T(8,128)S(1)}, bf16[512,128]{1,0:T(8,128)(2,1)S(1)}) custom-call(bf16[64,136,128]{2,1,0:T(8,128)(2,1)} %all-to-all-done.recv_hbm, f32[2048,128]{1,0:T(8,128)S(1)} %copy-done.6, f32[2048,128]{1,0:T(8,128)} %copy-done.1, f32[2048,128]{1,0:T(8,128)} %copy-done.7, f32[2048,128]{1,0:T(8,128)} %copy-done.8), custom_call_target="tpu_custom_call" | custom-call | flops 2147483648 | bytes 8000000 | tf_op jit(solution)/shard_map/gather_heat/pallas_call | solution.py:249
  99.3 0.0 collective-permute-done.2.left_ref
  99.3 0.0 collective-permute-done.3.right_ref
  99.3 12.2 %last_sweep.1 = (f32[2048,128]{1,0:T(8,128)}, bf16[64,128,128]{2,1,0:T(8,128)(2,1)S(1)}) custom-call(s32[32,16]{1,0:T(8,128)S(1)} %add_select_fusion.cols_ref, bf16[32,64,1024]{2,1,0:T(8,128)(2,1)S(1)} %copy-done, bf16[768,128]{1,0:T(8,128)(2,1)S(1)} %collective-permute-done.2.left_ref, bf16[768,128]{1,0:T(8,128)(2,1)S(1)} %get-tuple-element.24.head_ref, ...), custom_call_target="tpu_custom_call" | custom-call | tf_op jit(solution)/shard_map/last_sweep/pallas_call | solution.py:333
  111.5 61.9 %all_to_all.10.back_ref = bf16[64,128,128]{2,1,0:T(8,128)(2,1)S(1)} all-to-all(bf16[64,128,128]{2,1,0:T(8,128)(2,1)S(1)} %get-tuple-element.31), channel_id=1, replica_groups=mesh['dom'=64,'blk'=4] {'dom'}, dimensions={0} | all-to-all | bytes 4194304 | tf_op jit(solution)/shard_map/all_to_all | solution.py:430
  173.4 5.3 %unpack.1 = bf16[4096,128]{1,0:T(8,128)(2,1)} custom-call(s32[32,128]{1,0:T(8,128)S(1)} %copy-done.4, bf16[64,128,128]{2,1,0:T(8,128)(2,1)S(1)} %all_to_all.10.back_ref), custom_call_target="tpu_custom_call" | custom-call | tf_op jit(solution)/shard_map/unpack/pallas_call | solution.py:377
  (13 shorter events, 0.0 us)
Async XLA Ops:
  1.8 11.5 %collective-permute-start = (f32[768,128]{1,0:T(8,128)S(1)}, f32[768,128]{1,0:T(8,128)S(1)}, u32[]{:S(2)}, u32[]{:S(2)}) collective-permute-start(f32[768,128]{1,0:T(8,128)S(1)} %get-tuple-element.33), channel_id=1, source_target_pairs={{0,1},{1,2},{2,3},{3,4},{4,5},{5,6},{6,7},{7,8},{8,9},{9,10},{10,1... | collective-permute-start | bytes 1179656 | tf_op jit(solution)/shard_map/ppermute | solution.py:396
  1.9 11.4 %collective-permute-start.1 = (f32[768,128]{1,0:T(8,128)S(1)}, f32[768,128]{1,0:T(8,128)S(1)}, u32[]{:S(2)}, u32[]{:S(2)}) collective-permute-start(f32[768,128]{1,0:T(8,128)S(1)} %get-tuple-element.32), channel_id=1, source_target_pairs={{1,0},{2,1},{3,2},{4,3},{5,4},{6,5},{7,6},{8,7},{9,8},{10,9},{11,1... | collective-permute-start | bytes 1179656 | tf_op jit(solution)/shard_map/ppermute | solution.py:397
  13.3 13.9 %copy-start.10 = (s32[32,16]{0,1:T(8,128)S(1)}, s32[32,16]{0,1:T(8,128)}, u32[]{:S(2)}) copy-start(s32[32,16]{0,1:T(8,128)} %param.17) | copy-start | bytes 6148
  13.3 14.0 %copy-start.9 = (f32[2048]{0:T(1024)S(1)}, f32[2048]{0:T(1024)}, u32[]{:S(2)}) copy-start(f32[2048]{0:T(1024)} %param.15) | copy-start | bytes 24580
  13.3 15.4 %copy-start.3 = (f32[2048,128]{1,0:T(8,128)S(1)}, f32[2048,128]{1,0:T(8,128)}, u32[]{:S(2)}) copy-start(f32[2048,128]{1,0:T(8,128)} %old_ref.1) | copy-start | bytes 3145732
  13.3 67.9 %all-to-all-start = ((bf16[64,136,128]{2,1,0:T(8,128)(2,1)}), bf16[64,136,128]{2,1,0:T(8,128)(2,1)}, u32[]{:S(2)}, u32[]{:S(2)}) async-start(bf16[64,136,128]{2,1,0:T(8,128)(2,1)} %get-tuple-element.18), calls=%async_computation | async-start | bytes 4456448 | tf_op jit(solution)/shard_map/all_to_all | solution.py:417
  33.5 1.0 copy-start.1
  34.4 1.0 copy-start.5
  35.4 1.0 copy-start.7
  36.4 1.0 copy-start.8
  81.3 12.9 %copy-start.6 = (f32[2048,128]{1,0:T(8,128)S(1)}, f32[2048,128]{1,0:T(8,128)}, u32[]{:S(2)}) copy-start(f32[2048,128]{1,0:T(8,128)} %copy-done.5) | copy-start | bytes 3145732
  91.1 8.2 %collective-permute-start.2 = (bf16[768,128]{1,0:T(8,128)(2,1)S(1)}, bf16[768,128]{1,0:T(8,128)(2,1)S(1)}, u32[]{:S(2)}, u32[]{:S(2)}) collective-permute-start(bf16[768,128]{1,0:T(8,128)(2,1)S(1)} %get-tuple-element.23.tail_ref), channel_id=1, source_target_pairs={{0,1},{1,2},{2,3},{3,4},{4,5},{5,6},{6,7},{7,8},{8,9},{9,10},{10,1... | collective-permute-start | bytes 589832 | tf_op jit(solution)/shard_map/ppermute | solution.py:396
  91.2 8.1 %collective-permute-start.3 = (bf16[768,128]{1,0:T(8,128)(2,1)S(1)}, bf16[768,128]{1,0:T(8,128)(2,1)S(1)}, u32[]{:S(2)}, u32[]{:S(2)}) collective-permute-start(bf16[768,128]{1,0:T(8,128)(2,1)S(1)} %get-tuple-element.24.head_ref), channel_id=1, source_target_pairs={{1,0},{2,1},{3,2},{4,3},{5,4},{6,5},{7,6},{8,7},{9,8},{10,9},{11,1... | collective-permute-start | bytes 589832 | tf_op jit(solution)/shard_map/ppermute | solution.py:397
  94.2 5.1 %copy-start = (bf16[32,64,1024]{2,1,0:T(8,128)(2,1)S(1)}, bf16[32,64,1024]{2,1,0:T(8,128)(2,1)}, u32[]{:S(2)}) copy-start(bf16[32,64,1024]{2,1,0:T(8,128)(2,1)} %cond_ref.3) | copy-start | bytes 12582916
  94.2 5.1 %copy-start.2 = (f32[2048,128]{1,0:T(8,128)S(1)}, f32[2048,128]{1,0:T(8,128)}, u32[]{:S(2)}) copy-start(f32[2048,128]{1,0:T(8,128)} %copy-done.1) | copy-start | bytes 3145732
  111.5 61.9 %copy-start.4 = (s32[32,128]{1,0:T(8,128)S(1)}, s32[32,128]{1,0:T(8,128)}, u32[]{:S(2)}) copy-start(s32[32,128]{1,0:T(8,128)} %get-tuple-element.30.slot_ref) | copy-start | bytes 49156

commit v5 on v4

--- a/solution.py
+++ b/solution.py
@@ -173,10 +173,11 @@
 STEP = 8
 
 
-def gather_kernel(spans, recv_hbm, base_hbm, gain_hbm, next_hbm, slope_hbm, *rest):
+def gather_kernel(spans, turning, recv_hbm, base_hbm, gain_hbm, next_hbm, slope_hbm, *rest):
     count = len(spans)
     next_refs, low_refs = rest[:count], rest[count : 2 * count]
-    recv_ref, node_in, chosen, high, values, recv_sems, sems = rest[2 * count :]
+    turned_refs = rest[2 * count : 2 * count + turning]
+    recv_ref, node_in, chosen, high, values, recv_sems, sems = rest[2 * count + turning :]
     peers = recv_ref.shape[0]
     group = peers // PARTS
     samples = node_in.shape[2]
@@ -211,6 +212,10 @@
     for g in range(PARTS):
         arrivals[g].wait()
         lax.fori_loop(g * group, (g + 1) * group, split, 0, unroll=4)
+    for ref in turned_refs:
+        for g in range(peers // 16):
+            stacked = jnp.concatenate([recv_ref[g * 16 + j, CAP:].astype(F32) for j in range(16)], axis=0)
+            ref[g] = stacked.T
     part = peers * CAP // STEP
     for copy in copies:
         copy.wait()
@@ -241,13 +246,14 @@
         lax.fori_loop(0, size // LANES // mt, tile, 0)
 
 
-def gather_heat(recv, base, gain, following, slope, spans):
+def gather_heat(recv, base, gain, following, slope, spans, turning=0):
     samples = base.shape[1]
     slots = recv.shape[0] * CAP
     count = sum(size for _, size in spans)
     shapes = [jax.ShapeDtypeStruct((size, samples), kind) for kind in (F32, BF16) for _, size in spans]
+    shapes += [jax.ShapeDtypeStruct((recv.shape[0] // 16, CAP, LANES), F32)] * turning
     return pl.pallas_call(
-        functools.partial(gather_kernel, spans),
+        functools.partial(gather_kernel, spans, turning),
         out_shape=tuple(shapes),
         in_specs=[HBM] * 5,
         out_specs=(VMEM,) * len(shapes),
@@ -264,24 +270,6 @@
         cost_estimate=pl.CostEstimate(flops=4 * slots * count * samples, bytes_accessed=8_000_000, transcendentals=0),
         name="gather_heat",
     )(recv, base, gain, following, slope)
-
-
-def turn_kernel(meta_ref, turned_ref):
-    for g in range(meta_ref.shape[0] // 16):
-        stacked = jnp.concatenate([meta_ref[g * 16 + j].astype(F32) for j in range(16)], axis=0)
-        turned_ref[g] = stacked.T
-
-
-def turn(meta):
-    groups = meta.shape[0] // 16
-    return pl.pallas_call(
-        turn_kernel,
-        out_shape=jax.ShapeDtypeStruct((groups, CAP, LANES), F32),
-        in_specs=[VMEM],
-        out_specs=VMEM,
-        compiler_params=params(8),
-        name="turn",
-    )(meta)
 
 
 def last_kernel(cols_ref, cond_ref, left_ref, head_ref, mid_ref, tail_ref, right_ref, next_head, next_mid, next_tail, gain_ref, turned_ref, temp_hbm, back_ref, window_ref, temp, pair, temp_sem):
@@ -424,9 +412,9 @@
     inner = ((width, nodes - 2 * width),)
     next_head, next_tail, head, tail = gather_heat(recv, base, gain, following, slope, outer)
     left, right = halo(head, tail)
-    next_mid, mid = gather_heat(recv, base, gain, following, slope, inner)
+    next_mid, mid, turned = gather_heat(recv, base, gain, following, slope, inner, 1)
     window = (left, head, mid, tail, right)
-    temp, back = last_sweep(cols, conduction, window, (next_head, next_mid, next_tail), gain, turn(recv[:, CAP:]))
+    temp, back = last_sweep(cols, conduction, window, (next_head, next_mid, next_tail), gain, turned)
     returned = lax.all_to_all(back, "dom", split_axis=0, concat_axis=0, tiled=True)
     return temp, unpack(slots, returned)
 

time: 179 us -> 181 us (1.011)
    ppermute x2, starting transfers between devices: 0.18 us -> 2.22 us  [halo(): lax.ppermute(tail, axes, [(i, (i + 1) % count) for i in range(count)])]
    pallas_call x3 -> x2, Pallas kernels: 14.9 us -> 14.8 us  [gather_heat(): pl.pallas_call(functools.partial(gather_kernel, spans, turning), out_shap...]
  transfers between devices with their start and end apart: 5 -> 5, of which waited for: 1 -> 3; matrix products, arithmetic and copies ran while one was open for 1% -> 1% of each run, Pallas kernels for 11% -> 11%
where the time goes in v5:
time: 181 us
  blocking collectives  62.8 us (35%)
  Pallas kernels  46.3 us (26%)
  waiting for transfers between devices  44.4 us (25%)
  starting transfers between devices  19.6 us (11%)
  local copies, waits for them, and re-layouts  6.57 us (4%)
    all_to_all x1, blocking collectives, body(): lax.all_to_all(back, 'dom', split_axis=0, concat_axis=0, tiled=True)  62.8 us
    all_to_all x1, waiting for transfers between devices, body(): recv = lax.all_to_all(send, 'dom', split_axis=0, concat_axis=0, tiled=True)  43.9 us
    pallas_call x2, Pallas kernels, gather_heat(): pl.pallas_call(functools.partial(gather_kernel, spans, turning), out_shap...  14.8 us
    all_to_all x1, starting transfers between devices, body(): recv = lax.all_to_all(send, 'dom', split_axis=0, concat_axis=0, tiled=True)  14.5 us
    pallas_call x1, Pallas kernels, last_sweep(): pl.pallas_call(last_kernel, out_shape=(jax.ShapeDtypeStruct((nodes, sampl...  12.2 us
    pallas_call x1, Pallas kernels, pack(): pl.pallas_call(pack_kernel, out_shape=(jax.ShapeDtypeStruct((peers, CAP +...  9.36 us
    pallas_call x1, Pallas kernels, unpack(): pl.pallas_call(unpack_kernel, out_shape=jax.ShapeDtypeStruct((count, samp...  5.3 us
    pallas_call x1, Pallas kernels, first_sweep(): pl.pallas_call(first_kernel, out_shape=(jax.ShapeDtypeStruct((nodes, samp...  4.76 us
  transfers between devices with their start and end apart: 5, of which 3 were waited for; matrix products, arithmetic and copies ran while one was open for 1% of the time, Pallas kernels for 11%

profile of v5, /device:TPU:6, one launch (start us, length us, event | category | flops | bytes accessed | tf_op | source)
XLA Modules:
  0.0 180.7 jit_solution(15318129992501014564)
XLA Ops:
  0.6 1.2 fusion.1
  1.8 0.9 collective-permute-start.1
  2.7 2.1 %collective-permute-start = (f32[768,128]{1,0:T(8,128)S(1)}, f32[768,128]{1,0:T(8,128)S(1)}, u32[]{:S(2)}, u32[]{:S(2)}) collective-permute-start(f32[768,128]{1,0:T(8,128)S(1)} %get-tuple-element.35), channel_id=1, source_target_pairs={{0,1},{1,2},{2,3},{3,4},{4,5},{5,6},{6,7},{7,8},{8,9},{9,10},{10,1... | collective-permute-start | bytes 1179656 | tf_op jit(solution)/shard_map/ppermute | solution.py:384
  4.8 9.4 %pack.1 = (bf16[64,136,128]{2,1,0:T(8,128)(2,1)}, s32[32,128]{1,0:T(8,128)}) custom-call(s32[32,128]{1,0:T(8,128)} %bitcast.6, s32[32,128]{1,0:T(8,128)} %bitcast.7, bf16[32,128]{1,0:T(8,128)(2,1)} %bitcast.8, bf16[32,128]{1,0:T(8,128)(2,1)} %bitcast.9, bf16[4096,128]{1,0:T(8,128)(2,1)} %cur_hbm.1), custom_call_target="tpu_custom_call" | custom-call | flops 8000000000 | bytes 4000000 | tf_op jit(solution)/shard_map/pack/pallas_call | solution.py:94
  14.2 0.3 collective-permute-done.1.right_ref
  14.5 0.0 collective-permute-done.left_ref
  14.5 14.5 %all-to-all-start = ((bf16[64,136,128]{2,1,0:T(8,128)(2,1)}), bf16[64,136,128]{2,1,0:T(8,128)(2,1)}, u32[]{:S(2)}, u32[]{:S(2)}) async-start(bf16[64,136,128]{2,1,0:T(8,128)(2,1)} %get-tuple-element.19), calls=%async_computation | async-start | bytes 4456448 | tf_op jit(solution)/shard_map/all_to_all | solution.py:405
  29.0 0.0 copy-done.10
  29.0 0.1 copy.12
  29.1 0.0 copy-done.9
  29.1 1.3 copy.13.cap_ref
  30.5 0.0 copy-done.3
  30.5 4.8 %first_sweep.1 = (f32[2048,128]{1,0:T(8,128)S(1)}, f32[2048,128]{1,0:T(8,128)S(1)}, f32[2048,128]{1,0:T(8,128)S(1)}, f32[2048,128]{1,0:T(8,128)S(1)}) custom-call(s32[32,16]{1,0:T(8,128)S(1)} %add_select_fusion.cols_ref, bf16[32,64,1024]{2,1,0:T(8,128)(2,1)} %cond_ref.3, f32[768,128]{1,0:T(8,128)S(1)} %collective-permute-done.left_ref, ...), custom_call_target="tpu_custom_call" | custom-call | flops 8000000000 | bytes 8000000 | tf_op jit(solution)/shard_map/first_sweep/pallas_call | solution.py:161
  35.3 0.0 copy-start.1
  35.3 1.0 copy-done.1
  36.2 1.0 copy-done.5
  37.2 1.0 copy-done.7
  38.2 1.0 copy-done.8
  39.2 43.9 %all-to-all-done.recv_hbm = bf16[64,136,128]{2,1,0:T(8,128)(2,1)} async-done(((bf16[64,136,128]{2,1,0:T(8,128)(2,1)}), bf16[64,136,128]{2,1,0:T(8,128)(2,1)}, u32[]{:S(2)}, u32[]{:S(2)}) %all-to-all-start) | async-done | bytes 2228256 | tf_op jit(solution)/shard_map/all_to_all | solution.py:405
  83.1 9.8 %gather_heat.2 = (f32[768,128]{1,0:T(8,128)S(1)}, f32[768,128]{1,0:T(8,128)S(1)}, bf16[768,128]{1,0:T(8,128)(2,1)S(1)}, bf16[768,128]{1,0:T(8,128)(2,1)S(1)}) custom-call(bf16[64,136,128]{2,1,0:T(8,128)(2,1)} %all-to-all-done.recv_hbm, f32[2048,128]{1,0:T(8,128)} %copy-done.5, f32[2048,128]{1,0:T(8,128)} %copy-done.1, f32[2048,128]{1,0:T(8,128)} %copy-done.7, ...), custom_call_target="tpu_custom_call" | custom-call | flops 6442450944 | bytes 8000000 | tf_op jit(solution)/shard_map/gather_heat/pallas_call | solution.py:255
  92.9 0.1 collective-permute-start.2
  93.0 0.0 copy-start
  93.0 0.0 copy-start.2
  93.0 2.0 %collective-permute-start.3 = (bf16[768,128]{1,0:T(8,128)(2,1)S(1)}, bf16[768,128]{1,0:T(8,128)(2,1)S(1)}, u32[]{:S(2)}, u32[]{:S(2)}) collective-permute-start(bf16[768,128]{1,0:T(8,128)(2,1)S(1)} %get-tuple-element.25.head_ref), channel_id=1, source_target_pairs={{1,0},{2,1},{3,2},{4,3},{5,4},{6,5},{7,6},{8,7},{9,8},{10,9},{11,1... | collective-permute-start | bytes 589832 | tf_op jit(solution)/shard_map/ppermute | solution.py:385
  95.0 5.0 %gather_heat.3 = (f32[512,128]{1,0:T(8,128)S(1)}, bf16[512,128]{1,0:T(8,128)(2,1)S(1)}, f32[4,128,128]{2,1,0:T(8,128)S(1)}) custom-call(bf16[64,136,128]{2,1,0:T(8,128)(2,1)} %all-to-all-done.recv_hbm, f32[2048,128]{1,0:T(8,128)S(1)} %copy-done.6, f32[2048,128]{1,0:T(8,128)} %copy-done.1, f32[2048,128]{1,0:T(8,128)} %copy-done.7, f32[2048,128]{1,0:T(8,128)} %copy-done.8), custom_call_target="tpu_custom_call" | custom-call | flops 2147483648 | bytes 8000000 | tf_op jit(solution)/shard_map/gather_heat/pallas_call | solution.py:255
  100.0 0.0 collective-permute-done.2.left_ref
  100.0 0.2 collective-permute-done.3.right_ref
  100.2 0.0 copy-done.2
  100.2 12.2 %last_sweep.1 = (f32[2048,128]{1,0:T(8,128)}, bf16[64,128,128]{2,1,0:T(8,128)(2,1)S(1)}) custom-call(s32[32,16]{1,0:T(8,128)S(1)} %add_select_fusion.cols_ref, bf16[32,64,1024]{2,1,0:T(8,128)(2,1)S(1)} %copy-done, bf16[768,128]{1,0:T(8,128)(2,1)S(1)} %collective-permute-done.2.left_ref, bf16[768,128]{1,0:T(8,128)(2,1)S(1)} %get-tuple-element.25.head_ref, ...), custom_call_target="tpu_custom_call" | custom-call | tf_op jit(solution)/shard_map/last_sweep/pallas_call | solution.py:321
  112.4 62.8 %all_to_all.10.back_ref = bf16[64,128,128]{2,1,0:T(8,128)(2,1)S(1)} all-to-all(bf16[64,128,128]{2,1,0:T(8,128)(2,1)S(1)} %get-tuple-element.33), channel_id=1, replica_groups=mesh['dom'=64,'blk'=4] {'dom'}, dimensions={0} | all-to-all | bytes 4194304 | tf_op jit(solution)/shard_map/all_to_all | solution.py:418
  175.2 0.0 copy-done.4
  175.2 5.3 %unpack.1 = bf16[4096,128]{1,0:T(8,128)(2,1)} custom-call(s32[32,128]{1,0:T(8,128)S(1)} %copy-done.4, bf16[64,128,128]{2,1,0:T(8,128)(2,1)S(1)} %all_to_all.10.back_ref), custom_call_target="tpu_custom_call" | custom-call | tf_op jit(solution)/shard_map/unpack/pallas_call | solution.py:365
  (11 shorter events, 0.0 us)
Async XLA Ops:
  1.8 12.7 %collective-permute-start.1 = (f32[768,128]{1,0:T(8,128)S(1)}, f32[768,128]{1,0:T(8,128)S(1)}, u32[]{:S(2)}, u32[]{:S(2)}) collective-permute-start(f32[768,128]{1,0:T(8,128)S(1)} %get-tuple-element.34), channel_id=1, source_target_pairs={{1,0},{2,1},{3,2},{4,3},{5,4},{6,5},{7,6},{8,7},{9,8},{10,9},{11,1... | collective-permute-start | bytes 1179656 | tf_op jit(solution)/shard_map/ppermute | solution.py:385
  2.7 11.8 %collective-permute-start = (f32[768,128]{1,0:T(8,128)S(1)}, f32[768,128]{1,0:T(8,128)S(1)}, u32[]{:S(2)}, u32[]{:S(2)}) collective-permute-start(f32[768,128]{1,0:T(8,128)S(1)} %get-tuple-element.35), channel_id=1, source_target_pairs={{0,1},{1,2},{2,3},{3,4},{4,5},{5,6},{6,7},{7,8},{8,9},{9,10},{10,1... | collective-permute-start | bytes 1179656 | tf_op jit(solution)/shard_map/ppermute | solution.py:384
  14.5 14.5 %copy-start.10 = (s32[32,16]{0,1:T(8,128)S(1)}, s32[32,16]{0,1:T(8,128)}, u32[]{:S(2)}) copy-start(s32[32,16]{0,1:T(8,128)} %param.17) | copy-start | bytes 6148
  14.5 14.6 %copy-start.9 = (f32[2048]{0:T(1024)S(1)}, f32[2048]{0:T(1024)}, u32[]{:S(2)}) copy-start(f32[2048]{0:T(1024)} %param.15) | copy-start | bytes 24580
  14.5 16.0 %copy-start.3 = (f32[2048,128]{1,0:T(8,128)S(1)}, f32[2048,128]{1,0:T(8,128)}, u32[]{:S(2)}) copy-start(f32[2048,128]{1,0:T(8,128)} %old_ref.1) | copy-start | bytes 3145732
  14.5 68.5 %all-to-all-start = ((bf16[64,136,128]{2,1,0:T(8,128)(2,1)}), bf16[64,136,128]{2,1,0:T(8,128)(2,1)}, u32[]{:S(2)}, u32[]{:S(2)}) async-start(bf16[64,136,128]{2,1,0:T(8,128)(2,1)} %get-tuple-element.19), calls=%async_computation | async-start | bytes 4456448 | tf_op jit(solution)/shard_map/all_to_all | solution.py:405
  35.3 1.0 copy-start.1
  36.2 1.0 copy-start.5
  37.2 1.0 copy-start.7
  38.2 1.0 copy-start.8
  83.1 11.9 %copy-start.6 = (f32[2048,128]{1,0:T(8,128)S(1)}, f32[2048,128]{1,0:T(8,128)}, u32[]{:S(2)}) copy-start(f32[2048,128]{1,0:T(8,128)} %copy-done.5) | copy-start | bytes 3145732
  92.9 7.1 %collective-permute-start.2 = (bf16[768,128]{1,0:T(8,128)(2,1)S(1)}, bf16[768,128]{1,0:T(8,128)(2,1)S(1)}, u32[]{:S(2)}, u32[]{:S(2)}) collective-permute-start(bf16[768,128]{1,0:T(8,128)(2,1)S(1)} %get-tuple-element.24.tail_ref), channel_id=1, source_target_pairs={{0,1},{1,2},{2,3},{3,4},{4,5},{5,6},{6,7},{7,8},{8,9},{9,10},{10,1... | collective-permute-start | bytes 589832 | tf_op jit(solution)/shard_map/ppermute | solution.py:384
  93.0 7.2 %copy-start = (bf16[32,64,1024]{2,1,0:T(8,128)(2,1)S(1)}, bf16[32,64,1024]{2,1,0:T(8,128)(2,1)}, u32[]{:S(2)}) copy-start(bf16[32,64,1024]{2,1,0:T(8,128)(2,1)} %cond_ref.3) | copy-start | bytes 12582916
  93.0 7.2 %copy-start.2 = (f32[2048,128]{1,0:T(8,128)S(1)}, f32[2048,128]{1,0:T(8,128)}, u32[]{:S(2)}) copy-start(f32[2048,128]{1,0:T(8,128)} %copy-done.1) | copy-start | bytes 3145732
  93.0 7.2 %collective-permute-start.3 = (bf16[768,128]{1,0:T(8,128)(2,1)S(1)}, bf16[768,128]{1,0:T(8,128)(2,1)S(1)}, u32[]{:S(2)}, u32[]{:S(2)}) collective-permute-start(bf16[768,128]{1,0:T(8,128)(2,1)S(1)} %get-tuple-element.25.head_ref), channel_id=1, source_target_pairs={{1,0},{2,1},{3,2},{4,3},{5,4},{6,5},{7,6},{8,7},{9,8},{10,9},{11,1... | collective-permute-start | bytes 589832 | tf_op jit(solution)/shard_map/ppermute | solution.py:385
  112.4 62.8 %copy-start.4 = (s32[32,128]{1,0:T(8,128)S(1)}, s32[32,128]{1,0:T(8,128)}, u32[]{:S(2)}) copy-start(s32[32,128]{1,0:T(8,128)} %get-tuple-element.32.slot_ref) | copy-start | bytes 49156

commit v6 on v5

--- a/solution.py
+++ b/solution.py
@@ -392,7 +392,7 @@
     blocks, size, _ = conduction.shape
     chunks = count // LANES
     width = HB * size
-    left, right = halo(temp_old[:width], temp_old[-width:])
+    left, right = halo(temp_old[:width].astype(BF16), temp_old[-width:].astype(BF16))
     send, slots = pack(
         dest_part.reshape(chunks, LANES),
         dest_row.reshape(chunks, LANES),

time: 181 us -> 179 us (0.989)
  blocking collectives: 62.8 us -> 60.9 us
    all_to_all x1, blocking collectives: 62.8 us -> 60.9 us  [body(): lax.all_to_all(back, 'dom', split_axis=0, concat_axis=0, tiled=True)]
  transfers between devices with their start and end apart: 5 -> 5, of which waited for: 3 -> 1; matrix products, arithmetic and copies ran while one was open for 1% -> 1% of each run, Pallas kernels for 11% -> 11%
where the time goes in v6:
time: 179 us
  blocking collectives  60.9 us (34%)
  Pallas kernels  46.3 us (26%)
  waiting for transfers between devices  43.9 us (25%)
  starting transfers between devices  19.9 us (11%)
  local copies, waits for them, and re-layouts  5.44 us (3%)
    all_to_all x1, blocking collectives, body(): lax.all_to_all(back, 'dom', split_axis=0, concat_axis=0, tiled=True)  60.9 us
    all_to_all x1, waiting for transfers between devices, body(): recv = lax.all_to_all(send, 'dom', split_axis=0, concat_axis=0, tiled=True)  43.9 us
    pallas_call x2, Pallas kernels, gather_heat(): pl.pallas_call(functools.partial(gather_kernel, spans, turning), out_shap...  14.8 us
    all_to_all x1, starting transfers between devices, body(): recv = lax.all_to_all(send, 'dom', split_axis=0, concat_axis=0, tiled=True)  14.7 us
    pallas_call x1, Pallas kernels, last_sweep(): pl.pallas_call(last_kernel, out_shape=(jax.ShapeDtypeStruct((nodes, sampl...  12.2 us
    pallas_call x1, Pallas kernels, pack(): pl.pallas_call(pack_kernel, out_shape=(jax.ShapeDtypeStruct((peers, CAP +...  9.36 us
    pallas_call x1, Pallas kernels, unpack(): pl.pallas_call(unpack_kernel, out_shape=jax.ShapeDtypeStruct((count, samp...  5.3 us
    pallas_call x1, Pallas kernels, first_sweep(): pl.pallas_call(first_kernel, out_shape=(jax.ShapeDtypeStruct((nodes, samp...  4.73 us
  transfers between devices with their start and end apart: 5, of which 1 were waited for; matrix products, arithmetic and copies ran while one was open for 1% of the time, Pallas kernels for 11%

profile of v6, /device:TPU:6, one launch (start us, length us, event | category | flops | bytes accessed | tf_op | source)
XLA Modules:
  0.0 178.7 jit_solution(2765002065145323040)
XLA Ops:
  0.6 1.3 convert.4
  1.9 0.9 collective-permute-start.1
  2.9 2.1 %collective-permute-start = (bf16[768,128]{1,0:T(8,128)(2,1)S(1)}, bf16[768,128]{1,0:T(8,128)(2,1)S(1)}, u32[]{:S(2)}, u32[]{:S(2)}) collective-permute-start(bf16[768,128]{1,0:T(8,128)(2,1)S(1)} %get-tuple-element.35), channel_id=1, source_target_pairs={{0,1},{1,2},{2,3},{3,4},{4,5},{5,6},{6,7},{7,8},{8,9},{9,10},{10,1... | collective-permute-start | bytes 589832 | tf_op jit(solution)/shard_map/ppermute | solution.py:384
  5.0 9.4 %pack.1 = (bf16[64,136,128]{2,1,0:T(8,128)(2,1)}, s32[32,128]{1,0:T(8,128)}) custom-call(s32[32,128]{1,0:T(8,128)} %bitcast.6, s32[32,128]{1,0:T(8,128)} %bitcast.7, bf16[32,128]{1,0:T(8,128)(2,1)} %bitcast.8, bf16[32,128]{1,0:T(8,128)(2,1)} %bitcast.9, bf16[4096,128]{1,0:T(8,128)(2,1)} %cur_hbm.1), custom_call_target="tpu_custom_call" | custom-call | flops 8000000000 | bytes 4000000 | tf_op jit(solution)/shard_map/pack/pallas_call | solution.py:94
  14.4 0.0 collective-permute-done.1.right_ref
  14.4 0.0 collective-permute-done.left_ref
  14.4 0.0 copy-start.10
  14.4 0.0 copy-start.9
  14.4 0.0 copy-start.3
  14.4 14.7 %all-to-all-start = ((bf16[64,136,128]{2,1,0:T(8,128)(2,1)}), bf16[64,136,128]{2,1,0:T(8,128)(2,1)}, u32[]{:S(2)}, u32[]{:S(2)}) async-start(bf16[64,136,128]{2,1,0:T(8,128)(2,1)} %get-tuple-element.19), calls=%async_computation | async-start | bytes 4456448 | tf_op jit(solution)/shard_map/all_to_all | solution.py:405
  29.2 0.0 copy-done.10
  29.2 0.1 copy.12
  29.3 0.0 copy-done.9
  29.3 1.3 copy.13.cap_ref
  30.6 4.7 %first_sweep.1 = (f32[2048,128]{1,0:T(8,128)S(1)}, f32[2048,128]{1,0:T(8,128)S(1)}, f32[2048,128]{1,0:T(8,128)S(1)}, f32[2048,128]{1,0:T(8,128)S(1)}) custom-call(s32[32,16]{1,0:T(8,128)S(1)} %add_select_fusion.cols_ref, bf16[32,64,1024]{2,1,0:T(8,128)(2,1)} %cond_ref.3, bf16[768,128]{1,0:T(8,128)(2,1)S(1)} %collective-permute-done.left_ref, ...), custom_call_target="tpu_custom_call" | custom-call | flops 8000000000 | bytes 8000000 | tf_op jit(solution)/shard_map/first_sweep/pallas_call | solution.py:161
  35.4 0.0 copy-start.1
  35.4 1.0 copy-done.1
  36.3 1.0 copy-done.5
  37.3 1.0 copy-done.7
  38.3 1.0 copy-done.8
  39.3 43.9 %all-to-all-done.recv_hbm = bf16[64,136,128]{2,1,0:T(8,128)(2,1)} async-done(((bf16[64,136,128]{2,1,0:T(8,128)(2,1)}), bf16[64,136,128]{2,1,0:T(8,128)(2,1)}, u32[]{:S(2)}, u32[]{:S(2)}) %all-to-all-start) | async-done | bytes 2228256 | tf_op jit(solution)/shard_map/all_to_all | solution.py:405
  83.2 9.8 %gather_heat.2 = (f32[768,128]{1,0:T(8,128)S(1)}, f32[768,128]{1,0:T(8,128)S(1)}, bf16[768,128]{1,0:T(8,128)(2,1)S(1)}, bf16[768,128]{1,0:T(8,128)(2,1)S(1)}) custom-call(bf16[64,136,128]{2,1,0:T(8,128)(2,1)} %all-to-all-done.recv_hbm, f32[2048,128]{1,0:T(8,128)} %copy-done.5, f32[2048,128]{1,0:T(8,128)} %copy-done.1, f32[2048,128]{1,0:T(8,128)} %copy-done.7, ...), custom_call_target="tpu_custom_call" | custom-call | flops 6442450944 | bytes 8000000 | tf_op jit(solution)/shard_map/gather_heat/pallas_call | solution.py:255
  93.0 0.1 collective-permute-start.2
  93.1 0.0 copy-start
  93.1 0.0 copy-start.2
  93.1 2.0 %collective-permute-start.3 = (bf16[768,128]{1,0:T(8,128)(2,1)S(1)}, bf16[768,128]{1,0:T(8,128)(2,1)S(1)}, u32[]{:S(2)}, u32[]{:S(2)}) collective-permute-start(bf16[768,128]{1,0:T(8,128)(2,1)S(1)} %get-tuple-element.25.head_ref), channel_id=1, source_target_pairs={{1,0},{2,1},{3,2},{4,3},{5,4},{6,5},{7,6},{8,7},{9,8},{10,9},{11,1... | collective-permute-start | bytes 589832 | tf_op jit(solution)/shard_map/ppermute | solution.py:385
  95.1 5.0 %gather_heat.3 = (f32[512,128]{1,0:T(8,128)S(1)}, bf16[512,128]{1,0:T(8,128)(2,1)S(1)}, f32[4,128,128]{2,1,0:T(8,128)S(1)}) custom-call(bf16[64,136,128]{2,1,0:T(8,128)(2,1)} %all-to-all-done.recv_hbm, f32[2048,128]{1,0:T(8,128)S(1)} %copy-done.6, f32[2048,128]{1,0:T(8,128)} %copy-done.1, f32[2048,128]{1,0:T(8,128)} %copy-done.7, f32[2048,128]{1,0:T(8,128)} %copy-done.8), custom_call_target="tpu_custom_call" | custom-call | flops 2147483648 | bytes 8000000 | tf_op jit(solution)/shard_map/gather_heat/pallas_call | solution.py:255
  100.1 0.0 collective-permute-done.2.left_ref
  100.1 0.0 collective-permute-done.3.right_ref
  100.1 12.2 %last_sweep.1 = (f32[2048,128]{1,0:T(8,128)}, bf16[64,128,128]{2,1,0:T(8,128)(2,1)S(1)}) custom-call(s32[32,16]{1,0:T(8,128)S(1)} %add_select_fusion.cols_ref, bf16[32,64,1024]{2,1,0:T(8,128)(2,1)S(1)} %copy-done, bf16[768,128]{1,0:T(8,128)(2,1)S(1)} %collective-permute-done.2.left_ref, bf16[768,128]{1,0:T(8,128)(2,1)S(1)} %get-tuple-element.25.head_ref, ...), custom_call_target="tpu_custom_call" | custom-call | tf_op jit(solution)/shard_map/last_sweep/pallas_call | solution.py:321
  112.3 60.9 %all_to_all.10.back_ref = bf16[64,128,128]{2,1,0:T(8,128)(2,1)S(1)} all-to-all(bf16[64,128,128]{2,1,0:T(8,128)(2,1)S(1)} %get-tuple-element.33), channel_id=1, replica_groups=mesh['dom'=64,'blk'=4] {'dom'}, dimensions={0} | all-to-all | bytes 4194304 | tf_op jit(solution)/shard_map/all_to_all | solution.py:418
  173.3 5.3 %unpack.1 = bf16[4096,128]{1,0:T(8,128)(2,1)} custom-call(s32[32,128]{1,0:T(8,128)S(1)} %copy-done.4, bf16[64,128,128]{2,1,0:T(8,128)(2,1)S(1)} %all_to_all.10.back_ref), custom_call_target="tpu_custom_call" | custom-call | tf_op jit(solution)/shard_map/unpack/pallas_call | solution.py:365
  (12 shorter events, 0.1 us)
Async XLA Ops:
  1.9 12.4 %collective-permute-start.1 = (bf16[768,128]{1,0:T(8,128)(2,1)S(1)}, bf16[768,128]{1,0:T(8,128)(2,1)S(1)}, u32[]{:S(2)}, u32[]{:S(2)}) collective-permute-start(bf16[768,128]{1,0:T(8,128)(2,1)S(1)} %get-tuple-element.34), channel_id=1, source_target_pairs={{1,0},{2,1},{3,2},{4,3},{5,4},{6,5},{7,6},{8,7},{9,8},{10,9},{11,1... | collective-permute-start | bytes 589832 | tf_op jit(solution)/shard_map/ppermute | solution.py:385
  2.9 11.5 %collective-permute-start = (bf16[768,128]{1,0:T(8,128)(2,1)S(1)}, bf16[768,128]{1,0:T(8,128)(2,1)S(1)}, u32[]{:S(2)}, u32[]{:S(2)}) collective-permute-start(bf16[768,128]{1,0:T(8,128)(2,1)S(1)} %get-tuple-element.35), channel_id=1, source_target_pairs={{0,1},{1,2},{2,3},{3,4},{4,5},{5,6},{6,7},{7,8},{8,9},{9,10},{10,1... | collective-permute-start | bytes 589832 | tf_op jit(solution)/shard_map/ppermute | solution.py:384
  14.4 14.8 %copy-start.10 = (s32[32,16]{0,1:T(8,128)S(1)}, s32[32,16]{0,1:T(8,128)}, u32[]{:S(2)}) copy-start(s32[32,16]{0,1:T(8,128)} %param.17) | copy-start | bytes 6148
  14.4 14.9 %copy-start.9 = (f32[2048]{0:T(1024)S(1)}, f32[2048]{0:T(1024)}, u32[]{:S(2)}) copy-start(f32[2048]{0:T(1024)} %param.15) | copy-start | bytes 24580
  14.4 16.2 %copy-start.3 = (f32[2048,128]{1,0:T(8,128)S(1)}, f32[2048,128]{1,0:T(8,128)}, u32[]{:S(2)}) copy-start(f32[2048,128]{1,0:T(8,128)} %old_ref.1) | copy-start | bytes 3145732
  14.4 68.8 %all-to-all-start = ((bf16[64,136,128]{2,1,0:T(8,128)(2,1)}), bf16[64,136,128]{2,1,0:T(8,128)(2,1)}, u32[]{:S(2)}, u32[]{:S(2)}) async-start(bf16[64,136,128]{2,1,0:T(8,128)(2,1)} %get-tuple-element.19), calls=%async_computation | async-start | bytes 4456448 | tf_op jit(solution)/shard_map/all_to_all | solution.py:405
  35.4 1.0 copy-start.1
  36.3 1.0 copy-start.5
  37.3 1.0 copy-start.7
  38.3 1.0 copy-start.8
  83.2 11.9 %copy-start.6 = (f32[2048,128]{1,0:T(8,128)S(1)}, f32[2048,128]{1,0:T(8,128)}, u32[]{:S(2)}) copy-start(f32[2048,128]{1,0:T(8,128)} %copy-done.5) | copy-start | bytes 3145732
  93.0 7.1 %collective-permute-start.2 = (bf16[768,128]{1,0:T(8,128)(2,1)S(1)}, bf16[768,128]{1,0:T(8,128)(2,1)S(1)}, u32[]{:S(2)}, u32[]{:S(2)}) collective-permute-start(bf16[768,128]{1,0:T(8,128)(2,1)S(1)} %get-tuple-element.24.tail_ref), channel_id=1, source_target_pairs={{0,1},{1,2},{2,3},{3,4},{4,5},{5,6},{6,7},{7,8},{8,9},{9,10},{10,1... | collective-permute-start | bytes 589832 | tf_op jit(solution)/shard_map/ppermute | solution.py:384
  93.1 7.0 %copy-start = (bf16[32,64,1024]{2,1,0:T(8,128)(2,1)S(1)}, bf16[32,64,1024]{2,1,0:T(8,128)(2,1)}, u32[]{:S(2)}) copy-start(bf16[32,64,1024]{2,1,0:T(8,128)(2,1)} %cond_ref.3) | copy-start | bytes 12582916
  93.1 7.0 %copy-start.2 = (f32[2048,128]{1,0:T(8,128)S(1)}, f32[2048,128]{1,0:T(8,128)}, u32[]{:S(2)}) copy-start(f32[2048,128]{1,0:T(8,128)} %copy-done.1) | copy-start | bytes 3145732
  93.1 7.0 %collective-permute-start.3 = (bf16[768,128]{1,0:T(8,128)(2,1)S(1)}, bf16[768,128]{1,0:T(8,128)(2,1)S(1)}, u32[]{:S(2)}, u32[]{:S(2)}) collective-permute-start(bf16[768,128]{1,0:T(8,128)(2,1)S(1)} %get-tuple-element.25.head_ref), channel_id=1, source_target_pairs={{1,0},{2,1},{3,2},{4,3},{5,4},{6,5},{7,6},{8,7},{9,8},{10,9},{11,1... | collective-permute-start | bytes 589832 | tf_op jit(solution)/shard_map/ppermute | solution.py:385
  112.3 60.9 %copy-start.4 = (s32[32,128]{1,0:T(8,128)S(1)}, s32[32,128]{1,0:T(8,128)}, u32[]{:S(2)}) copy-start(s32[32,128]{1,0:T(8,128)} %get-tuple-element.32.slot_ref) | copy-start | bytes 49156

commit v7 on v6

--- a/solution.py
+++ b/solution.py
@@ -108,7 +108,7 @@
             pltpu.SemaphoreType.DMA((2,)),
             pltpu.SemaphoreType.DMA((PARTS,)),
         ],
-        compiler_params=params(60),
+        compiler_params=params(50),
         cost_estimate=pl.CostEstimate(flops=8_000_000_000, bytes_accessed=4_000_000, transcendentals=0),
         name="pack",
     )(part, row, res, coef, cur)

time: 179 us -> 179 us (level)
    unnamed x23 -> x31, local copies, waits for them, and re-layouts: 4.06 us -> 4.07 us
  transfers between devices with their start and end apart: 5 -> 5, of which waited for: 1 -> 1; matrix products, arithmetic and copies ran while one was open for 1% -> 1% of each run, Pallas kernels for 11% -> 10%
where the time goes in v7:
time: 179 us
  blocking collectives  61.3 us (34%)
  Pallas kernels  45.9 us (26%)
  waiting for transfers between devices  43.9 us (25%)
  starting transfers between devices  19.9 us (11%)
  local copies, waits for them, and re-layouts  5.45 us (3%)
    all_to_all x1, blocking collectives, body(): lax.all_to_all(back, 'dom', split_axis=0, concat_axis=0, tiled=True)  61.3 us
    all_to_all x1, waiting for transfers between devices, body(): recv = lax.all_to_all(send, 'dom', split_axis=0, concat_axis=0, tiled=True)  43.9 us
    pallas_call x2, Pallas kernels, gather_heat(): pl.pallas_call(functools.partial(gather_kernel, spans, turning), out_shap...  14.8 us
    all_to_all x1, starting transfers between devices, body(): recv = lax.all_to_all(send, 'dom', split_axis=0, concat_axis=0, tiled=True)  14.7 us
    pallas_call x1, Pallas kernels, last_sweep(): pl.pallas_call(last_kernel, out_shape=(jax.ShapeDtypeStruct((nodes, sampl...  12.2 us
    pallas_call x1, Pallas kernels, pack(): pl.pallas_call(pack_kernel, out_shape=(jax.ShapeDtypeStruct((peers, CAP +...  8.93 us
    pallas_call x1, Pallas kernels, unpack(): pl.pallas_call(unpack_kernel, out_shape=jax.ShapeDtypeStruct((count, samp...  5.3 us
    pallas_call x1, Pallas kernels, first_sweep(): pl.pallas_call(first_kernel, out_shape=(jax.ShapeDtypeStruct((nodes, samp...  4.74 us
  transfers between devices with their start and end apart: 5, of which 1 were waited for; matrix products, arithmetic and copies ran while one was open for 1% of the time, Pallas kernels for 10%

profile of v7, /device:TPU:6, one launch (start us, length us, event | category | flops | bytes accessed | tf_op | source)
XLA Modules:
  0.0 178.8 jit_solution(8335663206669259479)
XLA Ops:
  0.7 1.4 convert.4
  2.1 0.9 collective-permute-start.1
  3.0 2.1 %collective-permute-start = (bf16[768,128]{1,0:T(8,128)(2,1)S(1)}, bf16[768,128]{1,0:T(8,128)(2,1)S(1)}, u32[]{:S(2)}, u32[]{:S(2)}) collective-permute-start(bf16[768,128]{1,0:T(8,128)(2,1)S(1)} %get-tuple-element.35), channel_id=1, source_target_pairs={{0,1},{1,2},{2,3},{3,4},{4,5},{5,6},{6,7},{7,8},{8,9},{9,10},{10,1... | collective-permute-start | bytes 589832 | tf_op jit(solution)/shard_map/ppermute | solution.py:384
  5.1 0.0 copy-done.8
  5.2 8.9 %pack.1 = (bf16[64,136,128]{2,1,0:T(8,128)(2,1)}, s32[32,128]{1,0:T(8,128)S(1)}) custom-call(s32[32,128]{1,0:T(8,128)S(1)} %bitcast.5, s32[32,128]{1,0:T(8,128)S(1)} %bitcast.6, bf16[32,128]{1,0:T(8,128)(2,1)S(1)} %bitcast.7, bf16[32,128]{1,0:T(8,128)(2,1)S(1)} %bitcast.8, bf16[4096,128]{1,0:T(8,128)(2,1)S(1)} %copy-done.4), custom_call_target="tpu_custom_call" | custom-call | flops 8000000000 | bytes 4000000 | tf_op jit(solution)/shard_map/pack/pallas_call | solution.py:94
  14.1 0.0 collective-permute-done.1.right_ref
  14.1 0.0 collective-permute-done.left_ref
  14.1 0.0 copy-start.14
  14.1 0.0 copy-start.13
  14.1 0.0 copy-start.3
  14.1 14.7 %all-to-all-start = ((bf16[64,136,128]{2,1,0:T(8,128)(2,1)}), bf16[64,136,128]{2,1,0:T(8,128)(2,1)}, u32[]{:S(2)}, u32[]{:S(2)}) async-start(bf16[64,136,128]{2,1,0:T(8,128)(2,1)} %get-tuple-element.19), calls=%async_computation | async-start | bytes 4456448 | tf_op jit(solution)/shard_map/all_to_all | solution.py:405
  28.9 0.1 copy.12
  29.0 0.0 copy-done.13
  29.0 1.3 copy.13.cap_ref
  30.4 4.7 %first_sweep.1 = (f32[2048,128]{1,0:T(8,128)S(1)}, f32[2048,128]{1,0:T(8,128)S(1)}, f32[2048,128]{1,0:T(8,128)S(1)}, f32[2048,128]{1,0:T(8,128)S(1)}) custom-call(s32[32,16]{1,0:T(8,128)S(1)} %add_select_fusion.cols_ref, bf16[32,64,1024]{2,1,0:T(8,128)(2,1)} %cond_ref.3, bf16[768,128]{1,0:T(8,128)(2,1)S(1)} %collective-permute-done.left_ref, ...), custom_call_target="tpu_custom_call" | custom-call | flops 8000000000 | bytes 8000000 | tf_op jit(solution)/shard_map/first_sweep/pallas_call | solution.py:161
  35.1 0.0 copy-start.1
  35.1 1.0 copy-done.1
  36.1 1.0 copy-done.9
  37.1 1.0 copy-done.11
  38.1 1.0 copy-done.12
  39.1 43.9 %all-to-all-done.recv_hbm = bf16[64,136,128]{2,1,0:T(8,128)(2,1)} async-done(((bf16[64,136,128]{2,1,0:T(8,128)(2,1)}), bf16[64,136,128]{2,1,0:T(8,128)(2,1)}, u32[]{:S(2)}, u32[]{:S(2)}) %all-to-all-start) | async-done | bytes 2228256 | tf_op jit(solution)/shard_map/all_to_all | solution.py:405
  82.9 9.8 %gather_heat.2 = (f32[768,128]{1,0:T(8,128)S(1)}, f32[768,128]{1,0:T(8,128)S(1)}, bf16[768,128]{1,0:T(8,128)(2,1)S(1)}, bf16[768,128]{1,0:T(8,128)(2,1)S(1)}) custom-call(bf16[64,136,128]{2,1,0:T(8,128)(2,1)} %all-to-all-done.recv_hbm, f32[2048,128]{1,0:T(8,128)} %copy-done.9, f32[2048,128]{1,0:T(8,128)} %copy-done.1, f32[2048,128]{1,0:T(8,128)} %copy-done.11, ...), custom_call_target="tpu_custom_call" | custom-call | flops 6442450944 | bytes 8000000 | tf_op jit(solution)/shard_map/gather_heat/pallas_call | solution.py:255
  92.8 0.1 collective-permute-start.2
  92.8 0.0 copy-start
  92.9 0.0 copy-start.2
  92.9 2.0 %collective-permute-start.3 = (bf16[768,128]{1,0:T(8,128)(2,1)S(1)}, bf16[768,128]{1,0:T(8,128)(2,1)S(1)}, u32[]{:S(2)}, u32[]{:S(2)}) collective-permute-start(bf16[768,128]{1,0:T(8,128)(2,1)S(1)} %get-tuple-element.25.head_ref), channel_id=1, source_target_pairs={{1,0},{2,1},{3,2},{4,3},{5,4},{6,5},{7,6},{8,7},{9,8},{10,9},{11,1... | collective-permute-start | bytes 589832 | tf_op jit(solution)/shard_map/ppermute | solution.py:385
  94.9 5.0 %gather_heat.3 = (f32[512,128]{1,0:T(8,128)S(1)}, bf16[512,128]{1,0:T(8,128)(2,1)S(1)}, f32[4,128,128]{2,1,0:T(8,128)S(1)}) custom-call(bf16[64,136,128]{2,1,0:T(8,128)(2,1)} %all-to-all-done.recv_hbm, f32[2048,128]{1,0:T(8,128)S(1)} %copy-done.10, f32[2048,128]{1,0:T(8,128)} %copy-done.1, f32[2048,128]{1,0:T(8,128)} %copy-done.11, f32[2048,128]{1,0:T(8,128)} %copy-done.12), custom_call_target="tpu_custom_call" | custom-call | flops 2147483648 | bytes 8000000 | tf_op jit(solution)/shard_map/gather_heat/pallas_call | solution.py:255
  99.8 0.0 collective-permute-done.2.left_ref
  99.9 0.0 collective-permute-done.3.right_ref
  99.9 12.2 %last_sweep.1 = (f32[2048,128]{1,0:T(8,128)}, bf16[64,128,128]{2,1,0:T(8,128)(2,1)S(1)}) custom-call(s32[32,16]{1,0:T(8,128)S(1)} %add_select_fusion.cols_ref, bf16[32,64,1024]{2,1,0:T(8,128)(2,1)S(1)} %copy-done, bf16[768,128]{1,0:T(8,128)(2,1)S(1)} %collective-permute-done.2.left_ref, bf16[768,128]{1,0:T(8,128)(2,1)S(1)} %get-tuple-element.25.head_ref, ...), custom_call_target="tpu_custom_call" | custom-call | tf_op jit(solution)/shard_map/last_sweep/pallas_call | solution.py:321
  112.1 61.3 %all_to_all.10.back_ref = bf16[64,128,128]{2,1,0:T(8,128)(2,1)S(1)} all-to-all(bf16[64,128,128]{2,1,0:T(8,128)(2,1)S(1)} %get-tuple-element.33), channel_id=1, replica_groups=mesh['dom'=64,'blk'=4] {'dom'}, dimensions={0} | all-to-all | bytes 4194304 | tf_op jit(solution)/shard_map/all_to_all | solution.py:418
  173.4 5.3 %unpack.1 = bf16[4096,128]{1,0:T(8,128)(2,1)} custom-call(s32[32,128]{1,0:T(8,128)S(1)} %get-tuple-element.32.slot_ref, bf16[64,128,128]{2,1,0:T(8,128)(2,1)S(1)} %all_to_all.10.back_ref), custom_call_target="tpu_custom_call" | custom-call | tf_op jit(solution)/shard_map/unpack/pallas_call | solution.py:365
  (20 shorter events, 0.1 us)
Async XLA Ops:
  0.6 4.5 %copy-start.6 = (s32[4096]{0:T(1024)S(1)}, s32[4096]{0:T(1024)}, u32[]{:S(2)}) copy-start(s32[4096]{0:T(1024)} %param.13) | copy-start | bytes 49156
  0.6 4.5 %copy-start.5 = (s32[4096,1]{0,1:T(1,128)S(1)}, s32[4096,1]{0,1:T(1,128)}, u32[]{:S(2)}) copy-start(s32[4096,1]{0,1:T(1,128)} %param.12) | copy-start | bytes 49156
  0.7 4.5 %copy-start.8 = (bf16[4096]{0:T(1024)(128)(2,1)S(1)}, bf16[4096]{0:T(1024)(128)(2,1)}, u32[]{:S(2)}) copy-start(bf16[4096]{0:T(1024)(128)(2,1)} %param.11) | copy-start | bytes 24580
  0.7 4.5 %copy-start.7 = (bf16[4096]{0:T(1024)(128)(2,1)S(1)}, bf16[4096]{0:T(1024)(128)(2,1)}, u32[]{:S(2)}) copy-start(bf16[4096]{0:T(1024)(128)(2,1)} %param.10) | copy-start | bytes 24580
  0.7 4.5 %copy-start.4 = (bf16[4096,128]{1,0:T(8,128)(2,1)S(1)}, bf16[4096,128]{1,0:T(8,128)(2,1)}, u32[]{:S(2)}) copy-start(bf16[4096,128]{1,0:T(8,128)(2,1)} %cur_hbm.1) | copy-start | bytes 3145732
  2.1 12.0 %collective-permute-start.1 = (bf16[768,128]{1,0:T(8,128)(2,1)S(1)}, bf16[768,128]{1,0:T(8,128)(2,1)S(1)}, u32[]{:S(2)}, u32[]{:S(2)}) collective-permute-start(bf16[768,128]{1,0:T(8,128)(2,1)S(1)} %get-tuple-element.34), channel_id=1, source_target_pairs={{1,0},{2,1},{3,2},{4,3},{5,4},{6,5},{7,6},{8,7},{9,8},{10,9},{11,1... | collective-permute-start | bytes 589832 | tf_op jit(solution)/shard_map/ppermute | solution.py:385
  3.0 11.1 %collective-permute-start = (bf16[768,128]{1,0:T(8,128)(2,1)S(1)}, bf16[768,128]{1,0:T(8,128)(2,1)S(1)}, u32[]{:S(2)}, u32[]{:S(2)}) collective-permute-start(bf16[768,128]{1,0:T(8,128)(2,1)S(1)} %get-tuple-element.35), channel_id=1, source_target_pairs={{0,1},{1,2},{2,3},{3,4},{4,5},{5,6},{6,7},{7,8},{8,9},{9,10},{10,1... | collective-permute-start | bytes 589832 | tf_op jit(solution)/shard_map/ppermute | solution.py:384
  14.1 14.8 %copy-start.14 = (s32[32,16]{0,1:T(8,128)S(1)}, s32[32,16]{0,1:T(8,128)}, u32[]{:S(2)}) copy-start(s32[32,16]{0,1:T(8,128)} %param.17) | copy-start | bytes 6148
  14.1 14.9 %copy-start.13 = (f32[2048]{0:T(1024)S(1)}, f32[2048]{0:T(1024)}, u32[]{:S(2)}) copy-start(f32[2048]{0:T(1024)} %param.15) | copy-start | bytes 24580
  14.1 16.2 %copy-start.3 = (f32[2048,128]{1,0:T(8,128)S(1)}, f32[2048,128]{1,0:T(8,128)}, u32[]{:S(2)}) copy-start(f32[2048,128]{1,0:T(8,128)} %old_ref.1) | copy-start | bytes 3145732
  14.1 68.8 %all-to-all-start = ((bf16[64,136,128]{2,1,0:T(8,128)(2,1)}), bf16[64,136,128]{2,1,0:T(8,128)(2,1)}, u32[]{:S(2)}, u32[]{:S(2)}) async-start(bf16[64,136,128]{2,1,0:T(8,128)(2,1)} %get-tuple-element.19), calls=%async_computation | async-start | bytes 4456448 | tf_op jit(solution)/shard_map/all_to_all | solution.py:405
  35.1 1.0 copy-start.1
  36.1 1.0 copy-start.9
  37.1 1.0 copy-start.11
  38.1 1.0 copy-start.12
  82.9 11.9 %copy-start.10 = (f32[2048,128]{1,0:T(8,128)S(1)}, f32[2048,128]{1,0:T(8,128)}, u32[]{:S(2)}) copy-start(f32[2048,128]{1,0:T(8,128)} %copy-done.9) | copy-start | bytes 3145732
  92.8 7.1 %collective-permute-start.2 = (bf16[768,128]{1,0:T(8,128)(2,1)S(1)}, bf16[768,128]{1,0:T(8,128)(2,1)S(1)}, u32[]{:S(2)}, u32[]{:S(2)}) collective-permute-start(bf16[768,128]{1,0:T(8,128)(2,1)S(1)} %get-tuple-element.24.tail_ref), channel_id=1, source_target_pairs={{0,1},{1,2},{2,3},{3,4},{4,5},{5,6},{6,7},{7,8},{8,9},{9,10},{10,1... | collective-permute-start | bytes 589832 | tf_op jit(solution)/shard_map/ppermute | solution.py:384
  92.8 7.0 %copy-start = (bf16[32,64,1024]{2,1,0:T(8,128)(2,1)S(1)}, bf16[32,64,1024]{2,1,0:T(8,128)(2,1)}, u32[]{:S(2)}) copy-start(bf16[32,64,1024]{2,1,0:T(8,128)(2,1)} %cond_ref.3) | copy-start | bytes 12582916
  92.9 7.0 %copy-start.2 = (f32[2048,128]{1,0:T(8,128)S(1)}, f32[2048,128]{1,0:T(8,128)}, u32[]{:S(2)}) copy-start(f32[2048,128]{1,0:T(8,128)} %copy-done.1) | copy-start | bytes 3145732
  92.9 7.0 %collective-permute-start.3 = (bf16[768,128]{1,0:T(8,128)(2,1)S(1)}, bf16[768,128]{1,0:T(8,128)(2,1)S(1)}, u32[]{:S(2)}, u32[]{:S(2)}) collective-permute-start(bf16[768,128]{1,0:T(8,128)(2,1)S(1)} %get-tuple-element.25.head_ref), channel_id=1, source_target_pairs={{1,0},{2,1},{3,2},{4,3},{5,4},{6,5},{7,6},{8,7},{9,8},{10,9},{11,1... | collective-permute-start | bytes 589832 | tf_op jit(solution)/shard_map/ppermute | solution.py:385
